TPU v7x, 128 devices: a whole 4x4x4 slice. The times are simulated.
128 devices in a mesh: dp: 8 (over z, x_hi), tensor: 16 (over x_lo, y, core).
Axes of the slice: x: 4 (x_hi: 2, x_lo: 2; x = x_hi * 2 + x_lo), y: 4, z: 4, core: 2. Of those that a mesh axis runs over, the one named last changes fastest.
Arguments:
- tokens: bfloat16 [2560, 2048], P('dp', 'tensor'), may hold values from -6 to 6
- cotangent: bfloat16 [2560, 2048], P('dp', 'tensor'), may hold values from -6 to 6
- routes: int32 [2560, 4], P('dp'), may hold values from 0 to 5, all different within a row
- segments: int32 [2560], P('dp'), may hold values from 0 to 2, as said below
- parents: int32 [2560], P('dp'), may hold values from 0 to 1, as said below
- positions: int32 [2560], P('dp'), may hold values from 0 to 319, as said below
- norm_one: bfloat16 [2048], replicated, may hold values from 0.5 to 1.5
- w_query: bfloat16 [2048, 2048], P(None, 'tensor'), may hold values from -0.125 to 0.125
- b_query: bfloat16 [2048], P('tensor'), may hold values from -2 to 2
- w_key: bfloat16 [2048, 2048], P(None, 'tensor'), may hold values from -0.125 to 0.125
- b_key: bfloat16 [2048], P('tensor'), may hold values from -2 to 2
- w_value: bfloat16 [2048, 2048], P(None, 'tensor'), may hold values from -0.125 to 0.125
- b_value: bfloat16 [2048], P('tensor'), may hold values from -2 to 2
- w_out: bfloat16 [2048, 2048], P('tensor'), may hold values from -0.75 to 0.75
- norm_two: bfloat16 [2048], replicated, may hold values from 0.5 to 1.5
- router: bfloat16 [2048, 6], replicated, may hold values from -0.0625 to 0.0625
- expert_gate: bfloat16 [6, 2048, 1408], P(None, None, 'tensor'), may hold values from -0.125 to 0.125
- expert_up: bfloat16 [6, 2048, 1408], P(None, None, 'tensor'), may hold values from -0.125 to 0.125
- expert_down: bfloat16 [6, 1408, 2048], P(None, 'tensor'), may hold values from -1.25 to 1.25
- shared_gate: bfloat16 [2048, 5632], P(None, 'tensor'), may hold values from -0.125 to 0.125
- shared_up: bfloat16 [2048, 5632], P(None, 'tensor'), may hold values from -0.125 to 0.125
- shared_down: bfloat16 [5632, 2048], P('tensor'), may hold values from -0.3125 to 0.3125
- shared_switch: bfloat16 [2048], replicated, may hold values from -0.125 to 0.125
Outputs:
- output: bfloat16 [2560, 2048], P('dp', 'tensor')
- input_grad: float32 [2560, 2048], P('dp', 'tensor')
- grad_norm_one: float32 [2048], replicated
- grad_query: float32 [2048, 2048], P(None, 'tensor')
- grad_query_bias: float32 [2048], P('tensor')
- grad_key: float32 [2048, 2048], P(None, 'tensor')
- grad_key_bias: float32 [2048], P('tensor')
- grad_value: float32 [2048, 2048], P(None, 'tensor')
- grad_value_bias: float32 [2048], P('tensor')
- grad_out_proj: float32 [2048, 2048], P('tensor')
- grad_norm_two: float32 [2048], replicated
- grad_router: float32 [2048, 6], replicated
- grad_expert_gate: float32 [6, 2048, 1408], P(None, None, 'tensor')
- grad_expert_up: float32 [6, 2048, 1408], P(None, None, 'tensor')
- grad_expert_down: float32 [6, 1408, 2048], P(None, 'tensor')
- grad_shared_gate: float32 [2048, 5632], P(None, 'tensor')
- grad_shared_up: float32 [2048, 5632], P(None, 'tensor')
- grad_shared_down: float32 [5632, 2048], P('tensor')
- grad_shared_switch: float32 [2048], replicated
Inputs may be any that keep to these rules, and one draw needn't show every extreme that they name: `segments`: each tree's tokens come as segment 0 (its trunk), then segment 1, then segment 2; segment 0 is an ancestor of every segment. `parents`: the segment that a token's segment hangs from: 0 in segments 0 and 1, 0 or 1 in segment 2. `positions`: A token's place on its path from its tree's first token. `routes`: each token names 4 different experts.
All inputs are finite; a program needn't handle non-finite values.
Results may differ from a plain program's by a relative error of at most 0.034.
Values may be sent and summed in bfloat16 or wider, within the bound.
No kernel may reach another device: no remote copies, remote signals or barrier semaphores. Data moves between devices by JAX's collectives and lax.ppermute only.
A program may use at most 192 MiB of HBM per device.

v0:
```python
import jax
import jax.numpy as jnp
from jax import lax
from jax.sharding import PartitionSpec as P

HDIM = 128


EPSILON = 1e-06
THETA = 1000000.0
NEG_BIG = -1e30


def dot_plain(left_mat, right_mat):
    return jnp.dot(left_mat, right_mat, preferred_element_type=jnp.float32)


def dot_last(left_mat, right_mat):
    return lax.dot_general(
        left_mat, right_mat, (((1,), (1,)), ((), ())), preferred_element_type=jnp.float32
    )


def dot_first(left_mat, right_mat):
    return lax.dot_general(
        left_mat, right_mat, (((0,), (0,)), ((), ())), preferred_element_type=jnp.float32
    )


def heads_rotary(flat_rows, cosine, sine_table):
    row_count = flat_rows.shape[0]
    shaped = flat_rows.reshape(row_count, flat_rows.shape[1] // HDIM, HDIM)
    half_dim = HDIM // 2
    first_half = shaped[..., :half_dim]
    second_half = shaped[..., half_dim:]
    turned = jnp.concatenate(
        [
            first_half * cosine - second_half * sine_table,
            second_half * cosine + first_half * sine_table,
        ],
        axis=-1,
    )
    return turned.reshape(row_count, flat_rows.shape[1])


def silu_back(gate_val, up_val, grad_act):
    sigma_gate = jax.nn.sigmoid(gate_val)
    grad_gate = grad_act * up_val * sigma_gate * (1.0 + gate_val * (1.0 - sigma_gate))
    grad_up = grad_act * gate_val * sigma_gate
    return (grad_gate, grad_up)


def expert_pass(hidden_two, grad_out, mix_weight, w_gate_one, w_up_one, w_down_one):
    gate_val = dot_plain(hidden_two, w_gate_one)
    up_val = dot_plain(hidden_two, w_up_one)
    act_low = (jax.nn.silu(gate_val) * up_val).astype(jnp.bfloat16)
    branch_out = dot_plain(act_low, w_down_one)
    row_grad = jnp.sum(grad_out * branch_out, axis=1)
    grad_branch = (mix_weight[:, None] * grad_out).astype(jnp.bfloat16)
    grad_down = dot_first(act_low, grad_branch)
    grad_act = dot_last(grad_branch, w_down_one)
    grad_gate, grad_up = silu_back(gate_val, up_val, grad_act)
    gate_low = grad_gate.astype(jnp.bfloat16)
    up_low = grad_up.astype(jnp.bfloat16)
    grad_w_gate = dot_first(hidden_two, gate_low)
    grad_w_up = dot_first(hidden_two, up_low)
    grad_hidden = dot_last(gate_low, w_gate_one) + dot_last(up_low, w_up_one)
    return (
        mix_weight[:, None] * branch_out,
        row_grad,
        grad_w_gate,
        grad_w_up,
        grad_down,
        grad_hidden,
    )


def norm_back(grad_normed, normed, inverse, gain):
    scaled = grad_normed * gain.astype(jnp.float32)
    return inverse * (scaled - normed * jnp.mean(scaled * normed, axis=1, keepdims=True))


def on_device(
    tokens,
    cotangent,
    routes,
    segments,
    parents,
    positions,
    norm_one,
    w_query,
    b_query,
    w_key,
    b_key,
    w_value,
    b_value,
    w_out,
    norm_two,
    router,
    expert_gate,
    expert_up,
    expert_down,
    shared_gate,
    shared_up,
    shared_down,
    shared_switch,
):
    col_count = tokens.shape[1]
    col_start = lax.axis_index("tensor") * col_count
    token_rows, cot_rows = (
        lax.all_gather(tokens, "tensor", axis=1, tiled=True),
        lax.all_gather(cotangent, "tensor", axis=1, tiled=True),
    )
    whole_in = token_rows.astype(jnp.float32)
    grad_out = cot_rows.astype(jnp.float32)
    inverse_one = lax.rsqrt(jnp.mean(whole_in * whole_in, axis=1, keepdims=True) + EPSILON)
    normed_one = whole_in * inverse_one
    hidden_one = (normed_one * norm_one.astype(jnp.float32)).astype(jnp.bfloat16)
    half_dim = HDIM // 2
    frequency = jnp.power(THETA, -2.0 * jnp.arange(half_dim, dtype=jnp.float32) / HDIM)
    angles = positions.astype(jnp.float32)[:, None] * frequency[None, :]
    cosine = jnp.cos(angles)[:, None, :]
    sine_table = jnp.sin(angles)[:, None, :]
    q_pre = dot_plain(hidden_one, w_query) + b_query.astype(jnp.float32)
    k_pre = dot_plain(hidden_one, w_key) + b_key.astype(jnp.float32)
    v_pre = dot_plain(hidden_one, w_value) + b_value.astype(jnp.float32)
    query_rows = heads_rotary(q_pre, cosine, sine_table).astype(jnp.bfloat16)
    key_rows = heads_rotary(k_pre, cosine, sine_table).astype(jnp.bfloat16)
    value_rows = v_pre.astype(jnp.bfloat16)
    visible = (
        (segments[None, :] == 0)
        | (segments[None, :] == segments[:, None])
        | (segments[None, :] == parents[:, None])
    ) & (positions[None, :] <= positions[:, None])
    score_scale = HDIM ** (-0.5)
    scores = dot_last(query_rows, key_rows) * score_scale
    masked = jnp.where(visible, scores, NEG_BIG)
    top_score = jnp.max(masked, axis=1, keepdims=True)
    exp_scores = jnp.exp(masked - top_score)
    row_total = jnp.sum(exp_scores, axis=1, keepdims=True)
    probs_low = (exp_scores / row_total).astype(jnp.bfloat16)
    lse_parts = top_score + jnp.log(row_total)
    mixed_parts = dot_plain(probs_low, value_rows).astype(jnp.bfloat16)
    mixer_part = dot_plain(mixed_parts, w_out)
    mixer_cols = lax.psum_scatter(mixer_part, "tensor", scatter_dimension=1, tiled=True)
    resid_cols = tokens.astype(jnp.float32) + mixer_cols
    residual = lax.all_gather(resid_cols.astype(jnp.bfloat16), "tensor", axis=1, tiled=True).astype(
        resid_cols.dtype
    )
    inverse_two = lax.rsqrt(jnp.mean(residual * residual, axis=1, keepdims=True) + EPSILON)
    normed_two = residual * inverse_two
    hidden_two = (normed_two * norm_two.astype(jnp.float32)).astype(jnp.bfloat16)
    logits = dot_plain(hidden_two, router)
    gate_probs = jax.nn.softmax(logits, axis=1)
    expert_ids = jnp.arange(router.shape[1], dtype=jnp.int32)
    chosen = jnp.any(routes[:, :, None] == expert_ids[None, None, :], axis=1).astype(jnp.float32)
    mix_weights = gate_probs * chosen
    ffn_part = jnp.zeros(residual.shape, jnp.float32)
    grad_part = jnp.zeros(residual.shape, jnp.float32)
    row_grads = []
    gate_list = []
    up_list = []
    down_list = []
    for expert_id in range(expert_gate.shape[0]):
        contrib, row_grad, grad_wg, grad_wu, grad_wd, grad_hid = expert_pass(
            hidden_two,
            grad_out,
            mix_weights[:, expert_id],
            expert_gate[expert_id],
            expert_up[expert_id],
            expert_down[expert_id],
        )
        ffn_part = ffn_part + contrib
        grad_part = grad_part + grad_hid
        row_grads.append(row_grad)
        gate_list.append(grad_wg)
        up_list.append(grad_wu)
        down_list.append(grad_wd)
    switch = jax.nn.sigmoid(dot_plain(hidden_two, shared_switch))
    contrib, switch_part, grad_shared_gate, grad_shared_up, grad_shared_down, grad_hid = (
        expert_pass(hidden_two, grad_out, switch, shared_gate, shared_up, shared_down)
    )
    ffn_part = ffn_part + contrib
    grad_part = grad_part + grad_hid
    ffn_cols = lax.psum_scatter(
        ffn_part.astype(jnp.bfloat16), "tensor", scatter_dimension=1, tiled=True
    ).astype(jnp.float32)
    output = (resid_cols + ffn_cols).astype(jnp.bfloat16)
    gate_part = jnp.stack(row_grads, axis=1)
    mix_grad, switch_grad = lax.psum((gate_part, switch_part), "tensor")
    masked_grad = mix_grad * chosen
    logit_low = (
        gate_probs * (masked_grad - jnp.sum(gate_probs * masked_grad, axis=1, keepdims=True))
    ).astype(jnp.bfloat16)
    grad_router = dot_first(hidden_two, logit_low)
    switch_low = (switch_grad * switch * (1.0 - switch)).astype(jnp.bfloat16)
    grad_shared_switch = dot_plain(switch_low, hidden_two)
    local_two = (
        dot_last(logit_low, router)
        + switch_low.astype(jnp.float32)[:, None] * shared_switch.astype(jnp.float32)[None, :]
    )
    grad_expert_gate = jnp.stack(gate_list, axis=0)
    grad_expert_up = jnp.stack(up_list, axis=0)
    grad_expert_down = jnp.stack(down_list, axis=0)
    grad_two = lax.psum(grad_part.astype(jnp.bfloat16), "tensor").astype(jnp.float32) + local_two
    grad_norm_two = jnp.sum(grad_two * normed_two, axis=0)
    grad_res = norm_back(grad_two, normed_two, inverse_two, norm_two) + grad_out
    grad_attn = grad_res.astype(jnp.bfloat16)
    grad_out_proj = dot_first(mixed_parts, grad_attn)
    grad_heads = dot_last(grad_attn, w_out).astype(jnp.bfloat16)
    scores = dot_last(query_rows, key_rows) * score_scale
    masked = jnp.where(visible, scores, NEG_BIG)
    probs = jnp.exp(masked - lse_parts)
    probs_low = probs.astype(jnp.bfloat16)
    dprobs = dot_last(grad_heads, value_rows)
    dscores = probs * (dprobs - jnp.sum(probs * dprobs, axis=1, keepdims=True))
    dscores_low = dscores.astype(jnp.bfloat16)
    dq_parts = dot_plain(dscores_low, key_rows) * score_scale
    dk_parts = dot_first(dscores_low, query_rows) * score_scale
    dv_parts = dot_first(probs_low, grad_heads)
    dq_low = heads_rotary(dq_parts, cosine, -sine_table).astype(jnp.bfloat16)
    dk_low = heads_rotary(dk_parts, cosine, -sine_table).astype(jnp.bfloat16)
    dv_low = dv_parts.astype(jnp.bfloat16)
    grad_query = dot_first(hidden_one, dq_low)
    grad_key = dot_first(hidden_one, dk_low)
    grad_value = dot_first(hidden_one, dv_low)
    grad_query_bias = jnp.sum(dq_low.astype(jnp.float32), axis=0)
    grad_key_bias = jnp.sum(dk_low.astype(jnp.float32), axis=0)
    grad_value_bias = jnp.sum(dv_low.astype(jnp.float32), axis=0)
    part_one = dot_last(dq_low, w_query) + dot_last(dk_low, w_key) + dot_last(dv_low, w_value)
    share_one = lax.psum_scatter(
        part_one.astype(jnp.bfloat16), "tensor", scatter_dimension=1, tiled=True
    ).astype(jnp.float32)
    grad_one = lax.all_gather(share_one.astype(jnp.bfloat16), "tensor", axis=1, tiled=True).astype(
        share_one.dtype
    )
    grad_norm_one = jnp.sum(grad_one * normed_one, axis=0)
    input_full = norm_back(grad_one, normed_one, inverse_one, norm_one) + grad_res
    input_grad = lax.dynamic_slice_in_dim(input_full, col_start, col_count, 1)
    (
        grad_norm_one,
        grad_query,
        grad_query_bias,
        grad_key,
        grad_key_bias,
        grad_value,
        grad_value_bias,
        grad_out_proj,
        grad_norm_two,
        grad_router,
        grad_expert_gate,
        grad_expert_up,
        grad_expert_down,
        grad_shared_gate,
        grad_shared_up,
        grad_shared_down,
        grad_shared_switch,
    ) = (
        lax.psum(grad_norm_one.astype(jnp.bfloat16), "dp").astype(jnp.float32),
        lax.psum(grad_query.astype(jnp.bfloat16), "dp").astype(jnp.float32),
        lax.psum(grad_query_bias.astype(jnp.bfloat16), "dp").astype(jnp.float32),
        lax.psum(grad_key.astype(jnp.bfloat16), "dp").astype(jnp.float32),
        lax.psum(grad_key_bias.astype(jnp.bfloat16), "dp").astype(jnp.float32),
        lax.psum(grad_value.astype(jnp.bfloat16), "dp").astype(jnp.float32),
        lax.psum(grad_value_bias.astype(jnp.bfloat16), "dp").astype(jnp.float32),
        lax.psum(grad_out_proj.astype(jnp.bfloat16), "dp").astype(jnp.float32),
        lax.psum(grad_norm_two.astype(jnp.bfloat16), "dp").astype(jnp.float32),
        lax.psum(grad_router.astype(jnp.bfloat16), "dp").astype(jnp.float32),
        lax.psum(grad_expert_gate.astype(jnp.bfloat16), "dp").astype(jnp.float32),
        lax.psum(grad_expert_up.astype(jnp.bfloat16), "dp").astype(jnp.float32),
        lax.psum(grad_expert_down.astype(jnp.bfloat16), "dp").astype(jnp.float32),
        lax.psum(grad_shared_gate.astype(jnp.bfloat16), "dp").astype(jnp.float32),
        lax.psum(grad_shared_up.astype(jnp.bfloat16), "dp").astype(jnp.float32),
        lax.psum(grad_shared_down.astype(jnp.bfloat16), "dp").astype(jnp.float32),
        lax.psum(grad_shared_switch.astype(jnp.bfloat16), "dp").astype(jnp.float32),
    )
    return (
        output,
        input_grad,
        grad_norm_one,
        grad_query,
        grad_query_bias,
        grad_key,
        grad_key_bias,
        grad_value,
        grad_value_bias,
        grad_out_proj,
        grad_norm_two,
        grad_router,
        grad_expert_gate,
        grad_expert_up,
        grad_expert_down,
        grad_shared_gate,
        grad_shared_up,
        grad_shared_down,
        grad_shared_switch,
    )


def solution(mesh):
    placed = (
        P("dp", "tensor"),
        P("dp", "tensor"),
        P("dp", None),
        P("dp"),
        P("dp"),
        P("dp"),
        P(),
        P(None, "tensor"),
        P("tensor"),
        P(None, "tensor"),
        P("tensor"),
        P(None, "tensor"),
        P("tensor"),
        P("tensor", None),
        P(),
        P(),
        P(None, None, "tensor"),
        P(None, None, "tensor"),
        P(None, "tensor", None),
        P(None, "tensor"),
        P(None, "tensor"),
        P("tensor", None),
        P(),
    )
    return jax.shard_map(
        on_device,
        mesh=mesh,
        in_specs=placed,
        out_specs=(
            P("dp", "tensor"),
            P("dp", "tensor"),
            P(),
            P(None, "tensor"),
            P("tensor"),
            P(None, "tensor"),
            P("tensor"),
            P(None, "tensor"),
            P("tensor"),
            P("tensor", None),
            P(),
            P(),
            P(None, None, "tensor"),
            P(None, None, "tensor"),
            P(None, "tensor", None),
            P(None, "tensor"),
            P(None, "tensor"),
            P("tensor", None),
            P(),
        ),
        check_vma=False,
    )
```

profile of v0, /device:TPU:6, one launch (start us, length us, event | category | flops | bytes accessed | tf_op | source)
XLA Modules:
  0.0 1146.1 jit_solution(15830810808092853321)
XLA Ops:
  12.0 34.5 %all-gather.5.cloned.1.call-done = bf16[320,2048]{1,0:T(8,128)(2,1)} async-done(((bf16[320,128]{1,0:T(8,128)(2,1)}), bf16[320,2048]{1,0:T(8,128)(2,1)}) %all-gather.5.cloned.1.call-update) | async-done | bytes 1310736 | tf_op jit(solution)/shard_map/all_gather | solution.py:111
  46.6 1.8 fusion.13
  48.4 2.0 fusion.74
  54.2 2.0 fusion.262
  56.2 64.0 %reduce-scatter.8.cloned.1.call-done = f32[320,128]{1,0:T(8,128)} async-done(((f32[320,2048]{1,0:T(8,128)}), f32[320,128]{1,0:T(8,128)}) %reduce-scatter.8.cloned.1.call-update) | async-done | bytes 163856 | tf_op jit(solution)/shard_map/reduce_scatter | solution.py:145
  120.2 1.6 fusion.234
  122.8 33.4 %all-gather.7.cloned.1.call-done = bf16[320,2048]{1,0:T(8,128)(2,1)} async-done(((bf16[320,128]{1,0:T(8,128)(2,1)}), bf16[320,2048]{1,0:T(8,128)(2,1)}) %all-gather.7.cloned.1.call-update) | async-done | bytes 1310736 | tf_op jit(solution)/shard_map/all_gather | solution.py:147
  156.2 1.8 fusion.19
  173.2 19.3 %all-gather.9.cloned.1.call-done = bf16[320,2048]{1,0:T(8,128)(2,1)} async-done(((bf16[320,128]{1,0:T(8,128)(2,1)}), bf16[320,2048]{1,0:T(8,128)(2,1)}) %all-gather.9.cloned.1.call-update) | async-done | bytes 1310736 | tf_op jit(solution)/shard_map/all_gather | solution.py:112
  192.5 2.8 multiply_convert_fusion.15
  211.0 1.9 multiply_convert_fusion.4
  213.0 3.7 fusion.34
  217.2 2.0 fusion.158
  219.2 2.1 fusion.148
  221.3 2.0 fusion.138
  223.3 2.1 fusion.128
  225.4 2.0 fusion.118
  227.4 2.0 fusion.108
  229.5 54.8 %all-reduce = (f32[320,6]{0,1:T(8,128)S(1)}, f32[320]{0:T(512)S(1)}) all-reduce(f32[320,6]{0,1:T(8,128)S(1)} %stack.111, f32[320]{0:T(512)S(1)} %get-tuple-element.23), channel_id=1, replica_groups=mesh['dp'=8,'tensor'=16] {'tensor'}, use_global_device_ids=true, to_apply=%region_16.17 | all-reduce | flops 2240 | bytes 17920 | tf_op jit(solution)/shard_map/psum | solution.py:190
  284.9 2.7 multiply_convert_fusion.2
  300.2 1.9 fusion.12
  302.7 118.0 %all-reduce.6.cloned.1.call-done = bf16[320,2048]{1,0:T(8,128)(2,1)} async-done(((bf16[320,2048]{1,0:T(8,128)(2,1)}), bf16[320,2048]{1,0:T(8,128)(2,1)}) %all-reduce.6.cloned.1.call-update) | async-done | bytes 1310736 | tf_op jit(solution)/shard_map/psum | solution.py:205
  420.8 2.8 fusion.18
  430.2 1.6 copy.46
  431.9 7.0 add_convert_fusion
  438.9 1.6 copy.44
  459.7 35.4 %reduce-scatter.12.cloned.1.call-done = bf16[128,320]{1,0:T(8,128)(2,1)} async-done(((bf16[2048,320]{1,0:T(8,128)(2,1)}), bf16[128,320]{1,0:T(8,128)(2,1)}) %reduce-scatter.12.cloned.1.call-update) | async-done | bytes 81936
  495.1 1.6 copy.47
  499.3 2.0 convolution_convert_fusion.2
  501.3 2.1 convolution_convert_fusion.1
  503.4 2.2 convolution_convert_fusion
  505.6 1.6 convolution_convert_fusion.6
  507.2 1.6 convolution_convert_fusion.5
  508.8 1.6 convolution_convert_fusion.4
  513.0 46.2 %reduce-scatter.10.cloned.1.call-done = bf16[128,320]{1,0:T(8,128)(2,1)} async-done(((bf16[2048,320]{1,0:T(8,128)(2,1)}), bf16[128,320]{1,0:T(8,128)(2,1)}) %reduce-scatter.10.cloned.1.call-update) | async-done | bytes 81936
  560.9 34.3 %all-gather.11.cloned.1.call-done = bf16[320,2048]{1,0:T(8,128)(2,1)} async-done(((bf16[320,128]{1,0:T(8,128)(2,1)}), bf16[320,2048]{1,0:T(8,128)(2,1)}) %all-gather.11.cloned.1.call-update) | async-done | bytes 1310736 | tf_op jit(solution)/shard_map/all_gather | solution.py:234
  595.2 4.5 fusion.20
  599.7 38.8 %all-reduce.1 = (bf16[2048]{0:T(1024)(128)(2,1)S(1)}, bf16[128]{0:T(256)(128)(2,1)S(1)}, bf16[128]{0:T(256)(128)(2,1)S(1)}, bf16[128]{0:T(256)(128)(2,1)S(1)}, b...) all-reduce(bf16[2048]{0:T(1024)(128)(2,1)S(1)} %get-tuple-element.2, ...), channel_id=1, replica_groups=mesh['dp'=8,'tensor'=16] {'dp'}, use_global_device_ids=true, to_apply=%region_25.26 | all-reduce | flops 18816 | bytes 75264 | tf_op jit(solution)/shard_map/psum | solution.py:259
  642.5 1.9 dynamic-slice_add_fusion
  644.4 474.8 %all-reduce.8.cloned.1.call-done = (bf16[2048,128]{1,0:T(8,128)(2,1)}, bf16[2048,128]{1,0:T(8,128)(2,1)}, bf16[2048,128]{1,0:T(8,128)(2,1)}, bf16[128,2048]{1,0:...) async-done(((bf16[2048,128]{1,0:T(8,128)(2,1)}, ...) | async-done | bytes 12910608 | tf_op jit(solution)/shard_map/psum | solution.py:260
  1119.2 2.2 convert_element_type.369
  1121.4 2.2 convert_element_type.372
  1125.8 2.6 convert_element_type.383
  1128.4 2.6 convert_element_type.384
  1131.0 2.6 convert_element_type.385
  1133.6 1.9 convert_element_type.387
  1135.5 1.9 convert_element_type.389
  1137.4 1.9 convert_element_type.391
  (427 shorter events, 92.8 us)
Async XLA Ops:
  7.2 205.8 %copy-start = (bf16[352,2048]{1,0:T(8,128)(2,1)S(1)}, bf16[352,2048]{1,0:T(8,128)(2,1)}, u32[]{:S(2)}) copy-start(bf16[352,2048]{1,0:T(8,128)(2,1)} %param.44) | copy-start | bytes 4325380
  7.2 39.4 %all-gather.5.cloned.1.call-start = ((), (), s32[]{:S(2)}) async-start(), calls=%async_computation.3 | async-start | bytes 1392640 | tf_op jit(solution)/shard_map/all_gather | solution.py:111
  7.9 112.3 %reduce-scatter.8.cloned.1.call-start = ((), (), s32[]{:S(2)}) async-start(), calls=%async_computation.4 | async-start | bytes 2785280 | tf_op jit(solution)/shard_map/reduce_scatter | solution.py:145
  11.3 39.7 %copy-start.140 = (f32[64]{0:T(128)}, f32[64]{0:T(128)S(1)}, u32[]{:S(2)}) copy-start(f32[64]{0:T(128)S(1)} %multiply_power_fusion) | copy-start | bytes 772
  12.0 38.3 %copy-start.46 = (bf16[2048,128]{1,0:T(8,128)(2,1)S(1)}, bf16[2048,128]{1,0:T(8,128)(2,1)}, u32[]{:S(2)}) copy-start(bf16[2048,128]{1,0:T(8,128)(2,1)} %param.30) | copy-start | bytes 1572868
  46.6 3.8 copy-start.25
  54.2 66.1 %copy-start.43 = (bf16[320,128]{1,0:T(8,128)(2,1)S(1)}, bf16[320,128]{1,0:T(8,128)(2,1)}, u32[]{:S(2)}) copy-start(bf16[320,128]{1,0:T(8,128)(2,1)} %param.23) | copy-start | bytes 245764
  56.2 66.5 %copy-start.138 = (bf16[2048]{0:T(1024)(128)(2,1)S(1)}, bf16[2048]{0:T(1024)(128)(2,1)}, u32[]{:S(2)}) copy-start(bf16[2048]{0:T(1024)(128)(2,1)} %param.37) | copy-start | bytes 12292
  56.2 66.5 %copy-start.137 = (s32[320,4]{0,1:T(4,128)S(1)}, s32[320,4]{0,1:T(4,128)}, u32[]{:S(2)}) copy-start(s32[320,4]{0,1:T(4,128)} %param.25) | copy-start | bytes 15364
  56.2 66.6 %copy-start.117 = (bf16[2048]{0:T(1024)(128)(2,1)S(1)}, bf16[2048]{0:T(1024)(128)(2,1)}, u32[]{:S(2)}) copy-start(bf16[2048]{0:T(1024)(128)(2,1)} %param.45) | copy-start | bytes 12292
  56.2 100.0 %all-gather.7.cloned.1.call-start = ((), (), s32[]{:S(2)}) async-start(), calls=%async_computation.5 | async-start | bytes 1392640 | tf_op jit(solution)/shard_map/all_gather | solution.py:147
  121.8 70.7 %all-gather.9.cloned.1.call-start = ((), (), s32[]{:S(2)}) async-start(), calls=%async_computation.6 | async-start | bytes 1392640 | tf_op jit(solution)/shard_map/all_gather | solution.py:112
  122.4 298.4 %all-reduce.6.cloned.1.call-start = ((), (), s32[]{:S(2)}) async-start(), calls=%async_computation.7 | async-start | bytes 2621440 | tf_op jit(solution)/shard_map/psum | solution.py:205
  162.2 30.4 %copy-start.135 = (f32[320]{0:T(512)}, f32[320]{0:T(512)S(1)}, u32[]{:S(2)}) copy-start(f32[320]{0:T(512)S(1)} %get-tuple-element.30) | copy-start | bytes 3844
  162.2 33.8 %copy-start.133 = (f32[320]{0:T(512)}, f32[320]{0:T(512)S(1)}, u32[]{:S(2)}) copy-start(f32[320]{0:T(512)S(1)} %get-tuple-element.35) | copy-start | bytes 3844
  162.2 36.5 %copy-start.131 = (f32[320]{0:T(512)}, f32[320]{0:T(512)S(1)}, u32[]{:S(2)}) copy-start(f32[320]{0:T(512)S(1)} %get-tuple-element.34) | copy-start | bytes 3844
  162.2 38.7 %copy-start.129 = (f32[320]{0:T(512)}, f32[320]{0:T(512)S(1)}, u32[]{:S(2)}) copy-start(f32[320]{0:T(512)S(1)} %get-tuple-element.33) | copy-start | bytes 3844
  162.2 41.0 %copy-start.127 = (f32[320]{0:T(512)}, f32[320]{0:T(512)S(1)}, u32[]{:S(2)}) copy-start(f32[320]{0:T(512)S(1)} %get-tuple-element.32) | copy-start | bytes 3844
  162.2 43.3 %copy-start.125 = (f32[320]{0:T(512)}, f32[320]{0:T(512)S(1)}, u32[]{:S(2)}) copy-start(f32[320]{0:T(512)S(1)} %get-tuple-element.31) | copy-start | bytes 3844
  195.4 21.8 %copy-start.77 = (bf16[320,88]{0,1:T(8,128)(2,1)}, bf16[320,88]{0,1:T(8,128)(2,1)S(1)}, u32[]{:S(2)}) copy-start(bf16[320,88]{0,1:T(8,128)(2,1)S(1)} %get-tuple-element.78) | copy-start | bytes 168964
  196.0 17.0 %copy-start.4 = (f32[320,2048]{1,0:T(8,128)}, f32[320,2048]{1,0:T(8,128)S(1)}, u32[]{:S(2)}) copy-start(f32[320,2048]{1,0:T(8,128)S(1)} %fusion.153) | copy-start | bytes 7864324
  198.1 21.2 %copy-start.79 = (bf16[320,88]{0,1:T(8,128)(2,1)}, bf16[320,88]{0,1:T(8,128)(2,1)S(1)}, u32[]{:S(2)}) copy-start(bf16[320,88]{0,1:T(8,128)(2,1)S(1)} %get-tuple-element.75) | copy-start | bytes 168964
  198.7 14.2 %copy-start.5 = (f32[320,2048]{1,0:T(8,128)}, f32[320,2048]{1,0:T(8,128)S(1)}, u32[]{:S(2)}) copy-start(f32[320,2048]{1,0:T(8,128)S(1)} %fusion.143) | copy-start | bytes 7864324
  200.4 20.9 %copy-start.81 = (bf16[320,88]{0,1:T(8,128)(2,1)}, bf16[320,88]{0,1:T(8,128)(2,1)S(1)}, u32[]{:S(2)}) copy-start(bf16[320,88]{0,1:T(8,128)(2,1)S(1)} %get-tuple-element.72) | copy-start | bytes 168964
  200.9 12.0 %copy-start.6 = (f32[320,2048]{1,0:T(8,128)}, f32[320,2048]{1,0:T(8,128)S(1)}, u32[]{:S(2)}) copy-start(f32[320,2048]{1,0:T(8,128)S(1)} %fusion.133) | copy-start | bytes 7864324
  202.7 20.6 %copy-start.85 = (bf16[320,88]{0,1:T(8,128)(2,1)}, bf16[320,88]{0,1:T(8,128)(2,1)S(1)}, u32[]{:S(2)}) copy-start(bf16[320,88]{0,1:T(8,128)(2,1)S(1)} %get-tuple-element.69) | copy-start | bytes 168964
  203.2 9.7 copy-start.7
  205.0 20.4 %copy-start.87 = (bf16[320,88]{0,1:T(8,128)(2,1)}, bf16[320,88]{0,1:T(8,128)(2,1)S(1)}, u32[]{:S(2)}) copy-start(bf16[320,88]{0,1:T(8,128)(2,1)S(1)} %get-tuple-element.66) | copy-start | bytes 168964
  205.5 7.4 copy-start.8
  207.3 20.1 %copy-start.83 = (bf16[320,88]{0,1:T(8,128)(2,1)}, bf16[320,88]{0,1:T(8,128)(2,1)S(1)}, u32[]{:S(2)}) copy-start(bf16[320,88]{0,1:T(8,128)(2,1)S(1)} %get-tuple-element.63) | copy-start | bytes 168964
  208.7 4.3 copy-start.9
  213.0 4.3 copy-start.21
  287.5 11.9 %copy-start.41 = (bf16[320,352]{1,0:T(8,128)(2,1)}, bf16[320,352]{1,0:T(8,128)(2,1)S(1)}, u32[]{:S(2)}) copy-start(bf16[320,352]{1,0:T(8,128)(2,1)S(1)} %get-tuple-element.60) | copy-start | bytes 675844
  300.1 120.6 %copy-start.11 = (bf16[320,2048]{1,0:T(8,128)(2,1)S(1)}, bf16[320,2048]{1,0:T(8,128)(2,1)}, u32[]{:S(2)}) copy-start(bf16[320,2048]{1,0:T(8,128)(2,1)} %all-gather.7.cloned.1.call-done) | copy-start | bytes 3932164
  300.1 120.6 %copy-start.116 = (bf16[2048,6]{0,1:T(8,128)(2,1)S(1)}, bf16[2048,6]{0,1:T(8,128)(2,1)}, u32[]{:S(2)}) copy-start(bf16[2048,6]{0,1:T(8,128)(2,1)} %param.38) | copy-start | bytes 73732
  300.1 120.6 %copy-start.144 = (f32[320]{0:T(512)S(1)}, f32[320]{0:T(512)}, u32[]{:S(2)}) copy-start(f32[320]{0:T(512)} %get-tuple-element.55) | copy-start | bytes 3844
  302.1 193.0 %reduce-scatter.12.cloned.1.call-start = ((), (), s32[]{:S(2)}) async-start(), calls=%async_computation.10 | async-start | bytes 1671168
  431.8 127.4 %reduce-scatter.10.cloned.1.call-start = ((), (), s32[]{:S(2)}) async-start(), calls=%async_computation.9 | async-start | bytes 1671168
  447.4 147.8 %all-gather.11.cloned.1.call-start = ((), (), s32[]{:S(2)}) async-start(), calls=%async_computation.8 | async-start | bytes 1392640 | tf_op jit(solution)/shard_map/all_gather | solution.py:234
  457.2 39.6 %copy-start.66 = (bf16[320,88]{0,1:T(8,128)(2,1)S(1)}, bf16[320,88]{0,1:T(8,128)(2,1)}, u32[]{:S(2)}) copy-start(bf16[320,88]{0,1:T(8,128)(2,1)} %get-tuple-element.62) | copy-start | bytes 168964
  458.5 39.5 %copy-start.104 = (bf16[320,88]{0,1:T(8,128)(2,1)S(1)}, bf16[320,88]{0,1:T(8,128)(2,1)}, u32[]{:S(2)}) copy-start(bf16[320,88]{0,1:T(8,128)(2,1)} %copy-done.103) | copy-start | bytes 168964
  496.8 622.4 %all-reduce.8.cloned.1.call-start = ((), (), s32[]{:S(2)}) async-start(), calls=%async_computation.11 | async-start | bytes 25821184 | tf_op jit(solution)/shard_map/psum | solution.py:260
  511.7 48.5 %copy-start.44 = (bf16[320,128]{1,0:T(8,128)(2,1)S(1)}, bf16[320,128]{1,0:T(8,128)(2,1)}, u32[]{:S(2)}) copy-start(bf16[320,128]{1,0:T(8,128)(2,1)} %param.23) | copy-start | bytes 245764
  511.7 48.5 %copy-start.45 = (f32[320,128]{1,0:T(8,128)S(1)}, f32[320,128]{1,0:T(8,128)}, u32[]{:S(2)}) copy-start(f32[320,128]{1,0:T(8,128)} %reduce-scatter.8.cloned.1.call-done) | copy-start | bytes 491524
  511.7 83.5 %copy-start.27 = (bf16[320,2048]{1,0:T(8,128)(2,1)S(1)}, bf16[320,2048]{1,0:T(8,128)(2,1)}, u32[]{:S(2)}) copy-start(bf16[320,2048]{1,0:T(8,128)(2,1)} %all-gather.5.cloned.1.call-done) | copy-start | bytes 3932164
  1119.2 4.4 copy-start.52
  1119.2 5.4 copy-start.51
  1121.4 4.4 copy-start.30
  (108 other events, 199.5 us)
Sparse Core Ops, SparseCore 0:
  9.7 36.8 all-gather.4
  56.3 63.8 reduce-scatter.7
  122.4 33.6 all-gather.6
  157.6 34.8 all-gather.8
  302.2 118.4 all-reduce.5
  431.9 63.1 reduce-scatter.11
  498.2 60.9 reduce-scatter.9
  561.4 33.7 all-gather.10
  599.8 519.4 all-reduce.7
where the time goes:
time: 1150 us
  waiting for transfers between devices  861 us (75%)
  matrix products  101 us (9%)
  blocking collectives  93.5 us (8%)
  other arithmetic  51.2 us (4%)
  local copies, waits for them, and re-layouts  22.5 us (2%)
  between operations  15.4 us (1%)
    psum x1, waiting for transfers between devices, on_device(): lax.psum(grad_query.astype(jnp.bfloat16), 'dp').astype(jnp.float32)  475 us
    psum x1, waiting for transfers between devices, on_device(): lax.psum(grad_part.astype(jnp.bfloat16), 'tensor').astype(jnp.float32)  118 us
    unnamed x11, waiting for transfers between devices  82.9 us
    reduce_scatter x1, waiting for transfers between devices, on_device(): lax.psum_scatter(mixer_part, 'tensor', scatter_dimension=1, tiled=True)  64 us
    psum x1, blocking collectives, on_device(): mix_grad, switch_grad = lax.psum((gate_part, switch_part), 'tensor')  54.8 us
    psum x1, blocking collectives, on_device(): lax.psum(grad_norm_one.astype(jnp.bfloat16), 'dp').astype(jnp.float32)  38.8 us
    dot_general x28, matrix products, dot_last(): lax.dot_general(left_mat, right_mat, (((1,), (1,)), ((), ())), preferred_...  35.8 us
    all_gather x1, waiting for transfers between devices, on_device(): lax.all_gather(tokens, 'tensor', axis=1, tiled=True)  34.5 us
  transfers between devices with their start and end apart: 9, of which 9 were waited for; matrix products, arithmetic and copies ran while one was open for 7% of the time, Pallas kernels for 0%

commit v1 on v0

v1 whole, which is shorter than its diff:
```python
import jax
import jax.numpy as jnp
from jax import lax
from jax.sharding import Mesh
from jax.sharding import PartitionSpec as P

HDIM = 128
HALF = HDIM // 2
EPSILON = 1e-06
THETA = 1000000.0
NEG_BIG = -1e30
TREES = ("z", "xhi")
TENSOR = ("xlo", "y", "core")
NDP = 8
NTP = 16
ROWS = 320
COLS = 128
WIDTH = 2048
EXPERTS = 6
EFF = 88
ROUTED = EXPERTS * EFF
SHARED = 352
HIDDEN = ROUTED + SHARED
f32 = jnp.float32
bf16 = jnp.bfloat16


def dot_plain(left_mat, right_mat):
    return jnp.dot(left_mat, right_mat, preferred_element_type=f32)


def dot_last(left_mat, right_mat):
    return lax.dot_general(
        left_mat, right_mat, (((1,), (1,)), ((), ())), preferred_element_type=f32
    )


def dot_first(left_mat, right_mat):
    return lax.dot_general(
        left_mat, right_mat, (((0,), (0,)), ((), ())), preferred_element_type=f32
    )


def spread(block, axes, count):
    return lax.all_to_all(
        jnp.broadcast_to(block[None], (count,) + block.shape), axes, 0, 0
    )


def side_by_side(blocks):
    return jnp.transpose(blocks, (1, 0, 2)).reshape(blocks.shape[1], -1)


def cut_columns(rows):
    return jnp.transpose(rows.reshape(rows.shape[0], -1, COLS), (1, 0, 2))


def halves(values):
    high = lax.reduce_precision(values, 8, 7)
    return high.astype(bf16), (values - high).astype(bf16)


def rotate(rows, cosine, sine_table):
    first, second = rows[:, :HALF], rows[:, HALF:]
    return jnp.concatenate(
        [first * cosine - second * sine_table, second * cosine + first * sine_table], axis=1
    )


def per_hidden(weights):
    count = weights.shape[1]
    routed = jnp.broadcast_to(weights[:EXPERTS, None, :], (EXPERTS, EFF, count))
    shared = jnp.broadcast_to(weights[EXPERTS:], (SHARED, count))
    return jnp.concatenate([routed.reshape(ROUTED, count), shared], axis=0)


def per_expert(values):
    count = values.shape[1]
    routed = jnp.sum(values[:ROUTED].reshape(EXPERTS, EFF, count), axis=1)
    return jnp.concatenate([routed, jnp.sum(values[ROUTED:], axis=0, keepdims=True)], axis=0)


def expert_terms(gate_val, up_val, grad_plain, mixing):
    sigma = jax.nn.sigmoid(gate_val)
    silu = gate_val * sigma
    act = silu * up_val
    grad_act = mixing * grad_plain
    grad_gate = grad_act * up_val * sigma * (1.0 + gate_val * (1.0 - sigma))
    grad_up = grad_act * silu
    return act, grad_gate, grad_up


def on_device(
    tokens,
    cotangent,
    routes,
    segments,
    parents,
    positions,
    norm_one,
    w_query,
    b_query,
    w_key,
    b_key,
    w_value,
    b_value,
    w_out,
    norm_two,
    router,
    expert_gate,
    expert_up,
    expert_down,
    shared_gate,
    shared_up,
    shared_down,
    shared_switch,
):
    tree = lax.axis_index(TREES)
    col_start = lax.axis_index(TENSOR) * COLS
    gain_one = norm_one.astype(f32)
    gain_two = norm_two.astype(f32)
    gain_two_cols = lax.dynamic_slice_in_dim(gain_two, col_start, COLS, 0)
    gain_one_cols = lax.dynamic_slice_in_dim(gain_one, col_start, COLS, 0)
    gate_mat = jnp.concatenate(
        [jnp.transpose(expert_gate, (0, 2, 1)).reshape(ROUTED, WIDTH), shared_gate.T], axis=0
    )
    up_mat = jnp.concatenate(
        [jnp.transpose(expert_up, (0, 2, 1)).reshape(ROUTED, WIDTH), shared_up.T], axis=0
    )
    down_mat = jnp.concatenate([expert_down.reshape(ROUTED, WIDTH), shared_down], axis=0)
    w_qkv = jnp.concatenate([w_query, w_key, w_value], axis=1)
    bias = jnp.concatenate([b_query, b_key, b_value]).astype(f32)
    switch_mat = jnp.concatenate([router.T, shared_switch[None]], axis=0)

    cot_blocks = lax.all_gather(cotangent, TREES + TENSOR, axis=0)
    whole_cot = jnp.transpose(
        cot_blocks.reshape(NDP, NTP, ROWS, COLS), (0, 2, 1, 3)
    ).reshape(NDP * ROWS, WIDTH)

    whole_in = side_by_side(spread(tokens, TENSOR, NTP)).astype(f32)
    inverse_one = lax.rsqrt(jnp.mean(whole_in * whole_in, axis=1, keepdims=True) + EPSILON)
    normed_one = whole_in * inverse_one
    hidden_one = (normed_one * gain_one).astype(bf16)
    frequency = jnp.power(THETA, -2.0 * jnp.arange(HALF, dtype=f32) / HDIM)
    angles = positions.astype(f32)[:, None] * frequency[None, :]
    cosine = jnp.cos(angles)
    sine_table = jnp.sin(angles)
    plain = dot_plain(hidden_one, w_qkv)
    biased = plain + bias
    query_rows = rotate(biased[:, :HDIM], cosine, sine_table).astype(bf16)
    key_rows = rotate(biased[:, HDIM : 2 * HDIM], cosine, sine_table).astype(bf16)
    value_rows = biased[:, 2 * HDIM :].astype(bf16)
    visible = (
        (segments[None, :] == 0)
        | (segments[None, :] == segments[:, None])
        | (segments[None, :] == parents[:, None])
    ) & (positions[None, :] <= positions[:, None])
    score_scale = HDIM ** (-0.5)
    scores = dot_last(query_rows, key_rows) * score_scale
    masked = jnp.where(visible, scores, NEG_BIG)
    top_score = jnp.max(masked, axis=1, keepdims=True)
    exp_scores = jnp.exp(masked - top_score)
    row_total = jnp.sum(exp_scores, axis=1, keepdims=True)
    probs = exp_scores / row_total
    probs_low = probs.astype(bf16)
    mixed = dot_plain(probs_low, value_rows).astype(bf16)
    mixer_part = dot_plain(mixed, w_out).astype(bf16)
    mixer_cols = jnp.sum(
        lax.all_to_all(cut_columns(mixer_part), TENSOR, 0, 0).astype(f32), axis=0
    )
    resid_cols = tokens.astype(f32) + mixer_cols
    resid_low = resid_cols.astype(bf16)

    resid_blocks = lax.all_gather(resid_low, TREES + TENSOR, axis=0)
    residual = side_by_side(spread(resid_low, TENSOR, NTP)).astype(f32)
    inverse_two = lax.rsqrt(jnp.mean(residual * residual, axis=1, keepdims=True) + EPSILON)
    hidden_two = (residual * inverse_two * gain_two).astype(bf16)
    logits = dot_last(switch_mat, hidden_two)
    gate_probs = jax.nn.softmax(logits[:EXPERTS], axis=0)
    switch = jax.nn.sigmoid(logits[EXPERTS:])
    expert_ids = jnp.arange(EXPERTS, dtype=jnp.int32)
    chosen = jnp.any(routes.T[None] == expert_ids[:, None, None], axis=1).astype(f32)
    mixing = jnp.concatenate([gate_probs * chosen, switch], axis=0)
    mixing_all = spread(mixing, TREES, NDP)

    grad_plain_all = dot_last(down_mat, whole_cot)
    grad_plain = lax.dynamic_slice_in_dim(grad_plain_all, tree * ROWS, ROWS, 1)
    gate_val = dot_last(gate_mat, hidden_two)
    up_val = dot_last(up_mat, hidden_two)
    spread_mix = per_hidden(mixing)
    act, grad_gate, grad_up = expert_terms(gate_val, up_val, grad_plain, spread_mix)
    mix_part = per_expert(act * grad_plain)
    stat_part = jnp.sum(grad_gate * gate_val + grad_up * up_val, axis=0, keepdims=True)
    high, low = halves(jnp.concatenate([mix_part, stat_part], axis=0))
    extras = jnp.concatenate([high, low], axis=0).reshape(-1, COLS)
    grad_part = dot_first(grad_gate.astype(bf16), gate_mat) + dot_first(
        grad_up.astype(bf16), up_mat
    )
    payload = jnp.concatenate(
        [
            cut_columns(grad_part.astype(bf16)),
            jnp.broadcast_to(extras[None], (NTP,) + extras.shape),
        ],
        axis=1,
    )
    arrived = lax.all_to_all(payload, TENSOR, 0, 0).astype(f32)
    ffn_part = dot_first((spread_mix * act).astype(bf16), down_mat).astype(bf16)
    ffn_cols = jnp.sum(
        lax.all_to_all(cut_columns(ffn_part), TENSOR, 0, 0).astype(f32), axis=0
    )
    output = (resid_cols + ffn_cols).astype(bf16)

    summed = jnp.sum(arrived, axis=0)
    sums = jnp.sum(summed[ROWS:].reshape(2, EXPERTS + 2, ROWS), axis=0)
    masked_grad = sums[:EXPERTS] * chosen
    logit_low = (
        gate_probs * (masked_grad - jnp.sum(gate_probs * masked_grad, axis=0, keepdims=True))
    ).astype(bf16)
    switch_low = (sums[EXPERTS : EXPERTS + 1] * switch * (1.0 - switch)).astype(bf16)
    router_low = jnp.concatenate([logit_low, switch_low], axis=0)
    grad_router = dot_plain(router_low, hidden_two)
    switch_cols = lax.dynamic_slice_in_dim(switch_mat, col_start, COLS, 1)
    grad_two = summed[:ROWS] + dot_first(router_low, switch_cols)
    stat_two = sums[EXPERTS + 1] + jnp.sum(router_low.astype(f32) * logits, axis=0)
    resid_used = resid_low.astype(f32)
    normed_two = resid_used * inverse_two
    grad_gain_two = jnp.sum(grad_two * normed_two, axis=0)
    grad_res = (
        inverse_two * (grad_two * gain_two_cols - normed_two * (stat_two / WIDTH)[:, None])
        + cotangent.astype(f32)
    )
    grad_attn = side_by_side(spread(grad_res.astype(bf16), TENSOR, NTP))

    out_part = dot_first(mixed, grad_attn).astype(bf16)
    early = jnp.concatenate(
        [
            out_part.reshape(NDP, -1, COLS),
            jnp.broadcast_to(
                grad_router.astype(bf16).reshape(1, -1, COLS), (NDP, 7 * NTP, COLS)
            ),
        ],
        axis=1,
    )
    early_sum = jnp.sum(lax.all_to_all(early, TREES, 0, 0).astype(f32), axis=0)
    out_rows = early_sum[: ROWS - 64].astype(bf16)
    router_sum = early_sum[ROWS - 64 :].reshape(7, WIDTH)
    grad_heads = dot_last(grad_attn, w_out).astype(bf16)
    dprobs = dot_last(grad_heads, value_rows)
    dscores = probs * (dprobs - jnp.sum(probs * dprobs, axis=1, keepdims=True))
    dscores_low = dscores.astype(bf16)
    dq_low = rotate(
        dot_plain(dscores_low, key_rows) * score_scale, cosine, -sine_table
    ).astype(bf16)
    dk_low = rotate(
        dot_first(dscores_low, query_rows) * score_scale, cosine, -sine_table
    ).astype(bf16)
    dv_low = dot_first(probs_low, grad_heads).astype(bf16)
    d_low = jnp.concatenate([dq_low, dk_low, dv_low], axis=1)
    d_wide = d_low.astype(f32)
    grad_bias = jnp.sum(d_wide, axis=0)
    part_one = dot_last(d_low, w_qkv)
    stat_one = jnp.sum(d_wide * plain, axis=1)
    gain_part = jnp.sum(part_one * normed_one, axis=0)
    high, low = halves(jnp.concatenate([gain_part, stat_one, jnp.zeros((192,), f32)]))
    high_own, low_own = halves(grad_gain_two)
    extras = jnp.concatenate([high, low, high_own, low_own, jnp.zeros((256,), bf16)])
    extras = extras.reshape(-1, COLS)
    payload = jnp.concatenate(
        [
            cut_columns(part_one.astype(bf16)),
            jnp.broadcast_to(extras[None], (NTP,) + extras.shape),
        ],
        axis=1,
    )
    arrived = lax.all_to_all(payload, TENSOR, 0, 0).astype(f32)
    late = jnp.concatenate(
        [cut_columns((d_wide * inverse_one).astype(bf16)).reshape(-1, COLS), out_rows], axis=0
    )
    late_all = spread(late, TREES, NDP)
    summed = jnp.sum(arrived, axis=0)
    grad_one = summed[:ROWS]
    pair = jnp.sum(summed[ROWS : ROWS + 40].reshape(2, -1), axis=0)
    gain_one_sum = pair[:WIDTH]
    stat_one_sum = pair[WIDTH : WIDTH + ROWS]
    gain_two_sum = (arrived[:, ROWS + 40] + arrived[:, ROWS + 41]).reshape(-1)
    normed_cols = tokens.astype(f32) * inverse_one
    input_grad = (
        inverse_one
        * (grad_one * gain_one_cols - normed_cols * (stat_one_sum / WIDTH)[:, None])
        + grad_res
    )
    small = jnp.concatenate([gain_one_sum, gain_two_sum, grad_bias, jnp.zeros((640,), f32)])
    small = jnp.sum(spread(small.reshape(-1, COLS), TREES, NDP), axis=0).reshape(-1)

    whole_resid = (
        jnp.transpose(resid_blocks.reshape(NDP, NTP, ROWS, COLS), (0, 2, 1, 3))
        .reshape(NDP * ROWS, WIDTH)
        .astype(f32)
    )
    inverse_all = lax.rsqrt(jnp.mean(whole_resid * whole_resid, axis=1, keepdims=True) + EPSILON)
    hidden_all = (whole_resid * inverse_all * gain_two).astype(bf16)
    mix_all = per_hidden(jnp.transpose(mixing_all, (1, 0, 2)).reshape(7, -1))
    gate_all = dot_last(gate_mat, hidden_all)
    up_all = dot_last(up_mat, hidden_all)
    act_all, grad_gate_all, grad_up_all = expert_terms(gate_all, up_all, grad_plain_all, mix_all)
    grad_gate_w = dot_plain(grad_gate_all.astype(bf16), hidden_all)
    grad_up_w = dot_plain(grad_up_all.astype(bf16), hidden_all)
    grad_down_w = dot_plain((mix_all * act_all).astype(bf16), whole_cot)

    token_blocks = lax.all_gather(tokens, TREES + TENSOR, axis=0)
    whole_tokens = jnp.transpose(
        token_blocks.reshape(NDP, NTP, ROWS, COLS), (0, 2, 1, 3)
    ).reshape(NDP * ROWS, WIDTH)
    d_all = jnp.transpose(
        late_all[:, : 3 * ROWS].reshape(NDP, 3, ROWS, COLS), (0, 2, 1, 3)
    ).reshape(NDP * ROWS, 3 * COLS)
    grad_qkv = dot_first(whole_tokens, d_all) * gain_one[:, None]
    grad_out_proj = late_all[:, 3 * ROWS :].reshape(COLS, WIDTH).astype(f32)

    def routed_cols(mat):
        return jnp.transpose(mat[:ROUTED].reshape(EXPERTS, EFF, WIDTH), (0, 2, 1))

    return (
        output,
        input_grad,
        small[:WIDTH],
        grad_qkv[:, :COLS],
        small[2 * WIDTH : 2 * WIDTH + COLS],
        grad_qkv[:, COLS : 2 * COLS],
        small[2 * WIDTH + COLS : 2 * WIDTH + 2 * COLS],
        grad_qkv[:, 2 * COLS :],
        small[2 * WIDTH + 2 * COLS : 2 * WIDTH + 3 * COLS],
        grad_out_proj,
        small[WIDTH : 2 * WIDTH],
        router_sum[:EXPERTS].T,
        routed_cols(grad_gate_w),
        routed_cols(grad_up_w),
        grad_down_w[:ROUTED].reshape(EXPERTS, EFF, WIDTH),
        grad_gate_w[ROUTED:].T,
        grad_up_w[ROUTED:].T,
        grad_down_w[ROUTED:],
        router_sum[EXPERTS],
    )


def solution(mesh):
    fine = Mesh(mesh.devices.reshape(4, 2, 2, 4, 2), TREES + TENSOR)
    both = P(TREES, TENSOR)
    cols = P(None, TENSOR)
    placed = (
        both,
        both,
        P(TREES, None),
        P(TREES),
        P(TREES),
        P(TREES),
        P(),
        cols,
        P(TENSOR),
        cols,
        P(TENSOR),
        cols,
        P(TENSOR),
        P(TENSOR, None),
        P(),
        P(),
        P(None, None, TENSOR),
        P(None, None, TENSOR),
        P(None, TENSOR, None),
        cols,
        cols,
        P(TENSOR, None),
        P(),
    )
    return jax.shard_map(
        on_device,
        mesh=fine,
        in_specs=placed,
        out_specs=(
            both,
            both,
            P(),
            cols,
            P(TENSOR),
            cols,
            P(TENSOR),
            cols,
            P(TENSOR),
            P(TENSOR, None),
            P(),
            P(),
            P(None, None, TENSOR),
            P(None, None, TENSOR),
            P(None, TENSOR, None),
            cols,
            cols,
            P(TENSOR, None),
            P(),
        ),
        check_vma=False,
    )
```

time: 1150 us -> 529 us (0.46)
  waiting for transfers between devices: 861 us -> 108 us
  local copies, waits for them, and re-layouts: 22.5 us -> 125 us
  blocking collectives: 93.5 us -> 25.8 us
  starting transfers between devices: 1.21 us -> 58.6 us
  matrix products: 101 us -> 148 us
    psum x2 -> x0, waiting for transfers between devices: 593 us -> none  [the longest x1 475 us: on_device(): lax.psum(grad_query.astype(jnp.bfloat16), 'dp').astype(jnp.float32)]
    psum x2 -> x0, blocking collectives: 93.5 us -> none  [the longest x1 54.8 us: on_device(): mix_grad, switch_grad = lax.psum((gate_part, switch_part), 'tensor')]
    unnamed x11 -> x3, waiting for transfers between devices: 82.9 us -> 1.39 us
    all_gather x4 -> x3, waiting for transfers between devices: 122 us -> 40.2 us  [the longest x1 40.2 us: on_device(): resid_blocks = lax.all_gather(resid_low, TREES + TENSOR, axis=0)]
    all_to_all x0 -> x10, waiting for transfers between devices: none -> 66.4 us  [the longest x6 52.8 us: spread(): lax.all_to_all(jnp.broadcast_to(block[None], (count,) + block.shape), axe...]
    reduce_scatter x1 -> x0, waiting for transfers between devices: 64 us -> none  [on_device(): lax.psum_scatter(mixer_part, 'tensor', scatter_dimension=1, tiled=True)]
    all_to_all x0 -> x10, starting transfers between devices: none -> 58.5 us  [the longest x6 37.3 us: spread(): lax.all_to_all(jnp.broadcast_to(block[None], (count,) + block.shape), axe...]
    dot_general x30 -> x8, matrix products: 30.6 us -> 68.9 us  [dot_plain(): return jnp.dot(left_mat, right_mat, preferred_element_type=f32)]
  transfers between devices with their start and end apart: 9 -> 13, of which waited for: 9 -> 6; matrix products, arithmetic and copies ran while one was open for 7% -> 52% of each run, Pallas kernels for 0% -> 0%
where the time goes in v1:
time: 529 us; the launch traced here: 522 us
  matrix products  148 us (28%)
  local copies, waits for them, and re-layouts  125 us (24%)
  waiting for transfers between devices  108 us (20%)
  starting transfers between devices  58.6 us (11%)
  other arithmetic  41.8 us (8%)
  blocking collectives  25.8 us (5%)
  between operations  15.3 us (3%)
    dot_general x8, matrix products, dot_plain(): return jnp.dot(left_mat, right_mat, preferred_element_type=f32)  68.9 us
    dot_general x10, matrix products, dot_last(): lax.dot_general(left_mat, right_mat, (((1,), (1,)), ((), ())), preferred_...  55.5 us
    all_to_all x6, waiting for transfers between devices, spread(): lax.all_to_all(jnp.broadcast_to(block[None], (count,) + block.shape), axe...  52.8 us
    all_gather x1, waiting for transfers between devices, on_device(): resid_blocks = lax.all_gather(resid_low, TREES + TENSOR, axis=0)  40.2 us
    all_to_all x6, starting transfers between devices, spread(): lax.all_to_all(jnp.broadcast_to(block[None], (count,) + block.shape), axe...  37.3 us
    all_to_all x1, blocking collectives, on_device(): lax.all_to_all(cut_columns(mixer_part), TENSOR, 0, 0).astype(f32)  25.8 us
    dot_general x8, matrix products, dot_first(): lax.dot_general(left_mat, right_mat, (((0,), (0,)), ((), ())), preferred_...  23.3 us
    unnamed x170, local copies, waits for them, and re-layouts  20.6 us
  transfers between devices with their start and end apart: 13, of which 6 were waited for; matrix products, arithmetic and copies ran while one was open for 52% of the time, Pallas kernels for 0%

profile of v1, /device:TPU:6, one launch (start us, length us, event | category | flops | bytes accessed | tf_op | source)
XLA Modules:
  0.0 522.5 jit_solution(3977631724865719707)
XLA Ops:
  11.0 6.1 %all-to-all-start = ((bf16[16,320,128]{2,1,0:T(8,128)(2,1)}), bf16[16,320,128]{2,1,0:T(8,128)(2,1)S(1)}, u32[]{:S(2)}, u32[]{:S(2)}) async-start(bf16[16,320,128]{2,1,0:T(8,128)(2,1)} %broadcast_in_dim.60), calls=%async_computation | async-start | bytes 2621440 | tf_op jit(solution)/shard_map/all_to_all | solution.py:45
  19.8 16.0 %all-to-all-done = bf16[16,320,128]{2,1,0:T(8,128)(2,1)S(1)} async-done(((bf16[16,320,128]{2,1,0:T(8,128)(2,1)}), bf16[16,320,128]{2,1,0:T(8,128)(2,1)S(1)}, u32[]{:S(2)}, u32[]{:S(2)}) %all-to-all-start) | async-done | bytes 1310752 | tf_op jit(solution)/shard_map/all_to_all | solution.py:45
  36.2 3.2 broadcast_add_fusion
  43.7 25.8 %all_to_all.55 = bf16[16,320,128]{2,1,0:T(8,128)(2,1)S(1)} all-to-all(bf16[16,320,128]{2,1,0:T(8,128)(2,1)S(1)} %bitcast.198), channel_id=1, replica_groups=mesh['z'=4,'xhi'=2,'xlo'=2,'y'=4,'core'=2] {'xlo','y','core'}, dimensions={0} | all-to-all | bytes 2621440 | tf_op jit(solution)/shard_map/all_to_all | solution.py:169
  73.2 4.9 all-to-all-start.2
  78.3 31.2 %all-to-all-done.2 = bf16[16,320,128]{2,1,0:T(8,128)(2,1)S(1)} async-done(((bf16[16,320,128]{2,1,0:T(8,128)(2,1)}), bf16[16,320,128]{2,1,0:T(8,128)(2,1)S(1)}, u32[]{:S(2)}, u32[]{:S(2)}) %all-to-all-start.2) | async-done | bytes 1310752 | tf_op jit(solution)/shard_map/all_to_all | solution.py:45
  112.1 7.7 %all-to-all-start.10 = ((f32[8,7,320]{2,1,0:T(8,128)}), f32[8,7,320]{2,1,0:T(8,128)}, u32[]{:S(2)}, u32[]{:S(2)}) async-start(f32[8,7,320]{2,1,0:T(8,128)} %broadcast_in_dim.164), calls=%async_computation.10 | async-start | bytes 196608 | tf_op jit(solution)/shard_map/all_to_all | solution.py:45
  121.1 4.6 fusion.50
  125.7 14.6 %copy.106 = bf16[8,16,320,128]{3,1,2,0:T(8,128)(2,1)} copy(bf16[8,16,320,128]{3,2,1,0:T(8,128)(2,1)} %bitcast.188) | data formatting | bytes 20971520 | tf_op jit(solution)/shard_map/reshape | solution.py:137
  140.3 13.9 %fusion.7 = f32[880,2560]{1,0:T(8,128)S(1)} fusion(bf16[320,8,16,128]{3,2,1,0:T(8,128)(2,1)} %bitcast.186, bf16[352,2048]{1,0:T(8,128)(2,1)} %param.44, bf16[528,2048]{1,0:T(8,128)(2,1)} %bitcast.216), kind=kOutput, calls=%fused_computation.9 | convolution fusion | flops 9234677760 | bytes 23101440 | tf_op jit(solution)/shard_map/dot_general | solution.py:33
  154.2 3.4 copy-done.40
  159.6 6.0 %multiply_multiply_fusion = (f32[880,320]{0,1:T(8,128)S(1)}, f32[320]{0:T(512)S(1)}, f32[880,320]{0,1:T(8,128)}) fusion(f32[880,320]{0,1:T(8,128)} %copy.119, f32[880,320]{0,1:T(8,128)} %fusion.50, f32[352,320]{0,1:T(8,128)S(1)} %broadcast_in_dim.66, f32[528,320]{0,1:T(8,128)} %copy.104, bf16[320,2048]{1,0:T(8,128)(2,1)S(1)} %fusion.26, ...), kind=kOutput, calls=%fused_computation.97 | convolution fusion | flops 1165992704 | bytes 10548480 | tf_op jit(solution)/shard_map/dot_general | solution.py:33
  168.4 4.9 fusion.30
  174.9 5.1 all-to-all-start.3
  180.0 5.6 %fusion.49 = f32[320,2048]{1,0:T(8,128)S(1)} fusion(bf16[352,2048]{1,0:T(8,128)(2,1)} %bitcast.225, bf16[528,2048]{1,0:T(8,128)(2,1)} %bitcast.219, f32[880,320]{0,1:T(8,128)} %fusion.50, f32[880,320]{0,1:T(8,128)} %get-tuple-element.175, f32[880,320]{0,1:T(8,128)} %copy.119, f32[352,320]{0,1:T(8,128)} %copy-done.26, f32[528,320]{0,1:T(8,128)} %copy.104), kind=kOutput, calls=%fused_computation.87 | convolution fusion | flops 1164021760 | bytes 10731520 | tf_op jit(solution)/shard_map/dot_general | solution.py:39
  189.1 9.1 %all-to-all-done.3 = bf16[16,320,128]{2,1,0:T(8,128)(2,1)S(1)} async-done(((bf16[16,320,128]{2,1,0:T(8,128)(2,1)}), bf16[16,320,128]{2,1,0:T(8,128)(2,1)S(1)}, u32[]{:S(2)}, u32[]{:S(2)}) %all-to-all-start.3) | async-done | bytes 1310752 | tf_op jit(solution)/shard_map/all_to_all | solution.py:209
  199.3 5.1 all-to-all-start.4
  208.2 14.8 %copy.113 = bf16[8,16,320,128]{3,1,2,0:T(8,128)(2,1)} copy(bf16[8,16,320,128]{3,2,1,0:T(8,128)(2,1)} %bitcast.185) | data formatting | bytes 20971520 | tf_op jit(solution)/shard_map/reshape | solution.py:312
  223.0 2.2 convert_reduce_fusion.1
  231.8 6.1 %all-to-all-start.5 = ((bf16[16,320,128]{2,1,0:T(8,128)(2,1)}), bf16[16,320,128]{2,1,0:T(8,128)(2,1)S(1)}, u32[]{:S(2)}, u32[]{:S(2)}) async-start(bf16[16,320,128]{2,1,0:T(8,128)(2,1)} %broadcast_in_dim.71), calls=%async_computation.5 | async-start | bytes 2621440 | tf_op jit(solution)/shard_map/all_to_all | solution.py:45
  238.4 40.2 %all-gather.11.cloned.1.call-done = bf16[40960,128]{1,0:T(8,128)(2,1)} async-done(((bf16[320,128]{1,0:T(8,128)(2,1)}), bf16[40960,128]{1,0:T(8,128)(2,1)}) %all-gather.11.cloned.1.call-update) | async-done | bytes 10485776 | tf_op jit(solution)/shard_map/all_gather | solution.py:174
  278.6 8.3 %multiply_reduce_fusion = f32[40960]{0:T(1024)S(1)} fusion(bf16[40960,128]{1,0:T(8,128)(2,1)} %all-gather.11.cloned.1.call-done), kind=kLoop, calls=%fused_computation.3 | loop fusion | flops 15687680 | bytes 10649600 | tf_op jit(solution)/shard_map/reduce_sum | solution.py:300
  287.2 17.1 %copy.115 = f32[8,16,320,128]{3,1,2,0:T(8,128)} copy(bf16[8,16,320,128]{3,2,1,0:T(8,128)(2,1)} %bitcast.183) | data formatting | bytes 31457280 | tf_op jit(solution)/shard_map/convert_element_type | solution.py:298
  304.3 15.1 %fusion.1 = bf16[2560,2048]{1,0:T(8,128)(2,1)S(1)} fusion(f32[320,8,16,128]{3,2,1,0:T(8,128)} %bitcast.182, f32[2048]{0:T(1024)S(1)} %convert_element_type.231, f32[2560]{0:T(1024)S(1)} %rsqrt.30), kind=kLoop, calls=%fused_computation.2 | loop fusion | flops 15728640 | bytes 31475712 | tf_op jit(solution)/shard_map/convert_element_type | solution.py:301
  319.4 12.3 %fusion.48 = f32[880,2560]{1,0:T(8,128)} fusion(bf16[2560,2048]{1,0:T(8,128)(2,1)S(1)} %fusion.1, bf16[352,2048]{1,0:T(8,128)(2,1)S(1)} %bitcast.226, bf16[528,2048]{1,0:T(8,128)(2,1)S(1)} %bitcast.220), kind=kOutput, calls=%fused_computation.86 | convolution fusion | flops 9234677760 | bytes 23101440 | tf_op jit(solution)/shard_map/dot_general | solution.py:33
  331.8 13.7 %fusion.46 = f32[880,2560]{1,0:T(8,128)} fusion(bf16[2560,2048]{1,0:T(8,128)(2,1)S(1)} %fusion.1, bf16[352,2048]{1,0:T(8,128)(2,1)} %bitcast.228, bf16[528,2048]{1,0:T(8,128)(2,1)} %bitcast.222), kind=kOutput, calls=%fused_computation.84 | convolution fusion | flops 9234677760 | bytes 23101440 | tf_op jit(solution)/shard_map/dot_general | solution.py:33
  345.4 2.2 broadcast_in_dim.168
  347.7 3.1 broadcast_in_dim.166
  350.7 21.0 %fusion.5 = f32[880,2048]{1,0:T(8,128)} fusion(bf16[320,8,16,128]{3,2,1,0:T(8,128)(2,1)} %bitcast.187, f32[352,2560]{1,0:T(8,128)} %broadcast_in_dim.168, f32[528,2560]{1,0:T(8,128)} %bitcast.192, f32[880,2560]{1,0:T(8,128)} %fusion.46, f32[880,2560]{1,0:T(8,128)} %fusion.48), kind=kOutput, calls=%fused_computation.7 | convolution fusion | flops 9245491200 | bytes 44728320 | tf_op jit(solution)/shard_map/dot_general | solution.py:29
  377.0 5.9 %all-to-all-start.8 = ((bf16[8,368,128]{2,1,0:T(8,128)(2,1)}), bf16[8,368,128]{2,1,0:T(8,128)(2,1)S(1)}, u32[]{:S(2)}, u32[]{:S(2)}) async-start(bf16[8,368,128]{2,1,0:T(8,128)(2,1)} %pad_maximum_fusion.17), calls=%async_computation.8 | async-start | bytes 1507328 | tf_op jit(solution)/shard_map/all_to_all | solution.py:244
  384.8 2.4 convert_bitcast_fusion.2
  390.3 4.4 all-to-all-done.8
  394.7 5.0 all-to-all-start.6
  399.7 22.8 %fusion.17 = f32[880,2048]{1,0:T(8,128)} fusion(bf16[2560,2048]{1,0:T(8,128)(2,1)} %copy-done.1, f32[880,2560]{1,0:T(8,128)} %fusion.48, f32[880,2560]{1,0:T(8,128)} %fusion.46, f32[880,2560]{1,0:T(8,128)} %copy-done.40, f32[352,2560]{1,0:T(8,128)} %broadcast_in_dim.168, f32[528,2560]{1,0:T(8,128)} %bitcast.193), kind=kOutput, calls=%fused_computation.22 | convolution fusion | flops 9254502400 | bytes 53739520 | tf_op jit(solution)/shard_map/dot_general | solution.py:29
  424.7 6.0 %all-to-all-start.7 = ((f32[8,40,128]{2,1,0:T(8,128)}), f32[8,40,128]{2,1,0:T(8,128)S(1)}, u32[]{:S(2)}, u32[]{:S(2)}) async-start(f32[8,40,128]{2,1,0:T(8,128)} %broadcast_in_dim.78), calls=%async_computation.7 | async-start | bytes 327680 | tf_op jit(solution)/shard_map/all_to_all | solution.py:45
  430.7 5.6 %all-to-all-done.7 = f32[8,40,128]{2,1,0:T(8,128)S(1)} async-done(((f32[8,40,128]{2,1,0:T(8,128)}), f32[8,40,128]{2,1,0:T(8,128)S(1)}, u32[]{:S(2)}, u32[]{:S(2)}) %all-to-all-start.7) | async-done | bytes 163872 | tf_op jit(solution)/shard_map/all_to_all | solution.py:45
  438.1 6.5 %all-to-all-start.9 = ((bf16[8,1216,128]{2,1,0:T(8,128)(2,1)}), bf16[8,1216,128]{2,1,0:T(8,128)(2,1)S(1)}, u32[]{:S(2)}, u32[]{:S(2)}) async-start(bf16[8,1216,128]{2,1,0:T(8,128)(2,1)} %broadcast_in_dim.81), calls=%async_computation.9 | async-start | bytes 4980736 | tf_op jit(solution)/shard_map/all_to_all | solution.py:45
  444.6 20.6 %fusion.15 = f32[880,2048]{1,0:T(8,128)} fusion(bf16[2560,2048]{1,0:T(8,128)(2,1)} %copy-done.1, f32[880,2560]{1,0:T(8,128)} %copy-done.40, f32[352,2560]{1,0:T(8,128)} %broadcast_in_dim.168, f32[528,2560]{1,0:T(8,128)} %bitcast.194, f32[880,2560]{1,0:T(8,128)} %fusion.48), kind=kOutput, calls=%fused_computation.21 | convolution fusion | flops 9245491200 | bytes 44728320 | tf_op jit(solution)/shard_map/dot_general | solution.py:29
  465.2 3.9 slice.261
  469.1 4.9 slice.258
  474.0 2.5 slice.257
  477.4 2.3 slice.256
  479.7 2.9 slice_bitcast_fusion
  491.9 2.4 reshape.327
  495.7 3.2 copy.112
  499.0 2.7 reshape.318
  501.7 7.6 %multiply_bitcast_fusion = f32[2048,384]{0,1:T(8,128)S(1)} fusion(bf16[2560,384]{0,1:T(8,128)(2,1)} %reshape.318, bf16[320,8,16,128]{3,2,1,0:T(8,128)(2,1)} %bitcast.184, f32[2048]{0:T(1024)S(1)} %copy-done.58), kind=kOutput, calls=%fused_computation.30 | convolution fusion | flops 4027318272 | bytes 15605760 | tf_op jit(solution)/shard_map/dot_general | solution.py:39
  510.6 2.5 copy.118
  (303 shorter events, 69.7 us)
Async XLA Ops:
  7.2 35.7 %copy-start = (bf16[128,2048]{1,0:T(8,128)(2,1)S(1)}, bf16[128,2048]{1,0:T(8,128)(2,1)}, u32[]{:S(2)}) copy-start(bf16[128,2048]{1,0:T(8,128)(2,1)} %param.36) | copy-start | bytes 1572868
  7.2 9.9 %copy-start.66 = (s32[320]{0:T(512)S(1)}, s32[320]{0:T(512)}, u32[]{:S(2)}) copy-start(s32[320]{0:T(512)} %param.28) | copy-start | bytes 3844
  7.2 9.9 %copy-start.62 = (bf16[2048]{0:T(1024)(128)(2,1)S(1)}, bf16[2048]{0:T(1024)(128)(2,1)}, u32[]{:S(2)}) copy-start(bf16[2048]{0:T(1024)(128)(2,1)} %param.29) | copy-start | bytes 12292
  7.2 9.9 %copy-start.67 = (bf16[128]{0:T(256)(128)(2,1)S(1)}, bf16[128]{0:T(256)(128)(2,1)}, u32[]{:S(2)}) copy-start(bf16[128]{0:T(256)(128)(2,1)} %param.35) | copy-start | bytes 772
  7.2 9.9 %copy-start.68 = (bf16[128]{0:T(256)(128)(2,1)S(1)}, bf16[128]{0:T(256)(128)(2,1)}, u32[]{:S(2)}) copy-start(bf16[128]{0:T(256)(128)(2,1)} %param.33) | copy-start | bytes 772
  7.2 9.9 %copy-start.69 = (bf16[128]{0:T(256)(128)(2,1)S(1)}, bf16[128]{0:T(256)(128)(2,1)}, u32[]{:S(2)}) copy-start(bf16[128]{0:T(256)(128)(2,1)} %param.31) | copy-start | bytes 772
  7.3 10.0 %copy-start.65 = (s32[320]{0:T(512)S(1)}, s32[320]{0:T(512)}, u32[]{:S(2)}) copy-start(s32[320]{0:T(512)} %param.26) | copy-start | bytes 3844
  7.3 10.0 %copy-start.21 = (bf16[2048,128]{1,0:T(8,128)(2,1)S(1)}, bf16[2048,128]{1,0:T(8,128)(2,1)}, u32[]{:S(2)}) copy-start(bf16[2048,128]{1,0:T(8,128)(2,1)} %param.30) | copy-start | bytes 1572868
  7.3 10.8 %copy-start.22 = (bf16[2048,128]{1,0:T(8,128)(2,1)S(1)}, bf16[2048,128]{1,0:T(8,128)(2,1)}, u32[]{:S(2)}) copy-start(bf16[2048,128]{1,0:T(8,128)(2,1)} %param.32) | copy-start | bytes 1572868
  7.3 118.4 %all-gather.7.cloned.1.call-start = ((), (), s32[]{:S(2)}) async-start(), calls=%async_computation.11 | async-start | bytes 10567680 | tf_op jit(solution)/shard_map/all_gather | solution.py:135
  8.0 200.2 %all-gather.9.cloned.1.call-start = ((), (), s32[]{:S(2)}) async-start(), calls=%async_computation.12 | async-start | bytes 10567680 | tf_op jit(solution)/shard_map/all_gather | solution.py:310
  11.0 8.0 %copy-start.23 = (bf16[2048,128]{1,0:T(8,128)(2,1)S(1)}, bf16[2048,128]{1,0:T(8,128)(2,1)}, u32[]{:S(2)}) copy-start(bf16[2048,128]{1,0:T(8,128)(2,1)} %param.34) | copy-start | bytes 1572868
  11.0 24.8 %all-to-all-start = ((bf16[16,320,128]{2,1,0:T(8,128)(2,1)}), bf16[16,320,128]{2,1,0:T(8,128)(2,1)S(1)}, u32[]{:S(2)}, u32[]{:S(2)}) async-start(bf16[16,320,128]{2,1,0:T(8,128)(2,1)} %broadcast_in_dim.60), calls=%async_computation | async-start | bytes 2621440 | tf_op jit(solution)/shard_map/all_to_all | solution.py:45
  17.1 261.6 %all-gather.11.cloned.1.call-start = ((), (), s32[]{:S(2)}) async-start(), calls=%async_computation.13 | async-start | bytes 10567680 | tf_op jit(solution)/shard_map/all_gather | solution.py:174
  17.1 22.2 %copy-start.49 = (f32[320]{0:T(512)}, f32[320]{0:T(512)S(1)}, u32[]{:S(2)}) copy-start(f32[320]{0:T(512)S(1)} %convert_element_type.221) | copy-start | bytes 3844
  17.1 22.2 %copy-start.57 = (f32[2048]{0:T(1024)}, f32[2048]{0:T(1024)S(1)}, u32[]{:S(2)}) copy-start(f32[2048]{0:T(1024)S(1)} %convert_element_type.218) | copy-start | bytes 24580
  17.2 22.2 %copy-start.63 = (f32[64]{0:T(128)}, f32[64]{0:T(128)S(1)}, u32[]{:S(2)}) copy-start(f32[64]{0:T(128)S(1)} %multiply_power_fusion) | copy-start | bytes 772
  43.7 26.6 %copy-start.13 = (bf16[320,128]{1,0:T(8,128)(2,1)S(1)}, bf16[320,128]{1,0:T(8,128)(2,1)}, u32[]{:S(2)}) copy-start(bf16[320,128]{1,0:T(8,128)(2,1)} %param.23) | copy-start | bytes 245764
  69.5 8.7 %copy-start.60 = (bf16[2048]{0:T(1024)(128)(2,1)S(1)}, bf16[2048]{0:T(1024)(128)(2,1)}, u32[]{:S(2)}) copy-start(bf16[2048]{0:T(1024)(128)(2,1)} %param.45) | copy-start | bytes 12292
  69.5 8.7 %copy-start.61 = (bf16[2048]{0:T(1024)(128)(2,1)S(1)}, bf16[2048]{0:T(1024)(128)(2,1)}, u32[]{:S(2)}) copy-start(bf16[2048]{0:T(1024)(128)(2,1)} %param.37) | copy-start | bytes 12292
  69.5 8.7 %copy-start.59 = (s32[320,4]{0,1:T(4,128)S(1)}, s32[320,4]{0,1:T(4,128)}, u32[]{:S(2)}) copy-start(s32[320,4]{0,1:T(4,128)} %param.25) | copy-start | bytes 15364
  73.2 36.2 %all-to-all-start.2 = ((bf16[16,320,128]{2,1,0:T(8,128)(2,1)}), bf16[16,320,128]{2,1,0:T(8,128)(2,1)S(1)}, u32[]{:S(2)}, u32[]{:S(2)}) async-start(bf16[16,320,128]{2,1,0:T(8,128)(2,1)} %broadcast_in_dim.63), calls=%async_computation.2 | async-start | bytes 2621440 | tf_op jit(solution)/shard_map/all_to_all | solution.py:45
  78.1 32.2 %copy-start.41 = (bf16[2048,6]{0,1:T(8,128)(2,1)S(1)}, bf16[2048,6]{0,1:T(8,128)(2,1)}, u32[]{:S(2)}) copy-start(bf16[2048,6]{0,1:T(8,128)(2,1)} %param.38) | copy-start | bytes 73732
  112.1 62.8 %all-to-all-start.10 = ((f32[8,7,320]{2,1,0:T(8,128)}), f32[8,7,320]{2,1,0:T(8,128)}, u32[]{:S(2)}, u32[]{:S(2)}) async-start(f32[8,7,320]{2,1,0:T(8,128)} %broadcast_in_dim.164), calls=%async_computation.10 | async-start | bytes 196608 | tf_op jit(solution)/shard_map/all_to_all | solution.py:45
  174.9 23.3 %all-to-all-start.3 = ((bf16[16,320,128]{2,1,0:T(8,128)(2,1)}), bf16[16,320,128]{2,1,0:T(8,128)(2,1)S(1)}, u32[]{:S(2)}, u32[]{:S(2)}) async-start(bf16[16,320,128]{2,1,0:T(8,128)(2,1)} %bitcast.196), calls=%async_computation.3 | async-start | bytes 2621440 | tf_op jit(solution)/shard_map/all_to_all | solution.py:209
  199.3 26.0 %all-to-all-start.4 = ((bf16[16,360,128]{2,1,0:T(8,128)(2,1)}), bf16[16,360,128]{2,1,0:T(8,128)(2,1)S(1)}, u32[]{:S(2)}, u32[]{:S(2)}) async-start(bf16[16,360,128]{2,1,0:T(8,128)(2,1)} %pad_maximum_fusion.7), calls=%async_computation.4 | async-start | bytes 2949120 | tf_op jit(solution)/shard_map/all_to_all | solution.py:206
  228.6 58.3 %copy-start.45 = (f32[320]{0:T(512)}, f32[320]{0:T(512)S(1)}, u32[]{:S(2)}) copy-start(f32[320]{0:T(512)S(1)} %add_multiply_fusion.1) | copy-start | bytes 3844
  231.8 139.9 %all-to-all-start.5 = ((bf16[16,320,128]{2,1,0:T(8,128)(2,1)}), bf16[16,320,128]{2,1,0:T(8,128)(2,1)S(1)}, u32[]{:S(2)}, u32[]{:S(2)}) async-start(bf16[16,320,128]{2,1,0:T(8,128)(2,1)} %broadcast_in_dim.71), calls=%async_computation.5 | async-start | bytes 2621440 | tf_op jit(solution)/shard_map/all_to_all | solution.py:45
  304.3 15.1 %copy-start.72 = (bf16[6,2048,88]{1,2,0:T(8,128)(2,1)S(1)}, bf16[6,2048,88]{1,2,0:T(8,128)(2,1)}, u32[]{:S(2)}) copy-start(bf16[6,2048,88]{1,2,0:T(8,128)(2,1)} %param.39) | copy-start | bytes 6488068
  304.3 15.1 %copy-start.74 = (bf16[2048,352]{0,1:T(8,128)(2,1)S(1)}, bf16[2048,352]{0,1:T(8,128)(2,1)}, u32[]{:S(2)}) copy-start(bf16[2048,352]{0,1:T(8,128)(2,1)} %param.42) | copy-start | bytes 4325380
  319.4 12.3 %copy-start.1 = (bf16[2560,2048]{1,0:T(8,128)(2,1)}, bf16[2560,2048]{1,0:T(8,128)(2,1)S(1)}, u32[]{:S(2)}) copy-start(bf16[2560,2048]{1,0:T(8,128)(2,1)S(1)} %fusion.1) | copy-start | bytes 31457284
  350.7 21.5 %copy-start.9 = (f32[320,320]{0,1:T(8,128)S(1)}, f32[320,320]{0,1:T(8,128)}, u32[]{:S(2)}) copy-start(f32[320,320]{0,1:T(8,128)} %copy-done.8) | copy-start | bytes 1228804
  350.7 21.5 %copy-start.54 = (f32[320]{0:T(512)S(1)}, f32[320]{0:T(512)}, u32[]{:S(2)}) copy-start(f32[320]{0:T(512)} %copy-done.53) | copy-start | bytes 3844
  350.7 21.5 %copy-start.56 = (f32[320]{0:T(512)S(1)}, f32[320]{0:T(512)}, u32[]{:S(2)}) copy-start(f32[320]{0:T(512)} %copy-done.55) | copy-start | bytes 3844
  375.7 7.2 %copy-start.50 = (f32[320]{0:T(512)S(1)}, f32[320]{0:T(512)}, u32[]{:S(2)}) copy-start(f32[320]{0:T(512)} %copy-done.49) | copy-start | bytes 3844
  375.7 7.2 %copy-start.64 = (f32[64]{0:T(128)S(1)}, f32[64]{0:T(128)}, u32[]{:S(2)}) copy-start(f32[64]{0:T(128)} %copy-done.63) | copy-start | bytes 772
  376.0 8.8 %copy-start.4 = (bf16[16,320,128]{2,1,0:T(8,128)(2,1)S(1)}, bf16[16,320,128]{2,1,0:T(8,128)(2,1)}, u32[]{:S(2)}) copy-start(bf16[16,320,128]{2,1,0:T(8,128)(2,1)} %copy-done.3) | copy-start | bytes 3932164
  376.0 8.8 %copy-start.48 = (f32[320]{0:T(512)S(1)}, f32[320]{0:T(512)}, u32[]{:S(2)}) copy-start(f32[320]{0:T(512)} %copy-done.47) | copy-start | bytes 3844
  377.0 17.7 %all-to-all-start.8 = ((bf16[8,368,128]{2,1,0:T(8,128)(2,1)}), bf16[8,368,128]{2,1,0:T(8,128)(2,1)S(1)}, u32[]{:S(2)}, u32[]{:S(2)}) async-start(bf16[8,368,128]{2,1,0:T(8,128)(2,1)} %pad_maximum_fusion.17), calls=%async_computation.8 | async-start | bytes 1507328 | tf_op jit(solution)/shard_map/all_to_all | solution.py:244
  394.7 28.8 %all-to-all-start.6 = ((bf16[16,364,128]{2,1,0:T(8,128)(2,1)}), bf16[16,364,128]{2,1,0:T(8,128)(2,1)S(1)}, u32[]{:S(2)}, u32[]{:S(2)}) async-start(bf16[16,364,128]{2,1,0:T(8,128)(2,1)} %pad_maximum_fusion.6), calls=%async_computation.6 | async-start | bytes 3014656 | tf_op jit(solution)/shard_map/all_to_all | solution.py:275
  399.7 22.8 %copy-start.36 = (bf16[320,128]{1,0:T(8,128)(2,1)S(1)}, bf16[320,128]{1,0:T(8,128)(2,1)}, u32[]{:S(2)}) copy-start(bf16[320,128]{1,0:T(8,128)(2,1)} %convolution_convert_fusion.4) | copy-start | bytes 245764
  424.7 11.6 %all-to-all-start.7 = ((f32[8,40,128]{2,1,0:T(8,128)}), f32[8,40,128]{2,1,0:T(8,128)S(1)}, u32[]{:S(2)}, u32[]{:S(2)}) async-start(f32[8,40,128]{2,1,0:T(8,128)} %broadcast_in_dim.78), calls=%async_computation.7 | async-start | bytes 327680 | tf_op jit(solution)/shard_map/all_to_all | solution.py:45
  438.1 52.8 %all-to-all-start.9 = ((bf16[8,1216,128]{2,1,0:T(8,128)(2,1)}), bf16[8,1216,128]{2,1,0:T(8,128)(2,1)S(1)}, u32[]{:S(2)}, u32[]{:S(2)}) async-start(bf16[8,1216,128]{2,1,0:T(8,128)(2,1)} %broadcast_in_dim.81), calls=%async_computation.9 | async-start | bytes 4980736 | tf_op jit(solution)/shard_map/all_to_all | solution.py:45
  465.2 8.8 %copy-start.2 = (f32[880,2048]{1,0:T(8,128)S(1)}, f32[880,2048]{1,0:T(8,128)}, u32[]{:S(2)}) copy-start(f32[880,2048]{1,0:T(8,128)} %fusion.15) | copy-start | bytes 21626884
  469.1 7.4 %slice-start = ((s8[7208960]{0:T(1024)(128)(4,1)}), s8[4194304]{0:T(1024)(128)(4,1)S(1)}, s32[]{:S(2)}) async-start(s8[7208960]{0:T(1024)(128)(4,1)} %bitcast.190), calls=%async_computation.14 | async-start | bytes 8388608
  479.7 7.1 %copy-start.14 = (bf16[320,128]{1,0:T(8,128)(2,1)S(1)}, bf16[320,128]{1,0:T(8,128)(2,1)}, u32[]{:S(2)}) copy-start(bf16[320,128]{1,0:T(8,128)(2,1)} %param.23) | copy-start | bytes 245764
  479.7 7.1 %copy-start.44 = (f32[320]{0:T(512)S(1)}, f32[320]{0:T(512)}, u32[]{:S(2)}) copy-start(f32[320]{0:T(512)} %copy-done.43) | copy-start | bytes 3844
  479.7 7.1 %copy-start.46 = (f32[320]{0:T(512)S(1)}, f32[320]{0:T(512)}, u32[]{:S(2)}) copy-start(f32[320]{0:T(512)} %copy-done.45) | copy-start | bytes 3844
  (45 other events, 122.1 us)
Sparse Core Ops, SparseCore 0:
  11.3 98.8 all-gather.6
  113.3 71.8 all-gather.8
  188.9 89.6 all-gather.10

commit v2 on v1

v2 whole, which is shorter than its diff:
```python
import functools

import jax
import jax.numpy as jnp
from jax import lax
from jax.experimental import pallas as pl
from jax.experimental.pallas import tpu as pltpu
from jax.sharding import Mesh
from jax.sharding import PartitionSpec as P

HDIM = 128
HALF = HDIM // 2
EPSILON = 1e-06
THETA = 1000000.0
NEG_BIG = -1e30
TREES = ("z", "xhi")
CHIPS = ("xlo", "y")
TENSOR = ("xlo", "y", "core")
SWAP = [(0, 1), (1, 0)]
NDP = 8
NCHIP = 8
NTP = 16
ROWS = 320
COLS = 128
WIDTH = 2048
EXPERTS = 6
EFF = 88
ROUTED = EXPERTS * EFF
SHARED = 352
HIDDEN = ROUTED + SHARED
ALL_ROWS = NDP * ROWS
EXTRA = 24
SHOWN = 32
SENT = ROWS + 2 * EXTRA
QKV = 3 * HDIM
OUT_CHUNK = HDIM // NDP
QKV_CHUNK = QKV // NDP
SCALE = HDIM ** (-0.5)
f32 = jnp.float32
bf16 = jnp.bfloat16
MIB = 1024 * 1024


def dot_plain(left_mat, right_mat):
    return jnp.dot(left_mat, right_mat, preferred_element_type=f32)


def dot_last(left_mat, right_mat):
    return lax.dot_general(
        left_mat, right_mat, (((1,), (1,)), ((), ())), preferred_element_type=f32
    )


def dot_first(left_mat, right_mat):
    return lax.dot_general(
        left_mat, right_mat, (((0,), (0,)), ((), ())), preferred_element_type=f32
    )


def sds(shape, dtype):
    return jax.ShapeDtypeStruct(shape, dtype)


def call(body, out_shape, args, *, scratch=(), smem=0, flops=0, moved=0, limit=24):
    specs = [pl.BlockSpec(memory_space=pltpu.SMEM)] * smem
    specs += [pl.BlockSpec(memory_space=pltpu.VMEM)] * (len(args) - smem)
    return pl.pallas_call(
        body,
        in_specs=specs,
        out_specs=[pl.BlockSpec(memory_space=pltpu.VMEM)] * len(out_shape),
        out_shape=out_shape,
        scratch_shapes=list(scratch),
        compiler_params=pltpu.CompilerParams(vmem_limit_bytes=limit * MIB),
        cost_estimate=pl.CostEstimate(flops=flops, bytes_accessed=moved, transcendentals=0),
    )(*args)


def lay_rows(rows_ref, core, own_ref, other_ref):
    for chip in range(NCHIP):
        own = pl.multiple_of((2 * chip + core) * COLS, COLS)
        other = pl.multiple_of((2 * chip + 1 - core) * COLS, COLS)
        rows_ref[:, pl.ds(own, COLS)] = own_ref[chip]
        rows_ref[:, pl.ds(other, COLS)] = other_ref[chip]


def part_chips(core, part, keep_ref, send_ref):
    first = core == 0
    for chip in range(NCHIP):
        even = part[:, 2 * chip * COLS : (2 * chip + 1) * COLS]
        odd = part[:, (2 * chip + 1) * COLS : (2 * chip + 2) * COLS]
        keep_ref[chip] = jnp.where(first, even, odd).astype(keep_ref.dtype)
        send_ref[chip] = jnp.where(first, odd, even).astype(send_ref.dtype)


def rotate(rows, cosine, sine_table):
    first, second = rows[:, :HALF], rows[:, HALF:]
    return jnp.concatenate(
        [first * cosine - second * sine_table, second * cosine + first * sine_table], axis=1
    )


def to_row(column):
    return jnp.transpose(jnp.broadcast_to(column, (column.shape[0], COLS)))[:1]


def to_columns(row):
    return jnp.transpose(jnp.broadcast_to(row, (COLS, row.shape[1])))


def sigmoid(values):
    return 0.5 * jnp.tanh(0.5 * values) + 0.5


def per_hidden(weights):
    count = weights.shape[1]
    parts = [jnp.broadcast_to(weights[e : e + 1], (EFF, count)) for e in range(EXPERTS)]
    parts.append(jnp.broadcast_to(weights[EXPERTS : EXPERTS + 1], (SHARED, count)))
    return jnp.concatenate(parts, axis=0)


def routing(rows, inv_row, switch_mat):
    logits = dot_last(switch_mat, rows) * inv_row
    place = lax.broadcasted_iota(jnp.int32, logits.shape, 0)
    shown = jnp.where(place < EXPERTS, logits, NEG_BIG)
    powers = jnp.exp(shown - jnp.max(shown, axis=0, keepdims=True))
    probs = powers / jnp.sum(powers, axis=0, keepdims=True)
    return logits, jnp.where(place == EXPERTS, sigmoid(logits), probs)


def mean_square_inverse(rows):
    wide = rows.astype(f32)
    return lax.rsqrt(jnp.sum(wide * wide, axis=1, keepdims=True) * (1.0 / WIDTH) + EPSILON)


def attend_body(
    core_ref, own_ref, other_ref, w_ref, bias_ref, cos_ref, sin_ref, see_ref, w_out_ref,
    keep_ref, send_ref, rows_ref, inv_ref, plain_ref, qkv_ref, probs_ref, mixed_ref,
):
    core = core_ref[0]
    lay_rows(rows_ref, core, own_ref, other_ref)
    rows = rows_ref[...]
    inverse = mean_square_inverse(rows)
    inv_ref[...] = jnp.broadcast_to(inverse, (ROWS, COLS))
    plain = dot_plain(rows, w_ref[...]) * inverse
    plain_ref[...] = plain
    biased = plain + bias_ref[...]
    cosine, sine_table = cos_ref[...], sin_ref[...]
    query = rotate(biased[:, :HDIM], cosine, sine_table).astype(bf16)
    keys = rotate(biased[:, HDIM : 2 * HDIM], cosine, sine_table).astype(bf16)
    values = biased[:, 2 * HDIM :].astype(bf16)
    qkv_ref[:, :HDIM] = query
    qkv_ref[:, HDIM : 2 * HDIM] = keys
    qkv_ref[:, 2 * HDIM :] = values
    scores = dot_last(query, keys) * SCALE
    masked = jnp.where(see_ref[...] > 0.5, scores, NEG_BIG)
    powers = jnp.exp(masked - jnp.max(masked, axis=1, keepdims=True))
    probs = powers / jnp.sum(powers, axis=1, keepdims=True)
    probs_ref[...] = probs
    mixed = dot_plain(probs.astype(bf16), values).astype(bf16)
    mixed_ref[...] = mixed
    part_chips(core, dot_plain(mixed, w_out_ref[...]), keep_ref, send_ref)


def residual_body(tokens_ref, arrived_ref, resid_ref, wide_ref):
    total = tokens_ref[...].astype(f32)
    for chip in range(NCHIP):
        total = total + arrived_ref[chip].astype(f32)
    resid_ref[...] = total
    low = total.astype(bf16)
    for chip in range(NCHIP):
        wide_ref[chip] = low


def plain_grad_body(core_ref, own_ref, other_ref, down_ref, out_ref, rows_ref):
    lay_rows(rows_ref, core_ref[0], own_ref, other_ref)
    out_ref[...] = dot_last(down_ref[...], rows_ref[...])


def experts_body(
    core_ref, own_ref, other_ref, chosen_ref, switch_ref, gate_ref, up_ref, plain_ref,
    keep_ref, send_ref, act_ref, extra_ref, rows_ref, inv_ref, inv_row_ref, probs_ref, logits_ref,
):
    core = core_ref[0]
    lay_rows(rows_ref, core, own_ref, other_ref)
    rows = rows_ref[...]
    inverse = mean_square_inverse(rows)
    inv_ref[...] = jnp.broadcast_to(inverse, (ROWS, COLS))
    inv_row = to_row(inverse)
    inv_row_ref[...] = inv_row
    logits, probs = routing(rows, inv_row, switch_ref[...])
    logits_ref[...] = logits
    probs_ref[...] = probs
    mixing = probs * chosen_ref[...]
    gate_val = dot_last(gate_ref[...], rows) * inv_row
    up_val = dot_last(up_ref[...], rows) * inv_row
    spread_mix = per_hidden(mixing)
    sigma = sigmoid(gate_val)
    silu = gate_val * sigma
    act = silu * up_val
    grad_plain = plain_ref[...]
    pair = act * grad_plain
    grad_act = spread_mix * grad_plain
    grad_gate = grad_act * up_val * (sigma + silu * (1.0 - sigma))
    grad_up = grad_act * silu
    sums = [
        jnp.sum(pair[e * EFF : (e + 1) * EFF], axis=0, keepdims=True) for e in range(EXPERTS)
    ]
    sums.append(jnp.sum(pair[ROUTED:], axis=0, keepdims=True))
    sums.append(jnp.sum(grad_gate * gate_val + grad_up * up_val, axis=0, keepdims=True))
    sums = jnp.concatenate(sums, axis=0)
    extra_ref[0] = sums[:, :COLS]
    extra_ref[1] = sums[:, COLS : 2 * COLS]
    extra_ref[2] = jnp.concatenate([sums[:, 2 * COLS :], jnp.zeros((8, HALF), f32)], axis=1)
    part = dot_first(grad_gate.astype(bf16), gate_ref[...])
    part = part + dot_first(grad_up.astype(bf16), up_ref[...])
    part_chips(core, part, keep_ref, send_ref)
    act_ref[...] = (spread_mix * act).astype(bf16)


def branches_body(act_ref, down_ref, out_ref):
    part = dot_first(act_ref[...], down_ref[...]).astype(bf16)
    for block in range(NTP):
        out_ref[block * ROWS : (block + 1) * ROWS] = part[:, block * COLS : (block + 1) * COLS]


def payload_body(keep_ref, came_ref, extra_ref, extra_came_ref, out_ref):
    extra = extra_ref[...] + extra_came_ref[...]
    high = extra.astype(bf16)
    low = (extra - high.astype(f32)).astype(bf16)
    for chip in range(NCHIP):
        out_ref[chip, :ROWS] = (keep_ref[chip] + came_ref[chip].astype(f32)).astype(bf16)
        out_ref[chip, ROWS:] = jnp.concatenate([high, low], axis=0)


def second_norm_body(
    core_ref, arrived_ref, probs_ref, chosen_ref, logits_ref, inv_row_ref, switch_ref, cot_ref,
    resid_ref, inv_ref, gain_ref, wide_ref, grad_ref, router_ref, extra_ref,
):
    dn = arrived_ref[0, :ROWS].astype(f32)
    extra = arrived_ref[0, ROWS:].astype(f32)
    for chip in range(1, NCHIP):
        dn = dn + arrived_ref[chip, :ROWS].astype(f32)
        extra = extra + arrived_ref[chip, ROWS:].astype(f32)
    extra = extra[:EXTRA] + extra[EXTRA:]
    sums = jnp.concatenate([extra[:8], extra[8:16], extra[16:24]], axis=1)[:, :ROWS]
    place = lax.broadcasted_iota(jnp.int32, (8, ROWS), 0)
    probs = probs_ref[...]
    routed = place < EXPERTS
    weighed = jnp.where(routed, probs * (sums * chosen_ref[...]), 0.0)
    total = jnp.sum(weighed, axis=0, keepdims=True)
    low = jnp.where(routed, weighed - probs * total, sums * probs * (1.0 - probs))
    low = jnp.where(place <= EXPERTS, low, 0.0).astype(bf16)
    low_wide = low.astype(f32)
    router_ref[...] = (low_wide * inv_row_ref[...]).astype(bf16)
    dn = dn + dot_first(low, switch_ref[...])
    stat = sums[EXPERTS + 1 :] + jnp.sum(low_wide * logits_ref[...], axis=0, keepdims=True)
    inverse = inv_ref[...]
    normed = resid_ref[...].astype(bf16).astype(f32) * inverse
    own = jnp.sum(dn * normed, axis=0, keepdims=True) / gain_ref[...]
    first = core_ref[0] == 0
    spot = lax.broadcasted_iota(jnp.int32, (8, COLS), 0)
    extra_ref[...] = jnp.where(spot == jnp.where(first, 0, 1), own, 0.0)
    grad = inverse * (dn - normed * (to_columns(stat) * (1.0 / WIDTH)))
    grad = grad + cot_ref[...].astype(f32)
    grad_ref[...] = grad
    low_grad = grad.astype(bf16)
    for chip in range(NCHIP):
        wide_ref[chip] = low_grad


def attend_back_body(
    core_ref, own_ref, other_ref, w_out_ref, qkv_ref, probs_ref, mixed_ref, plain_ref, inv_ref,
    cos_ref, sin_ref, w_ref, rows_ref, router_ref, rows_two_ref, gain_two_ref, gain_own_ref,
    keep_ref, send_ref, extra_ref, trees_ref, tail_ref, grad_rows_ref,
):
    core = core_ref[0]
    lay_rows(grad_rows_ref, core, own_ref, other_ref)
    grad_attn = grad_rows_ref[...]
    query, keys = qkv_ref[:, :HDIM], qkv_ref[:, HDIM : 2 * HDIM]
    values = qkv_ref[:, 2 * HDIM :]
    probs = probs_ref[...]
    heads = dot_last(grad_attn, w_out_ref[...]).astype(bf16)
    dprobs = dot_last(heads, values)
    dscores = probs * (dprobs - jnp.sum(probs * dprobs, axis=1, keepdims=True))
    dscores = dscores.astype(bf16)
    cosine, sine_table = cos_ref[...], -sin_ref[...]
    dq = rotate(dot_plain(dscores, keys) * SCALE, cosine, sine_table)
    dk = rotate(dot_first(dscores, query) * SCALE, cosine, sine_table)
    dv = dot_first(probs.astype(bf16), heads)
    d_low = jnp.concatenate([dq, dk, dv], axis=1).astype(bf16)
    d_wide = d_low.astype(f32)
    part = dot_last(d_low, w_ref[...])
    part_chips(core, part, keep_ref, send_ref)
    inverse = inv_ref[...]
    rows = rows_ref[...]
    normed = rows.astype(f32) * inverse[:, :1]
    gains = jnp.sum(part * normed, axis=0, keepdims=True)
    for block in range(NTP):
        extra_ref[block : block + 1] = gains[:, block * COLS : (block + 1) * COLS]
    stat = to_row(jnp.sum(d_wide * plain_ref[...], axis=1, keepdims=True))
    stat = jnp.concatenate([stat, jnp.zeros((1, HALF), f32)], axis=1)
    for block in range(3):
        extra_ref[NTP + block : NTP + block + 1] = stat[:, block * COLS : (block + 1) * COLS]
    extra_ref[NTP + 3 :] = gain_own_ref[: EXTRA - NTP - 3]
    scaled = (d_wide * jnp.concatenate([inverse] * 3, axis=1)).astype(bf16)
    grad_w = dot_first(scaled, rows).astype(bf16)
    grad_out = dot_first(mixed_ref[...], grad_attn).astype(bf16)
    for tree in range(NDP):
        trees_ref[tree, :QKV_CHUNK] = grad_w[tree * QKV_CHUNK : (tree + 1) * QKV_CHUNK]
        trees_ref[tree, QKV_CHUNK:] = grad_out[tree * OUT_CHUNK : (tree + 1) * OUT_CHUNK]
    bias = jnp.sum(d_wide, axis=0, keepdims=True)
    bias = jnp.concatenate([bias, jnp.zeros((1, WIDTH - QKV), f32)], axis=1)
    router = dot_plain(router_ref[...], rows_two_ref[...]) * gain_two_ref[...]
    place = lax.broadcasted_iota(jnp.int32, (8, WIDTH), 0)
    router = jnp.where(place == EXPERTS + 1, bias, router)
    tail_ref[...] = router


def first_norm_body(arrived_ref, tokens_ref, inv_ref, grad_res_ref, out_ref, small_ref):
    dn = arrived_ref[0, :ROWS].astype(f32)
    tails = [arrived_ref[chip, ROWS:].astype(f32) for chip in range(NCHIP)]
    for chip in range(1, NCHIP):
        dn = dn + arrived_ref[chip, :ROWS].astype(f32)
    tails = [tail[:EXTRA] + tail[EXTRA:] for tail in tails]
    extra = sum(tails[1:], tails[0])
    stat = jnp.concatenate([extra[NTP + k : NTP + k + 1] for k in range(3)], axis=1)
    stat = to_columns(stat)[:ROWS] * (1.0 / WIDTH)
    inverse = inv_ref[...]
    normed = tokens_ref[...].astype(f32) * inverse
    out_ref[...] = inverse * (dn - normed * stat) + grad_res_ref[...]
    small_ref[...] = jnp.zeros((8, WIDTH), f32)
    for block in range(NTP):
        spot = slice(block * COLS, (block + 1) * COLS)
        small_ref[0:1, spot] = extra[block : block + 1]
        place = NTP + 3 + block % 2
        small_ref[1:2, spot] = tails[block // 2][place : place + 1]


def trees_body(arrived_ref, tail_ref, small_ref, out_ref):
    total = arrived_ref[0].astype(f32)
    for tree in range(1, NDP):
        total = total + arrived_ref[tree].astype(f32)
    low = total.astype(bf16)
    tail = jnp.concatenate([tail_ref[...], small_ref[...]], axis=0).astype(bf16)
    for tree in range(NDP):
        out_ref[tree, : QKV_CHUNK + OUT_CHUNK] = low
        out_ref[tree, QKV_CHUNK + OUT_CHUNK :] = tail


def last_body(all_ref, gain_ref, query_ref, key_ref, value_ref, out_ref, tail_ref):
    mats = jnp.concatenate([all_ref[tree, :QKV_CHUNK] for tree in range(NDP)], axis=0)
    mats = mats.astype(f32) * gain_ref[...]
    query_ref[...] = jnp.transpose(mats[:HDIM])
    key_ref[...] = jnp.transpose(mats[HDIM : 2 * HDIM])
    value_ref[...] = jnp.transpose(mats[2 * HDIM :])
    start = QKV_CHUNK + OUT_CHUNK
    tail = jnp.zeros((16, WIDTH), f32)
    for tree in range(NDP):
        out_ref[tree * OUT_CHUNK : (tree + 1) * OUT_CHUNK] = all_ref[
            tree, QKV_CHUNK:start
        ].astype(f32)
        tail = tail + all_ref[tree, start:].astype(f32)
    tail_ref[...] = tail


def lay_trees(rows_ref, blocks_ref, trees):
    for tree in range(trees):
        for block in range(NTP):
            rows_ref[tree * ROWS : (tree + 1) * ROWS, block * COLS : (block + 1) * COLS] = (
                blocks_ref[tree, block, :ROWS]
            )


def plain_all_body(blocks_ref, down_ref, out_ref, rows_ref):
    lay_trees(rows_ref, blocks_ref, 2)
    out_ref[...] = dot_last(down_ref[...], rows_ref[...])


def hidden_all_body(
    blocks_ref, plain_ref, chosen_ref, switch_ref, gate_ref, up_ref,
    grad_gate_ref, grad_up_ref, act_ref, rows_ref,
):
    lay_trees(rows_ref, blocks_ref, 2)
    rows = rows_ref[...]
    inverse = to_row(mean_square_inverse(rows))
    chosen = []
    for tree in range(2):
        shown = chosen_ref[tree].astype(f32)
        chosen.append(
            jnp.concatenate([shown[:8], shown[8:16], shown[16:24]], axis=1)[:, :ROWS]
        )
    _, probs = routing(rows, inverse, switch_ref[...])
    mix = probs * jnp.concatenate(chosen, axis=1)
    gate_val = dot_last(gate_ref[...], rows) * inverse
    up_val = dot_last(up_ref[...], rows) * inverse
    spread_mix = per_hidden(mix)
    sigma = sigmoid(gate_val)
    silu = gate_val * sigma
    act_ref[...] = (spread_mix * (silu * up_val)).astype(bf16)
    grad_act = (spread_mix * inverse) * plain_ref[...]
    grad_gate_ref[...] = (grad_act * up_val * (sigma + silu * (1.0 - sigma))).astype(bf16)
    grad_up_ref[...] = (grad_act * silu).astype(bf16)


def weights_body(
    grad_gate_ref, grad_up_ref, act_ref, resid_ref, cot_ref, gain_ref,
    gate_r_ref, gate_s_ref, up_r_ref, up_s_ref, down_r_ref, down_s_ref,
):
    resid = jnp.concatenate(
        [resid_ref[:, k].reshape(ALL_ROWS, COLS) for k in range(2)], axis=1
    )
    cot = jnp.concatenate(
        [cot_ref[:, k, :ROWS].reshape(ALL_ROWS, COLS) for k in range(2)], axis=1
    )
    gain = gain_ref[...]
    grad = dot_plain(grad_gate_ref[...], resid) * gain
    gate_r_ref[...] = grad[:ROUTED]
    gate_s_ref[...] = grad[ROUTED:]
    grad = dot_plain(grad_up_ref[...], resid) * gain
    up_r_ref[...] = grad[:ROUTED]
    up_s_ref[...] = grad[ROUTED:]
    grad = dot_plain(act_ref[...], cot)
    down_r_ref[...] = grad[:ROUTED]
    down_s_ref[...] = grad[ROUTED:]


def once(shape):
    zero = (0,) * len(shape)
    return pl.BlockSpec(shape, lambda i: zero, pipeline_mode=pl.Buffered(1))


PAIR = 2 * ROWS
PAIR_FLOPS = 2 * HIDDEN * WIDTH * ALL_ROWS


def plain_all(blocks, down_mat):
    return pl.pallas_call(
        plain_all_body,
        grid=(NDP // 2,),
        in_specs=[
            pl.BlockSpec((2, NTP, ROWS + SHOWN, COLS), lambda i: (i, 0, 0, 0)),
            once((HIDDEN, WIDTH)),
        ],
        out_specs=pl.BlockSpec((HIDDEN, PAIR), lambda i: (0, i)),
        out_shape=sds((HIDDEN, ALL_ROWS), f32),
        scratch_shapes=[pltpu.VMEM((PAIR, WIDTH), bf16)],
        compiler_params=pltpu.CompilerParams(vmem_limit_bytes=28 * MIB),
        cost_estimate=pl.CostEstimate(
            flops=PAIR_FLOPS, bytes_accessed=23 * MIB, transcendentals=0
        ),
    )(blocks, down_mat)


def hidden_all(blocks, plain, chosen, switch_mat, gate_mat, up_mat):
    return pl.pallas_call(
        hidden_all_body,
        grid=(NDP // 2,),
        in_specs=[
            pl.BlockSpec((2, NTP, ROWS, COLS), lambda i: (i, 0, 0, 0)),
            pl.BlockSpec((HIDDEN, PAIR), lambda i: (0, i)),
            pl.BlockSpec((2, SHOWN, COLS), lambda i: (i, 0, 0)),
            once((8, WIDTH)),
            once((HIDDEN, WIDTH)),
            once((HIDDEN, WIDTH)),
        ],
        out_specs=[pl.BlockSpec((HIDDEN, PAIR), lambda i: (0, i))] * 3,
        out_shape=[sds((HIDDEN, ALL_ROWS), bf16)] * 3,
        scratch_shapes=[pltpu.VMEM((PAIR, WIDTH), bf16)],
        compiler_params=pltpu.CompilerParams(vmem_limit_bytes=44 * MIB),
        cost_estimate=pl.CostEstimate(
            flops=2 * PAIR_FLOPS, bytes_accessed=40 * MIB, transcendentals=HIDDEN * ALL_ROWS
        ),
    )(blocks, plain, chosen, switch_mat, gate_mat, up_mat)


def weight_grads(grad_gate, grad_up, act, resid, cot, gain):
    step = 2 * COLS
    wide = pl.BlockSpec((NDP, 2, ROWS, COLS), lambda i: (0, i, 0, 0))
    tall = pl.BlockSpec((NDP, 2, ROWS + SHOWN, COLS), lambda i: (0, i, 0, 0))
    return pl.pallas_call(
        weights_body,
        grid=(WIDTH // step,),
        in_specs=[
            once((HIDDEN, ALL_ROWS)),
            once((HIDDEN, ALL_ROWS)),
            once((HIDDEN, ALL_ROWS)),
            wide,
            tall,
            pl.BlockSpec((1, step), lambda i: (0, i)),
        ],
        out_specs=[
            pl.BlockSpec((ROUTED, step), lambda i: (0, i)),
            pl.BlockSpec((SHARED, step), lambda i: (0, i)),
        ]
        * 3,
        out_shape=[sds((ROUTED, WIDTH), f32), sds((SHARED, WIDTH), f32)] * 3,
        compiler_params=pltpu.CompilerParams(vmem_limit_bytes=44 * MIB),
        cost_estimate=pl.CostEstimate(
            flops=3 * PAIR_FLOPS, bytes_accessed=56 * MIB, transcendentals=0
        ),
    )(grad_gate, grad_up, act, resid, cot, gain)


def widen(block, count):
    return jnp.broadcast_to(block[None], (count,) + block.shape)


def over_chips(blocks):
    return lax.all_to_all(blocks, CHIPS, 0, 0)


def over_trees(blocks):
    return lax.all_to_all(blocks, TREES, 0, 0)


def after(value, *others):
    return lax.optimization_barrier((value,) + others)[0]


def swap(block):
    return lax.ppermute(block, "core", SWAP)


def on_device(
    tokens,
    cotangent,
    routes,
    segments,
    parents,
    positions,
    norm_one,
    w_query,
    b_query,
    w_key,
    b_key,
    w_value,
    b_value,
    w_out,
    norm_two,
    router,
    expert_gate,
    expert_up,
    expert_down,
    shared_gate,
    shared_up,
    shared_down,
    shared_switch,
):
    core = lax.axis_index("core").astype(jnp.int32).reshape(1)
    col_start = lax.axis_index(TENSOR) * COLS
    gain_one = norm_one.astype(f32)
    gain_two = norm_two.astype(f32)

    def to_hidden(routed, shared):
        mat = jnp.concatenate(
            [jnp.transpose(routed, (0, 2, 1)).reshape(ROUTED, WIDTH), shared.T], axis=0
        )
        return (mat.astype(f32) * gain_two).astype(bf16)

    gate_mat = to_hidden(expert_gate, shared_gate)
    up_mat = to_hidden(expert_up, shared_up)
    down_mat = jnp.concatenate([expert_down.reshape(ROUTED, WIDTH), shared_down], axis=0)
    w_qkv = jnp.concatenate([w_query, w_key, w_value], axis=1)
    w_qkv = (w_qkv.astype(f32) * gain_one[:, None]).astype(bf16)
    bias = jnp.concatenate([b_query, b_key, b_value]).astype(f32)[None]
    switch_mat = jnp.concatenate(
        [router.T, shared_switch[None], jnp.zeros((1, WIDTH), bf16)], axis=0
    )
    switch_mat = (switch_mat.astype(f32) * gain_two).astype(bf16)
    switch_cols = lax.dynamic_slice_in_dim(switch_mat, col_start, COLS, 1)
    gain_two_cols = lax.dynamic_slice_in_dim(gain_two, col_start, COLS, 0)[None]
    frequency = jnp.power(THETA, -2.0 * jnp.arange(HALF, dtype=f32) / HDIM)
    angles = positions.astype(f32)[:, None] * frequency[None, :]
    cosine = jnp.cos(angles)
    sine_table = jnp.sin(angles)
    visible = (
        (segments[None, :] == 0)
        | (segments[None, :] == segments[:, None])
        | (segments[None, :] == parents[:, None])
    ) & (positions[None, :] <= positions[:, None])
    visible = visible.astype(f32)
    expert_ids = jnp.arange(8, dtype=jnp.int32)
    chosen = jnp.any(routes.T[None] == expert_ids[:, None, None], axis=1)
    chosen = (chosen | (expert_ids[:, None] >= EXPERTS)).astype(f32)

    own = over_chips(widen(tokens, NCHIP))
    shown = jnp.pad(chosen, ((0, 0), (0, 2 * HALF - ROWS % COLS)))
    shown = jnp.transpose(shown.reshape(8, 3, COLS), (1, 0, 2)).reshape(EXTRA, COLS)
    shown = jnp.pad(shown, ((0, SHOWN - EXTRA), (0, 0))).astype(bf16)
    cot_blocks = lax.all_gather(
        jnp.concatenate([cotangent, shown], axis=0), TREES + TENSOR, axis=0
    )
    cot_blocks = cot_blocks.reshape(NDP, NTP, ROWS + SHOWN, COLS)
    chosen_all = cot_blocks[:, 0, ROWS:]
    own_cot = over_chips(widen(cotangent, NCHIP))
    other = swap(own)
    blocks8 = (NCHIP, ROWS, COLS)
    keep, send, rows_one, inv_one, plain, qkv, probs, mixed = call(
        attend_body,
        [
            sds(blocks8, f32), sds(blocks8, bf16), sds((ROWS, WIDTH), bf16),
            sds((ROWS, COLS), f32), sds((ROWS, QKV), f32), sds((ROWS, QKV), bf16),
            sds((ROWS, ROWS), f32), sds((ROWS, HDIM), bf16),
        ],
        [core, own, other, w_qkv, bias, cosine, sine_table, visible, w_out],
        smem=1, flops=900_000_000, moved=8 * MIB,
    )
    arrived = over_chips((keep + swap(send).astype(f32)).astype(bf16))
    grad_plain = call(
        plain_grad_body,
        [sds((HIDDEN, ROWS), f32)],
        [core, own_cot, swap(own_cot), down_mat],
        scratch=[pltpu.VMEM((ROWS, WIDTH), bf16)],
        smem=1, flops=2 * HIDDEN * WIDTH * ROWS, moved=6 * MIB,
    )[0]
    resid_cols, wide = call(
        residual_body,
        [sds((ROWS, COLS), f32), sds(blocks8, bf16)],
        [tokens, after(arrived, grad_plain, gate_mat, up_mat)],
        moved=2 * MIB,
    )

    own = over_chips(wide)
    resid_blocks = lax.all_gather(wide[0], TREES + TENSOR, axis=0)
    resid_blocks = resid_blocks.reshape(NDP, NTP, ROWS, COLS)
    (
        keep, send, act, extra, rows_two, inv_two, inv_row, gates, logits,
    ) = call(
        experts_body,
        [
            sds(blocks8, f32), sds(blocks8, bf16), sds((HIDDEN, ROWS), bf16),
            sds((3, 8, COLS), f32), sds((ROWS, WIDTH), bf16), sds((ROWS, COLS), f32),
            sds((1, ROWS), f32), sds((8, ROWS), f32), sds((8, ROWS), f32),
        ],
        [core, own, swap(own), chosen, switch_mat, gate_mat, up_mat, grad_plain],
        smem=1, flops=8 * HIDDEN * WIDTH * ROWS, moved=20 * MIB,
    )
    extra = extra.reshape(EXTRA, COLS)
    payload = call(
        payload_body,
        [sds((NCHIP, SENT, COLS), bf16)],
        [keep, swap(send), extra, swap(extra)],
        moved=4 * MIB,
    )[0]
    arrived = over_chips(payload)
    plain_rows = plain_all(cot_blocks, down_mat)
    wide, grad_res, router_low, gain_own = call(
        second_norm_body,
        [
            sds(blocks8, bf16), sds((ROWS, COLS), f32), sds((8, ROWS), bf16),
            sds((8, COLS), f32),
        ],
        [
            core, after(arrived, plain_rows), gates, chosen, logits, inv_row, switch_cols, cotangent,
            resid_cols,
            inv_two, gain_two_cols,
        ],
        smem=1, moved=3 * MIB,
    )
    own = over_chips(wide)
    ffn = call(
        branches_body,
        [sds((NTP * ROWS, COLS), bf16)],
        [after(act, grad_res), down_mat],
        flops=2 * HIDDEN * WIDTH * ROWS, moved=8 * MIB,
    )[0]
    keep, send, extra, trees, tail = call(
        attend_back_body,
        [
            sds(blocks8, f32), sds(blocks8, bf16), sds((EXTRA, COLS), f32),
            sds((NDP, QKV_CHUNK + OUT_CHUNK, WIDTH), bf16), sds((8, WIDTH), f32),
        ],
        [
            core, own, swap(own), w_out, qkv, probs, mixed, plain, inv_one, cosine, sine_table,
            w_qkv, rows_one, router_low, rows_two, gain_two[None], gain_own,
        ],
        scratch=[pltpu.VMEM((ROWS, WIDTH), bf16)],
        smem=1, flops=2_000_000_000, moved=14 * MIB,
    )
    payload = call(
        payload_body,
        [sds((NCHIP, SENT, COLS), bf16)],
        [keep, swap(send), extra, swap(extra)],
        moved=4 * MIB,
    )[0]
    arrived = over_chips(payload)
    tree_sums = over_trees(trees)
    grads = hidden_all(
        after(resid_blocks, payload), plain_rows, chosen_all, switch_mat, gate_mat, up_mat
    )
    ffn = lax.psum_scatter(
        after(ffn, resid_blocks, payload), TENSOR, scatter_dimension=0, tiled=True
    )
    input_grad, small = call(
        first_norm_body,
        [sds((ROWS, COLS), f32), sds((8, WIDTH), f32)],
        [arrived, tokens, inv_one, grad_res],
        moved=2 * MIB,
    )
    chunk = QKV_CHUNK + OUT_CHUNK
    wide = call(
        trees_body,
        [sds((NDP, chunk + 16, WIDTH), bf16)],
        [after(tree_sums, *grads), tail, small],
        moved=6 * MIB,
    )[0]
    everything = over_trees(wide)
    output = (resid_cols + after(ffn, everything).astype(f32)).astype(bf16)
    grad_query, grad_key, grad_value, grad_out_proj, tail = call(
        last_body,
        [
            sds((WIDTH, HDIM), f32), sds((WIDTH, HDIM), f32), sds((WIDTH, HDIM), f32),
            sds((HDIM, WIDTH), f32), sds((16, WIDTH), f32),
        ],
        [everything, gain_one[None]],
        moved=7 * MIB,
    )

    gate_r, gate_s, up_r, up_s, down_r, down_s = weight_grads(
        after(grads[0], wide, input_grad), *grads[1:], resid_blocks, cot_blocks, gain_two[None]
    )

    def routed_cols(mat):
        return jnp.transpose(mat.reshape(EXPERTS, EFF, WIDTH), (0, 2, 1))

    return (
        output,
        input_grad,
        tail[8] / gain_one,
        grad_query,
        tail[EXPERTS + 1, :HDIM],
        grad_key,
        tail[EXPERTS + 1, HDIM : 2 * HDIM],
        grad_value,
        tail[EXPERTS + 1, 2 * HDIM : QKV],
        grad_out_proj,
        tail[9],
        tail[:EXPERTS].T,
        routed_cols(gate_r),
        routed_cols(up_r),
        down_r.reshape(EXPERTS, EFF, WIDTH),
        gate_s.T,
        up_s.T,
        down_s,
        tail[EXPERTS],
    )


def solution(mesh):
    fine = Mesh(mesh.devices.reshape(4, 2, 2, 4, 2), TREES + TENSOR)
    both = P(TREES, TENSOR)
    cols = P(None, TENSOR)
    placed = (
        both,
        both,
        P(TREES, None),
        P(TREES),
        P(TREES),
        P(TREES),
        P(),
        cols,
        P(TENSOR),
        cols,
        P(TENSOR),
        cols,
        P(TENSOR),
        P(TENSOR, None),
        P(),
        P(),
        P(None, None, TENSOR),
        P(None, None, TENSOR),
        P(None, TENSOR, None),
        cols,
        cols,
        P(TENSOR, None),
        P(),
    )
    return jax.shard_map(
        on_device,
        mesh=fine,
        in_specs=placed,
        out_specs=(
            both,
            both,
            P(),
            cols,
            P(TENSOR),
            cols,
            P(TENSOR),
            cols,
            P(TENSOR),
            P(TENSOR, None),
            P(),
            P(),
            P(None, None, TENSOR),
            P(None, None, TENSOR),
            P(None, TENSOR, None),
            cols,
            cols,
            P(TENSOR, None),
            P(),
        ),
        check_vma=False,
    )
```

time: 529 us -> 325 us (0.61)
  matrix products: 148 us -> 0 us
  Pallas kernels: 0 us -> 109 us
  waiting for transfers between devices: 108 us -> 35.3 us
  local copies, waits for them, and re-layouts: 125 us -> 62 us
  other arithmetic: 41.8 us -> 19.9 us
  starting transfers between devices: 58.6 us -> 41.6 us
  blocking collectives: 25.8 us -> 40.9 us
    dot_general x26 -> x0, matrix products: 148 us -> none  [the longest x8 68.9 us: dot_plain(): return jnp.dot(left_mat, right_mat, preferred_element_type=f32)]
    pallas_call x0 -> x15, Pallas kernels: none -> 109 us  [the longest x1 33.8 us: weight_grads(): pl.pallas_call(weights_body, grid=(WIDTH // step,), in_specs=[once((HIDDE...]
    all_gather x3 -> x2, waiting for transfers between devices: 40.2 us -> 0.01 us  [the longest x1 0.01 us: on_device(): lax.all_gather(jnp.concatenate([cotangent, shown], axis=0), TREES + TENSO...]
    all_to_all x10 -> x7, waiting for transfers between devices: 66.4 us -> 30.1 us  [the longest x5 30.1 us: over_chips(): return lax.all_to_all(blocks, CHIPS, 0, 0)]
    reshape x11 -> x1, local copies, waits for them, and re-layouts: 36 us -> 0.01 us  [on_device(): jnp.transpose(shown.reshape(8, 3, COLS), (1, 0, 2)).reshape(EXTRA, COLS)]
    unnamed x170 -> x132, local copies, waits for them, and re-layouts: 20.6 us -> 53.4 us
    slice x18 -> x2, local copies, waits for them, and re-layouts: 22.5 us -> 1.25 us  [the longest x1 0.63 us: on_device(): resid_blocks = lax.all_gather(wide[0], TREES + TENSOR, axis=0)]
    convert_element_type x2 -> x0, local copies, waits for them, and re-layouts: 19.5 us -> none  [the longest x1 17.1 us: on_device(): whole_resid = jnp.transpose(resid_blocks.reshape(NDP, NTP, ROWS, COLS), (...]
  transfers between devices with their start and end apart: 13 -> 19, of which waited for: 6 -> 7; matrix products, arithmetic and copies ran while one was open for 52% -> 7% of each run, Pallas kernels for 0% -> 34%
where the time goes in v2:
time: 325 us; the launch traced here: 323 us
  Pallas kernels  109 us (34%)
  local copies, waits for them, and re-layouts  62 us (19%)
  starting transfers between devices  41.6 us (13%)
  blocking collectives  40.9 us (13%)
  waiting for transfers between devices  35.3 us (11%)
  other arithmetic  19.9 us (6%)
  between operations  14.2 us (4%)
    unnamed x132, local copies, waits for them, and re-layouts  53.4 us
    all_to_all x2, blocking collectives, over_chips(): return lax.all_to_all(blocks, CHIPS, 0, 0)  40.9 us
    pallas_call x1, Pallas kernels, weight_grads(): pl.pallas_call(weights_body, grid=(WIDTH // step,), in_specs=[once((HIDDE...  33.8 us
    pallas_call x1, Pallas kernels, hidden_all(): pl.pallas_call(hidden_all_body, grid=(NDP // 2,), in_specs=[pl.BlockSpec(...  31.8 us
    all_to_all x5, waiting for transfers between devices, over_chips(): return lax.all_to_all(blocks, CHIPS, 0, 0)  30.1 us
    pallas_call x12, Pallas kernels, call(): pl.pallas_call(body, in_specs=specs, out_specs=[pl.BlockSpec(memory_space...  30 us
    all_to_all x5, starting transfers between devices, over_chips(): return lax.all_to_all(blocks, CHIPS, 0, 0)  25.2 us
    all_to_all x2, starting transfers between devices, over_trees(): return lax.all_to_all(blocks, TREES, 0, 0)  14.9 us
  transfers between devices with their start and end apart: 19, of which 7 were waited for; matrix products, arithmetic and copies ran while one was open for 7% of the time, Pallas kernels for 34%

profile of v2, /device:TPU:6, one launch (start us, length us, event | category | flops | bytes accessed | tf_op | source)
XLA Modules:
  0.0 323.2 jit_solution(16336354136947057186)
XLA Ops:
  8.1 1.6 fusion.1
  9.7 1.8 broadcast_in_dim.14
  11.5 5.9 %all-to-all-start = ((bf16[8,320,128]{2,1,0:T(8,128)(2,1)}), bf16[8,320,128]{2,1,0:T(8,128)(2,1)S(1)}, u32[]{:S(2)}, u32[]{:S(2)}) async-start(bf16[8,320,128]{2,1,0:T(8,128)(2,1)} %broadcast_in_dim.14), calls=%async_computation | async-start | bytes 1310720 | tf_op jit(solution)/shard_map/all_to_all | solution.py:509
  19.8 7.7 %all-to-all-done.own_ref = bf16[8,320,128]{2,1,0:T(8,128)(2,1)S(1)} async-done(((bf16[8,320,128]{2,1,0:T(8,128)(2,1)}), bf16[8,320,128]{2,1,0:T(8,128)(2,1)S(1)}, u32[]{:S(2)}, u32[]{:S(2)}) %all-to-all-start) | async-done | bytes 655392 | tf_op jit(solution)/shard_map/all_to_all | solution.py:509
  27.5 1.3 multiply_sine_fusion
  28.8 1.8 multiply_convert_fusion.2.w_ref
  30.7 4.2 %shard_map.366 = (f32[8,320,128]{2,1,0:T(8,128)S(1)}, bf16[8,320,128]{2,1,0:T(8,128)(2,1)}, bf16[320,2048]{1,0:T(8,128)(2,1)S(1)}, f32[320,128]{1,0:T(8,128)S(1)...) custom-call(s32[1]{0:T(128)} %bitcast.core_ref, ...), custom_call_target="tpu_custom_call" | custom-call | flops 900000000 | bytes 8388608 | tf_op jit(solution)/shard_map/pallas_call | solution.py:67
  42.0 4.3 %all-to-all-start.2 = ((bf16[8,320,128]{2,1,0:T(8,128)(2,1)}), bf16[8,320,128]{2,1,0:T(8,128)(2,1)S(1)}, u32[]{:S(2)}, u32[]{:S(2)}) async-start(bf16[8,320,128]{2,1,0:T(8,128)(2,1)} %broadcast_in_dim.15), calls=%async_computation.2 | async-start | bytes 1310720 | tf_op jit(solution)/shard_map/all_to_all | solution.py:509
  46.3 12.2 %all-to-all-done.2.own_ref = bf16[8,320,128]{2,1,0:T(8,128)(2,1)S(1)} async-done(((bf16[8,320,128]{2,1,0:T(8,128)(2,1)}), bf16[8,320,128]{2,1,0:T(8,128)(2,1)S(1)}, u32[]{:S(2)}, u32[]{:S(2)}) %all-to-all-start.2) | async-done | bytes 655392 | tf_op jit(solution)/shard_map/all_to_all | solution.py:509
  58.5 2.3 add_convert_fusion
  60.8 4.6 %all-to-all-start.1 = ((bf16[8,320,128]{2,1,0:T(8,128)(2,1)}), bf16[8,320,128]{2,1,0:T(8,128)(2,1)S(1)}, u32[]{:S(2)}, u32[]{:S(2)}) async-start(bf16[8,320,128]{2,1,0:T(8,128)(2,1)} %add_convert_fusion), calls=%async_computation.1 | async-start | bytes 1310720 | tf_op jit(solution)/shard_map/all_to_all | solution.py:509
  65.4 6.3 %multiply_convert_fusion = (bf16[880,2048]{1,0:T(8,128)(2,1)}, bf16[880,2048]{1,0:T(8,128)(2,1)}) fusion(bf16[352,2048]{1,0:T(8,128)(2,1)} %bitcast.62, bf16[528,2048]{1,0:T(8,128)(2,1)} %bitcast.59, f32[2048]{0:T(1024)S(1)} %convert_element_type.75, bf16[352,2048]{1,0:T(8,128)(2,1)} %bitcast.63, bf16[528,2048]{1,0:T(8,128)(2,1)} %bitcast.60), kind=kLoop, calls=%fused_computation | loop fusion | flops 21626880 | bytes 14426112 | tf_op jit(solution)/shard_map/convert_element_type | solution.py:558
  72.2 3.5 %shard_map.367.plain_ref = f32[880,320]{1,0:T(8,128)S(1)} custom-call(s32[1]{0:T(128)} %bitcast.core_ref, bf16[8,320,128]{2,1,0:T(8,128)(2,1)S(1)} %all-to-all-done.2.own_ref, bf16[8,320,128]{2,1,0:T(8,128)(2,1)} %collective-permute-done.2.other_ref, bf16[880,2048]{1,0:T(8,128)(2,1)S(1)} %pad_maximum_fusion.down_ref), custom_call_target="tpu_custom_call" | custom-call | flops 1153433600 | bytes 6291456 | tf_op jit(solution)/shard_map/pallas_call | solution.py:67
  75.7 1.8 copy-done
  80.9 17.9 %all_to_all.45.own_ref = bf16[8,320,128]{2,1,0:T(8,128)(2,1)S(1)} all-to-all(bf16[8,320,128]{2,1,0:T(8,128)(2,1)S(1)} %get-tuple-element.75), channel_id=1, replica_groups=mesh['z'=4,'xhi'=2,'xlo'=2,'y'=4,'core'=2] {'xlo','y'}, dimensions={0} | all-to-all | bytes 1310720 | tf_op jit(solution)/shard_map/all_to_all | solution.py:509
  101.0 2.0 copy-done.4
  103.0 2.0 copy-done.6
  105.0 1.3 copy-done.15
  106.3 8.6 %shard_map.369 = (f32[8,320,128]{2,1,0:T(8,128)S(1)}, bf16[8,320,128]{2,1,0:T(8,128)(2,1)}, bf16[880,320]{1,0:T(8,128)(2,1)S(1)}, f32[3,8,128]{2,1,0:T(8,128)S(1...) custom-call(s32[1]{0:T(128)} %bitcast.core_ref, ...), custom_call_target="tpu_custom_call" | custom-call | flops 4613734400 | bytes 20971520 | tf_op jit(solution)/shard_map/pallas_call | solution.py:67
  120.7 2.1 shard_map.370
  122.7 4.8 %all-to-all-start.4 = ((bf16[8,368,128]{2,1,0:T(8,128)(2,1)}), bf16[8,368,128]{2,1,0:T(8,128)(2,1)S(1)}, u32[]{:S(2)}, u32[]{:S(2)}) async-start(bf16[8,368,128]{2,1,0:T(8,128)(2,1)} %shard_map.370), calls=%async_computation.4 | async-start | bytes 1507328 | tf_op jit(solution)/shard_map/all_to_all | solution.py:509
  127.6 2.0 copy-done.1
  129.6 4.4 %copy-done.53 = bf16[45056,128]{1,0:T(8,128)(2,1)S(1)} copy-done((bf16[45056,128]{1,0:T(8,128)(2,1)S(1)}, bf16[45056,128]{1,0:T(8,128)(2,1)}, u32[]{:S(2)}) %copy-start.53) | copy-done | bytes 11534360
  134.0 13.7 %shard_map.371.plain_ref = f32[880,2560]{1,0:T(8,128)S(1)} custom-call(bf16[8,16,352,128]{3,2,1,0:T(8,128)(2,1)S(1)} %bitcast.58, bf16[880,2048]{1,0:T(8,128)(2,1)S(1)} %copy-done.1), custom_call_target="tpu_custom_call" | custom-call | flops 9227468800 | bytes 24117248 | tf_op jit(solution)/shard_map/pallas_call | solution.py:437
  147.7 3.5 %copy-done.54 = f32[880,2560]{1,0:T(8,128)} copy-done((f32[880,2560]{1,0:T(8,128)}, f32[880,2560]{1,0:T(8,128)S(1)}, u32[]{:S(2)}) %copy-start.54) | copy-done | bytes 9011224
  153.1 23.0 %all_to_all.46.own_ref = bf16[8,320,128]{2,1,0:T(8,128)(2,1)S(1)} all-to-all(bf16[8,320,128]{2,1,0:T(8,128)(2,1)S(1)} %get-tuple-element.87), channel_id=1, replica_groups=mesh['z'=4,'xhi'=2,'xlo'=2,'y'=4,'core'=2] {'xlo','y'}, dimensions={0} | all-to-all | bytes 1310720 | tf_op jit(solution)/shard_map/all_to_all | solution.py:509
  176.1 2.1 collective-permute-done.6.other_ref
  178.2 1.3 copy-done.18
  179.5 1.4 copy-done.20
  185.7 4.1 %shard_map.374 = (f32[8,320,128]{2,1,0:T(8,128)S(1)}, bf16[8,320,128]{2,1,0:T(8,128)(2,1)S(1)}, f32[24,128]{1,0:T(8,128)S(1)}, bf16[8,64,2048]{2,1,0:T(8,128)(2,1)S(1)}, f32[8,2048]{1,0:T(8,128)S(1)}) custom-call(s32[1]{0:T(128)} %bitcast.core_ref, bf16[8,320,128]{2,1,0:T(8,128)(2,1)S(1)} %all_to_all.46.own_ref, ...), custom_call_target="tpu_custom_call" | custom-call | flops 2000000000 | bytes 14680064 | tf_op jit(solution)/shard_map/pallas_call | solution.py:67
  189.8 1.3 copy-done.8
  192.3 1.6 collective-permute-done.8.extra_came_ref
  195.0 5.5 %all-to-all-start.7 = ((bf16[8,368,128]{2,1,0:T(8,128)(2,1)}), bf16[8,368,128]{2,1,0:T(8,128)(2,1)S(1)}, u32[]{:S(2)}, u32[]{:S(2)}) async-start(bf16[8,368,128]{2,1,0:T(8,128)(2,1)} %shard_map.375), calls=%async_computation.8 | async-start | bytes 1507328 | tf_op jit(solution)/shard_map/all_to_all | solution.py:509
  200.4 1.5 slice_bitcast_fusion.chosen_ref
  201.9 10.3 %all-to-all-done.7.arrived_ref = bf16[8,368,128]{2,1,0:T(8,128)(2,1)S(1)} async-done(((bf16[8,368,128]{2,1,0:T(8,128)(2,1)}), bf16[8,368,128]{2,1,0:T(8,128)(2,1)S(1)}, u32[]{:S(2)}, u32[]{:S(2)}) %all-to-all-start.7) | async-done | bytes 753696 | tf_op jit(solution)/shard_map/all_to_all | solution.py:509
  212.2 7.7 %all-to-all-start.6 = ((bf16[8,64,2048]{2,1,0:T(8,128)(2,1)}), bf16[8,64,2048]{2,1,0:T(8,128)(2,1)S(1)}, u32[]{:S(2)}, u32[]{:S(2)}) async-start(bf16[8,64,2048]{2,1,0:T(8,128)(2,1)} %copy-done.8), calls=%async_computation.7 | async-start | bytes 4194304 | tf_op jit(solution)/shard_map/all_to_all | solution.py:513
  219.9 2.0 copy-done.2
  221.9 2.6 shard_map.373
  224.6 2.0 copy-done.5
  226.6 2.0 copy-done.7
  230.2 31.8 %shard_map.376 = (bf16[880,2560]{1,0:T(8,128)(2,1)}, bf16[880,2560]{1,0:T(8,128)(2,1)}, bf16[880,2560]{1,0:T(8,128)(2,1)}) custom-call(bf16[8,16,320,128]{3,2,1,0:T(8,128)(2,1)} %bitcast.72, f32[880,2560]{1,0:T(8,128)} %copy-done.54, bf16[8,32,128]{2,1,0:T(8,128)(2,1)S(1)} %copy-done.46, bf16[8,2048]{1,0:T(8,128)(2,1)S(1)} %copy-done.48, ...), custom_call_target="tpu_custom_call" | custom-call | flops 18454937600 | bytes 41943040 | tf_op jit(solution)/shard_map/pallas_call | solution.py:455
  263.2 1.6 copy-done.3
  264.7 7.2 %all-to-all-start.8 = ((bf16[8,80,2048]{2,1,0:T(8,128)(2,1)}), bf16[8,80,2048]{2,1,0:T(8,128)(2,1)S(1)}, u32[]{:S(2)}, u32[]{:S(2)}) async-start(bf16[8,80,2048]{2,1,0:T(8,128)(2,1)} %copy-done.3), calls=%async_computation.9 | async-start | bytes 5242880 | tf_op jit(solution)/shard_map/all_to_all | solution.py:513
  271.9 2.3 copy-done.55
  274.2 2.3 copy-done.56
  276.6 33.8 %shard_map.380 = (f32[528,2048]{1,0:T(8,128)}, f32[352,2048]{1,0:T(8,128)}, f32[528,2048]{1,0:T(8,128)}, f32[352,2048]{1,0:T(8,128)}, f32[528,2048]{1,0:T(8,128)}, /*index=5*/f32[352,2048]{1,0:T(8,128)}) custom-call(bf16[880,2560]{1,0:T(8,128)(2,1)S(1)} %copy-done.55, bf16[880,2560]{1,0:T(8,128)(2,1)S(1)} %copy-done.56, ...), custom_call_target="tpu_custom_call" | custom-call | flops 27682406400 | bytes 58720256 | tf_op jit(solution)/shard_map/pallas_call | solution.py:480
  310.4 2.3 shard_map.379
  314.5 1.5 add_convert_fusion.1
  (173 shorter events, 36.0 us)
Async XLA Ops:
  7.2 21.6 %copy-start.59 = (bf16[2048]{0:T(1024)(128)(2,1)S(1)}, bf16[2048]{0:T(1024)(128)(2,1)}, u32[]{:S(2)}) copy-start(bf16[2048]{0:T(1024)(128)(2,1)} %param.29) | copy-start | bytes 12292
  7.2 21.6 %copy-start.63 = (bf16[128]{0:T(256)(128)(2,1)S(1)}, bf16[128]{0:T(256)(128)(2,1)}, u32[]{:S(2)}) copy-start(bf16[128]{0:T(256)(128)(2,1)} %param.35) | copy-start | bytes 772
  7.2 21.6 %copy-start.64 = (bf16[128]{0:T(256)(128)(2,1)S(1)}, bf16[128]{0:T(256)(128)(2,1)}, u32[]{:S(2)}) copy-start(bf16[128]{0:T(256)(128)(2,1)} %param.33) | copy-start | bytes 772
  7.2 21.6 %copy-start.65 = (bf16[128]{0:T(256)(128)(2,1)S(1)}, bf16[128]{0:T(256)(128)(2,1)}, u32[]{:S(2)}) copy-start(bf16[128]{0:T(256)(128)(2,1)} %param.31) | copy-start | bytes 772
  7.2 120.3 %all-gather.6.cloned.1.call-start = ((), (), s32[]{:S(2)}) async-start(), calls=%async_computation.12 | async-start | bytes 11624448 | tf_op jit(solution)/shard_map/all_gather | solution.py:590
  8.1 22.6 %copy-start.9 = (bf16[128,2048]{1,0:T(8,128)(2,1)S(1)}, bf16[128,2048]{1,0:T(8,128)(2,1)}, u32[]{:S(2)}) copy-start(bf16[128,2048]{1,0:T(8,128)(2,1)} %w_out_ref.3) | copy-start | bytes 1572868
  11.5 16.0 %all-to-all-start = ((bf16[8,320,128]{2,1,0:T(8,128)(2,1)}), bf16[8,320,128]{2,1,0:T(8,128)(2,1)S(1)}, u32[]{:S(2)}, u32[]{:S(2)}) async-start(bf16[8,320,128]{2,1,0:T(8,128)(2,1)} %broadcast_in_dim.14), calls=%async_computation | async-start | bytes 1310720 | tf_op jit(solution)/shard_map/all_to_all | solution.py:509
  27.5 3.2 %collective-permute-start = (bf16[8,320,128]{2,1,0:T(8,128)(2,1)S(1)}, bf16[8,320,128]{2,1,0:T(8,128)(2,1)}, u32[]{:S(2)}, u32[]{:S(2)}) collective-permute-start(bf16[8,320,128]{2,1,0:T(8,128)(2,1)S(1)} %all-to-all-done.own_ref), channel_id=1, source_target_pairs={{0,1},{1,0},{2,3},{3,2},{4,5},{5,4},{6,7},{7,6},{8,9},{9,8},{10,11... | collective-permute-start | bytes 1966088 | tf_op jit(solution)/shard_map/ppermute | solution.py:521
  28.8 6.2 %copy-start.10 = (f32[320,64]{1,0:T(8,128)}, f32[320,64]{1,0:T(8,128)S(1)}, u32[]{:S(2)}) copy-start(f32[320,64]{1,0:T(8,128)S(1)} %get-tuple-element.133.sin_ref) | copy-start | bytes 245764
  28.8 12.2 %copy-start.21 = (bf16[320,128]{1,0:T(8,128)(2,1)S(1)}, bf16[320,128]{1,0:T(8,128)(2,1)}, u32[]{:S(2)}) copy-start(bf16[320,128]{1,0:T(8,128)(2,1)} %cot_ref.1) | copy-start | bytes 245764
  30.7 15.6 %copy-start.61 = (bf16[2048]{0:T(1024)(128)(2,1)S(1)}, bf16[2048]{0:T(1024)(128)(2,1)}, u32[]{:S(2)}) copy-start(bf16[2048]{0:T(1024)(128)(2,1)} %param.37) | copy-start | bytes 12292
  40.6 17.9 %collective-permute-start.1 = (bf16[8,320,128]{2,1,0:T(8,128)(2,1)}, bf16[8,320,128]{2,1,0:T(8,128)(2,1)S(1)}, u32[]{:S(2)}, u32[]{:S(2)}) collective-permute-start(bf16[8,320,128]{2,1,0:T(8,128)(2,1)} %get-tuple-element.72), channel_id=1, source_target_pairs={{0,1},{1,0},{2,3},{3,2},{4,5},{5,4},{6,7},{7,6},{8,9},{9,8},{10,11... | collective-permute-start | bytes 1966088 | tf_op jit(solution)/shard_map/ppermute | solution.py:521
  42.0 16.5 %all-to-all-start.2 = ((bf16[8,320,128]{2,1,0:T(8,128)(2,1)}), bf16[8,320,128]{2,1,0:T(8,128)(2,1)S(1)}, u32[]{:S(2)}, u32[]{:S(2)}) async-start(bf16[8,320,128]{2,1,0:T(8,128)(2,1)} %broadcast_in_dim.15), calls=%async_computation.2 | async-start | bytes 1310720 | tf_op jit(solution)/shard_map/all_to_all | solution.py:509
  58.5 13.7 %collective-permute-start.2 = (bf16[8,320,128]{2,1,0:T(8,128)(2,1)S(1)}, bf16[8,320,128]{2,1,0:T(8,128)(2,1)}, u32[]{:S(2)}, u32[]{:S(2)}) collective-permute-start(bf16[8,320,128]{2,1,0:T(8,128)(2,1)S(1)} %all-to-all-done.2.own_ref), channel_id=1, source_target_pairs={{0,1},{1,0},{2,3},{3,2},{4,5},{5,4},{6,7},{7,6},{8,9},{9,8},{10,11... | collective-permute-start | bytes 1966088 | tf_op jit(solution)/shard_map/ppermute | solution.py:521
  60.8 17.9 %all-to-all-start.1 = ((bf16[8,320,128]{2,1,0:T(8,128)(2,1)}), bf16[8,320,128]{2,1,0:T(8,128)(2,1)S(1)}, u32[]{:S(2)}, u32[]{:S(2)}) async-start(bf16[8,320,128]{2,1,0:T(8,128)(2,1)} %add_convert_fusion), calls=%async_computation.1 | async-start | bytes 1310720 | tf_op jit(solution)/shard_map/all_to_all | solution.py:509
  65.4 159.2 %all-gather.4.cloned.1.call-start = ((), (), s32[]{:S(2)}) async-start(), calls=%async_computation.10 | async-start | bytes 10567680 | tf_op jit(solution)/shard_map/all_gather | solution.py:624
  65.4 6.3 %copy-start.57 = (bf16[6,88,2048]{2,1,0:T(8,128)(2,1)S(1)}, bf16[6,88,2048]{2,1,0:T(8,128)(2,1)}, u32[]{:S(2)}) copy-start(bf16[6,88,2048]{2,1,0:T(8,128)(2,1)} %param.41) | copy-start | bytes 6488068
  65.4 6.3 %copy-start.58 = (bf16[352,2048]{1,0:T(8,128)(2,1)S(1)}, bf16[352,2048]{1,0:T(8,128)(2,1)}, u32[]{:S(2)}) copy-start(bf16[352,2048]{1,0:T(8,128)(2,1)} %param.44) | copy-start | bytes 4325380
  72.2 26.7 %copy-start.62 = (bf16[2048]{0:T(1024)(128)(2,1)S(1)}, bf16[2048]{0:T(1024)(128)(2,1)}, u32[]{:S(2)}) copy-start(bf16[2048]{0:T(1024)(128)(2,1)} %param.45) | copy-start | bytes 12292
  98.9 2.1 collective-permute-start.3
  99.8 15.2 %copy-start.47 = (bf16[8,2048]{1,0:T(8,128)(2,1)}, bf16[8,2048]{1,0:T(8,128)(2,1)S(1)}, u32[]{:S(2)}) copy-start(bf16[8,2048]{1,0:T(8,128)(2,1)S(1)} %multiply_convert_fusion.3.switch_ref) | copy-start | bytes 98308
  118.1 2.6 collective-permute-start.4
  119.5 1.2 collective-permute-start.5
  122.7 28.5 %all-to-all-start.4 = ((bf16[8,368,128]{2,1,0:T(8,128)(2,1)}), bf16[8,368,128]{2,1,0:T(8,128)(2,1)S(1)}, u32[]{:S(2)}, u32[]{:S(2)}) async-start(bf16[8,368,128]{2,1,0:T(8,128)(2,1)} %shard_map.370), calls=%async_computation.4 | async-start | bytes 1507328 | tf_op jit(solution)/shard_map/all_to_all | solution.py:509
  129.6 4.4 %copy-start.53 = (bf16[45056,128]{1,0:T(8,128)(2,1)S(1)}, bf16[45056,128]{1,0:T(8,128)(2,1)}, u32[]{:S(2)}) copy-start(bf16[45056,128]{1,0:T(8,128)(2,1)} %all-gather.6.cloned.1.call-done) | copy-start | bytes 34603012
  134.0 17.2 %copy-start.27 = (f32[320,128]{1,0:T(8,128)S(1)}, f32[320,128]{1,0:T(8,128)}, u32[]{:S(2)}) copy-start(f32[320,128]{1,0:T(8,128)} %copy-done.26) | copy-start | bytes 491524
  134.0 17.2 %copy-start.49 = (bf16[8,128]{1,0:T(8,128)(2,1)S(1)}, bf16[8,128]{1,0:T(8,128)(2,1)}, u32[]{:S(2)}) copy-start(bf16[8,128]{1,0:T(8,128)(2,1)} %constant_dynamic-slice_fusion.switch_ref) | copy-start | bytes 6148
  134.0 17.2 %copy-start.51 = (f32[1,320]{1,0:T(1,128)S(1)}, f32[1,320]{1,0:T(1,128)}, u32[]{:S(2)}) copy-start(f32[1,320]{1,0:T(1,128)} %copy-done.50) | copy-start | bytes 3844
  134.0 17.3 %copy-start.52 = (f32[1,128]{1,0:T(1,128)S(1)}, f32[1,128]{1,0:T(1,128)}, u32[]{:S(2)}) copy-start(f32[1,128]{1,0:T(1,128)} %dynamic-slice_bitcast_fusion.gain_ref) | copy-start | bytes 1540
  134.0 44.2 %copy-start.11 = (f32[320,64]{1,0:T(8,128)S(1)}, f32[320,64]{1,0:T(8,128)}, u32[]{:S(2)}) copy-start(f32[320,64]{1,0:T(8,128)} %copy-done.10) | copy-start | bytes 245764
  134.0 44.2 %copy-start.13 = (f32[320,64]{1,0:T(8,128)S(1)}, f32[320,64]{1,0:T(8,128)}, u32[]{:S(2)}) copy-start(f32[320,64]{1,0:T(8,128)} %get-tuple-element.134.cos_ref) | copy-start | bytes 245764
  147.7 3.5 %copy-start.54 = (f32[880,2560]{1,0:T(8,128)}, f32[880,2560]{1,0:T(8,128)S(1)}, u32[]{:S(2)}) copy-start(f32[880,2560]{1,0:T(8,128)S(1)} %shard_map.371.plain_ref) | copy-start | bytes 27033604
  176.1 2.1 collective-permute-start.6
  191.8 2.1 collective-permute-start.7
  192.0 1.9 collective-permute-start.8
  194.9 24.9 %copy-start.25 = (bf16[880,320]{1,0:T(8,128)(2,1)S(1)}, bf16[880,320]{1,0:T(8,128)(2,1)}, u32[]{:S(2)}) copy-start(bf16[880,320]{1,0:T(8,128)(2,1)} %copy-done.24) | copy-start | bytes 1689604
  195.0 17.2 %all-to-all-start.7 = ((bf16[8,368,128]{2,1,0:T(8,128)(2,1)}), bf16[8,368,128]{2,1,0:T(8,128)(2,1)S(1)}, u32[]{:S(2)}, u32[]{:S(2)}) async-start(bf16[8,368,128]{2,1,0:T(8,128)(2,1)} %shard_map.375), calls=%async_computation.8 | async-start | bytes 1507328 | tf_op jit(solution)/shard_map/all_to_all | solution.py:509
  212.2 50.7 %all-to-all-start.6 = ((bf16[8,64,2048]{2,1,0:T(8,128)(2,1)}), bf16[8,64,2048]{2,1,0:T(8,128)(2,1)S(1)}, u32[]{:S(2)}, u32[]{:S(2)}) async-start(bf16[8,64,2048]{2,1,0:T(8,128)(2,1)} %copy-done.8), calls=%async_computation.7 | async-start | bytes 4194304 | tf_op jit(solution)/shard_map/all_to_all | solution.py:513
  219.9 94.6 %reduce-scatter.2.cloned.1.call-start = ((), (), s32[]{:S(2)}) async-start(), calls=%async_computation.11 | async-start | bytes 1392640 | tf_op jit(solution)/shard_map/reduce_scatter | solution.py:691
  230.2 31.8 %copy-start.23 = (bf16[320,128]{1,0:T(8,128)(2,1)S(1)}, bf16[320,128]{1,0:T(8,128)(2,1)}, u32[]{:S(2)}) copy-start(bf16[320,128]{1,0:T(8,128)(2,1)} %tokens_ref.3) | copy-start | bytes 245764
  230.2 31.8 %copy-start.31 = (f32[320,128]{1,0:T(8,128)S(1)}, f32[320,128]{1,0:T(8,128)}, u32[]{:S(2)}) copy-start(f32[320,128]{1,0:T(8,128)} %copy-done.29) | copy-start | bytes 491524
  230.2 31.8 %copy-start.39 = (f32[320,128]{1,0:T(8,128)S(1)}, f32[320,128]{1,0:T(8,128)}, u32[]{:S(2)}) copy-start(f32[320,128]{1,0:T(8,128)} %copy-done.38) | copy-start | bytes 491524
  230.2 32.6 %copy-start.45 = (f32[8,2048]{1,0:T(8,128)S(1)}, f32[8,2048]{1,0:T(8,128)}, u32[]{:S(2)}) copy-start(f32[8,2048]{1,0:T(8,128)} %copy-done.44) | copy-start | bytes 196612
  264.7 45.7 %all-to-all-start.8 = ((bf16[8,80,2048]{2,1,0:T(8,128)(2,1)}), bf16[8,80,2048]{2,1,0:T(8,128)(2,1)S(1)}, u32[]{:S(2)}, u32[]{:S(2)}) async-start(bf16[8,80,2048]{2,1,0:T(8,128)(2,1)} %copy-done.3), calls=%async_computation.9 | async-start | bytes 5242880 | tf_op jit(solution)/shard_map/all_to_all | solution.py:513
  271.9 2.3 copy-start.55
  274.2 2.3 copy-start.56
  276.5 38.0 %copy-start.28 = (f32[320,128]{1,0:T(8,128)S(1)}, f32[320,128]{1,0:T(8,128)}, u32[]{:S(2)}) copy-start(f32[320,128]{1,0:T(8,128)} %copy-done.26) | copy-start | bytes 491524
  310.4 5.7 %copy-start.60 = (bf16[2048]{0:T(1024)(128)(2,1)S(1)}, bf16[2048]{0:T(1024)(128)(2,1)}, u32[]{:S(2)}) copy-start(bf16[2048]{0:T(1024)(128)(2,1)} %param.29) | copy-start | bytes 12292
  (37 other events, 42.8 us)
Sparse Core Ops, SparseCore 0:
  11.0 88.5 all-gather.5
  102.7 79.2 all-gather.3
  224.7 63.6 reduce-scatter.1

commit v3 on v2

--- a/solution.py
+++ b/solution.py
@@ -61,7 +61,7 @@
     return jax.ShapeDtypeStruct(shape, dtype)
 
 
-def call(body, out_shape, args, *, scratch=(), smem=0, flops=0, moved=0, limit=24):
+def call(body, out_shape, args, *, smem=0, flops=0, moved=0, limit=60):
     specs = [pl.BlockSpec(memory_space=pltpu.SMEM)] * smem
     specs += [pl.BlockSpec(memory_space=pltpu.VMEM)] * (len(args) - smem)
     return pl.pallas_call(
@@ -69,18 +69,17 @@
         in_specs=specs,
         out_specs=[pl.BlockSpec(memory_space=pltpu.VMEM)] * len(out_shape),
         out_shape=out_shape,
-        scratch_shapes=list(scratch),
         compiler_params=pltpu.CompilerParams(vmem_limit_bytes=limit * MIB),
         cost_estimate=pl.CostEstimate(flops=flops, bytes_accessed=moved, transcendentals=0),
     )(*args)
 
 
-def lay_rows(rows_ref, core, own_ref, other_ref):
+def lay_rows(rows_ref, core, own_ref, other_ref, window=slice(0, ROWS)):
     for chip in range(NCHIP):
         own = pl.multiple_of((2 * chip + core) * COLS, COLS)
         other = pl.multiple_of((2 * chip + 1 - core) * COLS, COLS)
-        rows_ref[:, pl.ds(own, COLS)] = own_ref[chip]
-        rows_ref[:, pl.ds(other, COLS)] = other_ref[chip]
+        rows_ref[:, pl.ds(own, COLS)] = own_ref[chip, window]
+        rows_ref[:, pl.ds(other, COLS)] = other_ref[chip, window]
 
 
 def part_chips(core, part, keep_ref, send_ref):
@@ -134,10 +133,11 @@
 
 def attend_body(
     core_ref, own_ref, other_ref, w_ref, bias_ref, cos_ref, sin_ref, see_ref, w_out_ref,
-    keep_ref, send_ref, rows_ref, inv_ref, plain_ref, qkv_ref, probs_ref, mixed_ref,
+    keep_ref, send_ref, rows_ref, cot_ref, inv_ref, plain_ref, qkv_ref, probs_ref, mixed_ref,
 ):
     core = core_ref[0]
     lay_rows(rows_ref, core, own_ref, other_ref)
+    lay_rows(cot_ref, core, own_ref, other_ref, slice(ROWS, 2 * ROWS))
     rows = rows_ref[...]
     inverse = mean_square_inverse(rows)
     inv_ref[...] = jnp.broadcast_to(inverse, (ROWS, COLS))
@@ -161,19 +161,37 @@
     part_chips(core, dot_plain(mixed, w_out_ref[...]), keep_ref, send_ref)
 
 
-def residual_body(tokens_ref, arrived_ref, resid_ref, wide_ref):
+def start_body(tokens_ref, cot_ref, routes_ref, wide_ref, tall_ref, chosen_ref):
+    tokens, cot = tokens_ref[...], cot_ref[...]
+    place = lax.broadcasted_iota(jnp.int32, (8, ROWS), 0)
+    routes = routes_ref[...]
+    found = place >= EXPERTS
+    for choice in range(routes.shape[0]):
+        found = found | (place == routes[choice : choice + 1])
+    chosen = jnp.where(found, 1.0, 0.0)
+    chosen_ref[...] = chosen
+    last = jnp.concatenate([chosen[:, 2 * COLS :], jnp.zeros((8, HALF), f32)], axis=1)
+    shown = [chosen[:, :COLS], chosen[:, COLS : 2 * COLS], last, jnp.zeros((8, COLS), f32)]
+    tall_ref[:ROWS] = cot
+    tall_ref[ROWS:] = jnp.concatenate(shown, axis=0).astype(bf16)
+    for chip in range(NCHIP):
+        wide_ref[chip, :ROWS] = tokens
+        wide_ref[chip, ROWS:] = cot
+
+
+def residual_body(tokens_ref, arrived_ref, resid_ref, wide_ref, low_ref):
     total = tokens_ref[...].astype(f32)
     for chip in range(NCHIP):
         total = total + arrived_ref[chip].astype(f32)
     resid_ref[...] = total
     low = total.astype(bf16)
+    low_ref[...] = low
     for chip in range(NCHIP):
         wide_ref[chip] = low
 
 
-def plain_grad_body(core_ref, own_ref, other_ref, down_ref, out_ref, rows_ref):
-    lay_rows(rows_ref, core_ref[0], own_ref, other_ref)
-    out_ref[...] = dot_last(down_ref[...], rows_ref[...])
+def plain_grad_body(rows_ref, down_ref, out_ref):
+    out_ref[...] = dot_last(down_ref[...], rows_ref[...]).astype(bf16)
 
 
 def experts_body(
@@ -197,7 +215,7 @@
     sigma = sigmoid(gate_val)
     silu = gate_val * sigma
     act = silu * up_val
-    grad_plain = plain_ref[...]
+    grad_plain = plain_ref[...].astype(f32)
     pair = act * grad_plain
     grad_act = spread_mix * grad_plain
     grad_gate = grad_act * up_val * (sigma + silu * (1.0 - sigma))
@@ -211,10 +229,10 @@
     extra_ref[0] = sums[:, :COLS]
     extra_ref[1] = sums[:, COLS : 2 * COLS]
     extra_ref[2] = jnp.concatenate([sums[:, 2 * COLS :], jnp.zeros((8, HALF), f32)], axis=1)
+    act_ref[...] = (spread_mix * act).astype(bf16)
     part = dot_first(grad_gate.astype(bf16), gate_ref[...])
     part = part + dot_first(grad_up.astype(bf16), up_ref[...])
     part_chips(core, part, keep_ref, send_ref)
-    act_ref[...] = (spread_mix * act).astype(bf16)
 
 
 def branches_body(act_ref, down_ref, out_ref):
@@ -228,7 +246,9 @@
     high = extra.astype(bf16)
     low = (extra - high.astype(f32)).astype(bf16)
     for chip in range(NCHIP):
-        out_ref[chip, :ROWS] = (keep_ref[chip] + came_ref[chip].astype(f32)).astype(bf16)
+        out_ref[chip, :ROWS] = (
+            keep_ref[chip].astype(f32) + came_ref[chip].astype(f32)
+        ).astype(bf16)
         out_ref[chip, ROWS:] = jnp.concatenate([high, low], axis=0)
 
 
@@ -269,9 +289,9 @@
 
 
 def attend_back_body(
-    core_ref, own_ref, other_ref, w_out_ref, qkv_ref, probs_ref, mixed_ref, plain_ref, inv_ref,
-    cos_ref, sin_ref, w_ref, rows_ref, router_ref, rows_two_ref, gain_two_ref, gain_own_ref,
-    keep_ref, send_ref, extra_ref, trees_ref, tail_ref, grad_rows_ref,
+    core_ref, own_ref, other_ref, w_out_ref, qkv_ref, probs_ref, plain_ref, inv_ref, cos_ref,
+    sin_ref, w_ref, rows_ref, gain_own_ref,
+    keep_ref, send_ref, extra_ref, grad_rows_ref, scaled_ref, bias_ref,
 ):
     core = core_ref[0]
     lay_rows(grad_rows_ref, core, own_ref, other_ref)
@@ -289,9 +309,11 @@
     dv = dot_first(probs.astype(bf16), heads)
     d_low = jnp.concatenate([dq, dk, dv], axis=1).astype(bf16)
     d_wide = d_low.astype(f32)
+    inverse = inv_ref[...]
+    scaled_ref[...] = (d_wide * jnp.concatenate([inverse] * 3, axis=1)).astype(bf16)
+    bias_ref[...] = jnp.sum(d_wide, axis=0, keepdims=True)
     part = dot_last(d_low, w_ref[...])
     part_chips(core, part, keep_ref, send_ref)
-    inverse = inv_ref[...]
     rows = rows_ref[...]
     normed = rows.astype(f32) * inverse[:, :1]
     gains = jnp.sum(part * normed, axis=0, keepdims=True)
@@ -302,14 +324,18 @@
     for block in range(3):
         extra_ref[NTP + block : NTP + block + 1] = stat[:, block * COLS : (block + 1) * COLS]
     extra_ref[NTP + 3 :] = gain_own_ref[: EXTRA - NTP - 3]
-    scaled = (d_wide * jnp.concatenate([inverse] * 3, axis=1)).astype(bf16)
-    grad_w = dot_first(scaled, rows).astype(bf16)
-    grad_out = dot_first(mixed_ref[...], grad_attn).astype(bf16)
+
+
+def attend_weights_body(
+    scaled_ref, bias_ref, rows_ref, mixed_ref, grad_rows_ref, router_ref, rows_two_ref, gain_two_ref,
+    trees_ref, tail_ref,
+):
+    grad_w = dot_first(scaled_ref[...], rows_ref[...]).astype(bf16)
+    grad_out = dot_first(mixed_ref[...], grad_rows_ref[...]).astype(bf16)
     for tree in range(NDP):
         trees_ref[tree, :QKV_CHUNK] = grad_w[tree * QKV_CHUNK : (tree + 1) * QKV_CHUNK]
         trees_ref[tree, QKV_CHUNK:] = grad_out[tree * OUT_CHUNK : (tree + 1) * OUT_CHUNK]
-    bias = jnp.sum(d_wide, axis=0, keepdims=True)
-    bias = jnp.concatenate([bias, jnp.zeros((1, WIDTH - QKV), f32)], axis=1)
+    bias = jnp.concatenate([bias_ref[...], jnp.zeros((1, WIDTH - QKV), f32)], axis=1)
     router = dot_plain(router_ref[...], rows_two_ref[...]) * gain_two_ref[...]
     place = lax.broadcasted_iota(jnp.int32, (8, WIDTH), 0)
     router = jnp.where(place == EXPERTS + 1, bias, router)
@@ -347,7 +373,10 @@
         out_ref[tree, QKV_CHUNK + OUT_CHUNK :] = tail
 
 
-def last_body(all_ref, gain_ref, query_ref, key_ref, value_ref, out_ref, tail_ref):
+def last_body(
+    all_ref, gain_ref, resid_ref, ffn_ref, query_ref, key_ref, value_ref, out_ref, bias_q_ref,
+    bias_k_ref, bias_v_ref, router_ref, switch_ref, one_ref, two_ref, output_ref,
+):
     mats = jnp.concatenate([all_ref[tree, :QKV_CHUNK] for tree in range(NDP)], axis=0)
     mats = mats.astype(f32) * gain_ref[...]
     query_ref[...] = jnp.transpose(mats[:HDIM])
@@ -360,58 +389,87 @@
             tree, QKV_CHUNK:start
         ].astype(f32)
         tail = tail + all_ref[tree, start:].astype(f32)
-    tail_ref[...] = tail
+    router_ref[...] = tail[:EXPERTS]
+    switch_ref[...] = tail[EXPERTS : EXPERTS + 1]
+    bias = tail[EXPERTS + 1 : EXPERTS + 2]
+    bias_q_ref[...] = bias[:, :HDIM]
+    bias_k_ref[...] = bias[:, HDIM : 2 * HDIM]
+    bias_v_ref[...] = bias[:, 2 * HDIM : QKV]
+    one_ref[...] = tail[8:9] / gain_ref[...]
+    two_ref[...] = tail[9:10]
+    output_ref[...] = (resid_ref[...] + ffn_ref[...].astype(f32)).astype(bf16)
 
 
 def lay_trees(rows_ref, blocks_ref, trees):
     for tree in range(trees):
         for block in range(NTP):
             rows_ref[tree * ROWS : (tree + 1) * ROWS, block * COLS : (block + 1) * COLS] = (
-                blocks_ref[tree, block, :ROWS]
+                blocks_ref[tree, block]
             )
 
 
-def plain_all_body(blocks_ref, down_ref, out_ref, rows_ref):
+def plain_all_body(blocks_ref, down_ref, *refs):
+    out_ref, rows_ref = refs[-2:]
     lay_trees(rows_ref, blocks_ref, 2)
-    out_ref[...] = dot_last(down_ref[...], rows_ref[...])
+    out_ref[...] = dot_last(down_ref[...], rows_ref[...]).astype(bf16)
+
+
+BLOCK = 512
+READY = ((0, 1), (2, 3), (4,), (5, 6), (7,))
 
 
 def hidden_all_body(
     blocks_ref, plain_ref, chosen_ref, switch_ref, gate_ref, up_ref,
-    grad_gate_ref, grad_up_ref, act_ref, rows_ref,
+    grad_gate_ref, grad_up_ref, act_ref, rows_ref, sems,
 ):
-    lay_trees(rows_ref, blocks_ref, 2)
-    rows = rows_ref[...]
+
+    def copy(tree, block):
+        where = slice(tree * ROWS, (tree + 1) * ROWS), slice(block * COLS, (block + 1) * COLS)
+        return pltpu.make_async_copy(
+            blocks_ref.at[tree, block, :ROWS], rows_ref.at[where], sems.at[tree, block]
+        )
+
+    step = pl.program_id(0)
+
+    @pl.when(step == 0)
+    def _():
+        for tree in range(NDP):
+            for block in range(NTP):
+                copy(tree, block).start()
+
+    for number, trees in enumerate(READY):
+
+        @pl.when(step == number)
+        def _(trees=trees):
+            for tree in trees:
+                for block in range(NTP):
+                    copy(tree, block).wait()
+
+    rows = rows_ref[pl.ds(pl.multiple_of(step * BLOCK, BLOCK), BLOCK), :]
     inverse = to_row(mean_square_inverse(rows))
-    chosen = []
-    for tree in range(2):
-        shown = chosen_ref[tree].astype(f32)
-        chosen.append(
-            jnp.concatenate([shown[:8], shown[8:16], shown[16:24]], axis=1)[:, :ROWS]
-        )
     _, probs = routing(rows, inverse, switch_ref[...])
-    mix = probs * jnp.concatenate(chosen, axis=1)
-    gate_val = dot_last(gate_ref[...], rows) * inverse
-    up_val = dot_last(up_ref[...], rows) * inverse
-    spread_mix = per_hidden(mix)
-    sigma = sigmoid(gate_val)
-    silu = gate_val * sigma
-    act_ref[...] = (spread_mix * (silu * up_val)).astype(bf16)
-    grad_act = (spread_mix * inverse) * plain_ref[...]
-    grad_gate_ref[...] = (grad_act * up_val * (sigma + silu * (1.0 - sigma))).astype(bf16)
+    mix = probs * chosen_ref[...]
+    half = dot_last(gate_ref[...], rows) * (0.5 * inverse)
+    up_val = dot_last(up_ref[...], rows)
+    twice = jnp.tanh(half) + 1.0
+    silu = half * twice
+    weight = per_hidden(mix * inverse)
+    act_ref[...] = (weight * (silu * up_val)).astype(bf16)
+    grad_act = weight * plain_ref[...].astype(f32)
     grad_up_ref[...] = (grad_act * silu).astype(bf16)
+    slope = twice + silu * (2.0 - twice)
+    grad_gate_ref[...] = (grad_act * (up_val * (0.5 * inverse)) * slope).astype(bf16)
 
 
 def weights_body(
     grad_gate_ref, grad_up_ref, act_ref, resid_ref, cot_ref, gain_ref,
     gate_r_ref, gate_s_ref, up_r_ref, up_s_ref, down_r_ref, down_s_ref,
 ):
-    resid = jnp.concatenate(
-        [resid_ref[:, k].reshape(ALL_ROWS, COLS) for k in range(2)], axis=1
-    )
-    cot = jnp.concatenate(
-        [cot_ref[:, k, :ROWS].reshape(ALL_ROWS, COLS) for k in range(2)], axis=1
-    )
+    def columns(ref):
+        blocks = [ref[:, k].reshape(ALL_ROWS, COLS) for k in range(ref.shape[1])]
+        return jnp.concatenate(blocks, axis=1)
+
+    resid = columns(resid_ref)
     gain = gain_ref[...]
     grad = dot_plain(grad_gate_ref[...], resid) * gain
     gate_r_ref[...] = grad[:ROUTED]
@@ -419,7 +477,7 @@
     grad = dot_plain(grad_up_ref[...], resid) * gain
     up_r_ref[...] = grad[:ROUTED]
     up_s_ref[...] = grad[ROUTED:]
-    grad = dot_plain(act_ref[...], cot)
+    grad = dot_plain(act_ref[...], columns(cot_ref))
     down_r_ref[...] = grad[:ROUTED]
     down_s_ref[...] = grad[ROUTED:]
 
@@ -433,50 +491,58 @@
 PAIR_FLOPS = 2 * HIDDEN * WIDTH * ALL_ROWS
 
 
-def plain_all(blocks, down_mat):
+def plain_all(blocks, down_mat, first, held):
+    held = [] if held is None else [held]
     return pl.pallas_call(
         plain_all_body,
-        grid=(NDP // 2,),
+        grid=(NDP // 4,),
         in_specs=[
-            pl.BlockSpec((2, NTP, ROWS + SHOWN, COLS), lambda i: (i, 0, 0, 0)),
+            pl.BlockSpec((2, NTP, ROWS, COLS), lambda i: (first + i, 0, 0, 0)),
             once((HIDDEN, WIDTH)),
-        ],
-        out_specs=pl.BlockSpec((HIDDEN, PAIR), lambda i: (0, i)),
-        out_shape=sds((HIDDEN, ALL_ROWS), f32),
+        ]
+        + [pl.BlockSpec(memory_space=pltpu.HBM)] * len(held),
+        out_specs=pl.BlockSpec((HIDDEN, PAIR), lambda i: (0, first + i)),
+        out_shape=sds((HIDDEN, ALL_ROWS), bf16),
         scratch_shapes=[pltpu.VMEM((PAIR, WIDTH), bf16)],
-        compiler_params=pltpu.CompilerParams(vmem_limit_bytes=28 * MIB),
+        input_output_aliases={2: 0} if held else {},
+        compiler_params=pltpu.CompilerParams(vmem_limit_bytes=60 * MIB),
         cost_estimate=pl.CostEstimate(
-            flops=PAIR_FLOPS, bytes_accessed=23 * MIB, transcendentals=0
+            flops=PAIR_FLOPS // 2, bytes_accessed=14 * MIB, transcendentals=0
         ),
-    )(blocks, down_mat)
+    )(blocks, down_mat, *held)
 
 
 def hidden_all(blocks, plain, chosen, switch_mat, gate_mat, up_mat):
     return pl.pallas_call(
         hidden_all_body,
-        grid=(NDP // 2,),
+        grid=(ALL_ROWS // BLOCK,),
         in_specs=[
-            pl.BlockSpec((2, NTP, ROWS, COLS), lambda i: (i, 0, 0, 0)),
-            pl.BlockSpec((HIDDEN, PAIR), lambda i: (0, i)),
-            pl.BlockSpec((2, SHOWN, COLS), lambda i: (i, 0, 0)),
+            pl.BlockSpec(memory_space=pltpu.HBM),
+            pl.BlockSpec((HIDDEN, BLOCK), lambda i: (0, i)),
+            pl.BlockSpec((8, BLOCK), lambda i: (0, i)),
             once((8, WIDTH)),
             once((HIDDEN, WIDTH)),
             once((HIDDEN, WIDTH)),
         ],
-        out_specs=[pl.BlockSpec((HIDDEN, PAIR), lambda i: (0, i))] * 3,
+        out_specs=[pl.BlockSpec((HIDDEN, BLOCK), lambda i: (0, i))] * 3,
         out_shape=[sds((HIDDEN, ALL_ROWS), bf16)] * 3,
-        scratch_shapes=[pltpu.VMEM((PAIR, WIDTH), bf16)],
-        compiler_params=pltpu.CompilerParams(vmem_limit_bytes=44 * MIB),
+        scratch_shapes=[
+            pltpu.VMEM((ALL_ROWS, WIDTH), bf16),
+            pltpu.SemaphoreType.DMA((NDP, NTP)),
+        ],
+        compiler_params=pltpu.CompilerParams(vmem_limit_bytes=60 * MIB),
         cost_estimate=pl.CostEstimate(
             flops=2 * PAIR_FLOPS, bytes_accessed=40 * MIB, transcendentals=HIDDEN * ALL_ROWS
         ),
     )(blocks, plain, chosen, switch_mat, gate_mat, up_mat)
 
 
+WIDE = 2
+
+
 def weight_grads(grad_gate, grad_up, act, resid, cot, gain):
-    step = 2 * COLS
-    wide = pl.BlockSpec((NDP, 2, ROWS, COLS), lambda i: (0, i, 0, 0))
-    tall = pl.BlockSpec((NDP, 2, ROWS + SHOWN, COLS), lambda i: (0, i, 0, 0))
+    step = WIDE * COLS
+    wide = pl.BlockSpec((NDP, WIDE, ROWS, COLS), lambda i: (0, i, 0, 0))
     return pl.pallas_call(
         weights_body,
         grid=(WIDTH // step,),
@@ -485,7 +551,7 @@
             once((HIDDEN, ALL_ROWS)),
             once((HIDDEN, ALL_ROWS)),
             wide,
-            tall,
+            wide,
             pl.BlockSpec((1, step), lambda i: (0, i)),
         ],
         out_specs=[
@@ -494,7 +560,7 @@
         ]
         * 3,
         out_shape=[sds((ROUTED, WIDTH), f32), sds((SHARED, WIDTH), f32)] * 3,
-        compiler_params=pltpu.CompilerParams(vmem_limit_bytes=44 * MIB),
+        compiler_params=pltpu.CompilerParams(vmem_limit_bytes=60 * MIB),
         cost_estimate=pl.CostEstimate(
             flops=3 * PAIR_FLOPS, bytes_accessed=56 * MIB, transcendentals=0
         ),
@@ -579,71 +645,73 @@
         | (segments[None, :] == parents[:, None])
     ) & (positions[None, :] <= positions[:, None])
     visible = visible.astype(f32)
-    expert_ids = jnp.arange(8, dtype=jnp.int32)
-    chosen = jnp.any(routes.T[None] == expert_ids[:, None, None], axis=1)
-    chosen = (chosen | (expert_ids[:, None] >= EXPERTS)).astype(f32)
-
-    own = over_chips(widen(tokens, NCHIP))
-    shown = jnp.pad(chosen, ((0, 0), (0, 2 * HALF - ROWS % COLS)))
-    shown = jnp.transpose(shown.reshape(8, 3, COLS), (1, 0, 2)).reshape(EXTRA, COLS)
-    shown = jnp.pad(shown, ((0, SHOWN - EXTRA), (0, 0))).astype(bf16)
-    cot_blocks = lax.all_gather(
-        jnp.concatenate([cotangent, shown], axis=0), TREES + TENSOR, axis=0
-    )
+    wide, tall, chosen = call(
+        start_body,
+        [
+            sds((NCHIP, 2 * ROWS, COLS), bf16), sds((ROWS + SHOWN, COLS), bf16),
+            sds((8, ROWS), f32),
+        ],
+        [tokens, cotangent, routes.T],
+        moved=2 * MIB, limit=16,
+    )
+    own = over_chips(wide)
+    own = after(own, gate_mat, up_mat, down_mat, w_qkv, bias, cosine, sine_table, visible)
+    cot_blocks = lax.all_gather(tall, TREES + TENSOR, axis=0)
     cot_blocks = cot_blocks.reshape(NDP, NTP, ROWS + SHOWN, COLS)
-    chosen_all = cot_blocks[:, 0, ROWS:]
-    own_cot = over_chips(widen(cotangent, NCHIP))
+    chosen_all = cot_blocks[:, 0, ROWS : ROWS + EXTRA].reshape(NDP, 3, 8, COLS)
+    chosen_all = jnp.transpose(chosen_all, (2, 0, 1, 3)).reshape(8, NDP, 3 * COLS)
+    chosen_all = chosen_all[:, :, :ROWS].reshape(8, ALL_ROWS).astype(f32)
     other = swap(own)
     blocks8 = (NCHIP, ROWS, COLS)
-    keep, send, rows_one, inv_one, plain, qkv, probs, mixed = call(
+    keep, send, rows_one, cot_rows, inv_one, plain, qkv, probs, mixed = call(
         attend_body,
         [
-            sds(blocks8, f32), sds(blocks8, bf16), sds((ROWS, WIDTH), bf16),
-            sds((ROWS, COLS), f32), sds((ROWS, QKV), f32), sds((ROWS, QKV), bf16),
+            sds(blocks8, bf16), sds(blocks8, bf16), sds((ROWS, WIDTH), bf16),
+            sds((ROWS, WIDTH), bf16), sds((ROWS, COLS), f32), sds((ROWS, QKV), f32), sds((ROWS, QKV), bf16),
             sds((ROWS, ROWS), f32), sds((ROWS, HDIM), bf16),
         ],
         [core, own, other, w_qkv, bias, cosine, sine_table, visible, w_out],
         smem=1, flops=900_000_000, moved=8 * MIB,
     )
-    arrived = over_chips((keep + swap(send).astype(f32)).astype(bf16))
+    arrived = over_chips((keep.astype(f32) + swap(send).astype(f32)).astype(bf16))
     grad_plain = call(
         plain_grad_body,
-        [sds((HIDDEN, ROWS), f32)],
-        [core, own_cot, swap(own_cot), down_mat],
-        scratch=[pltpu.VMEM((ROWS, WIDTH), bf16)],
-        smem=1, flops=2 * HIDDEN * WIDTH * ROWS, moved=6 * MIB,
+        [sds((HIDDEN, ROWS), bf16)],
+        [cot_rows, down_mat],
+        flops=2 * HIDDEN * WIDTH * ROWS, moved=6 * MIB,
     )[0]
-    resid_cols, wide = call(
+    resid_cols, wide, low = call(
         residual_body,
-        [sds((ROWS, COLS), f32), sds(blocks8, bf16)],
-        [tokens, after(arrived, grad_plain, gate_mat, up_mat)],
+        [sds((ROWS, COLS), f32), sds(blocks8, bf16), sds((ROWS, COLS), bf16)],
+        [tokens, after(arrived, grad_plain)],
         moved=2 * MIB,
     )
 
     own = over_chips(wide)
-    resid_blocks = lax.all_gather(wide[0], TREES + TENSOR, axis=0)
+    resid_blocks = lax.all_gather(low, TREES + TENSOR, axis=0)
     resid_blocks = resid_blocks.reshape(NDP, NTP, ROWS, COLS)
     (
         keep, send, act, extra, rows_two, inv_two, inv_row, gates, logits,
     ) = call(
         experts_body,
         [
-            sds(blocks8, f32), sds(blocks8, bf16), sds((HIDDEN, ROWS), bf16),
+            sds(blocks8, bf16), sds(blocks8, bf16), sds((HIDDEN, ROWS), bf16),
             sds((3, 8, COLS), f32), sds((ROWS, WIDTH), bf16), sds((ROWS, COLS), f32),
             sds((1, ROWS), f32), sds((8, ROWS), f32), sds((8, ROWS), f32),
         ],
         [core, own, swap(own), chosen, switch_mat, gate_mat, up_mat, grad_plain],
-        smem=1, flops=8 * HIDDEN * WIDTH * ROWS, moved=20 * MIB,
+        smem=1, flops=8 * HIDDEN * WIDTH * ROWS,
+        moved=20 * MIB,
     )
     extra = extra.reshape(EXTRA, COLS)
     payload = call(
         payload_body,
         [sds((NCHIP, SENT, COLS), bf16)],
         [keep, swap(send), extra, swap(extra)],
-        moved=4 * MIB,
+        moved=4 * MIB, limit=16,
     )[0]
     arrived = over_chips(payload)
-    plain_rows = plain_all(cot_blocks, down_mat)
+    plain_half = plain_all(cot_blocks, down_mat, 0, None)
     wide, grad_res, router_low, gain_own = call(
         second_norm_body,
         [
@@ -651,7 +719,7 @@
             sds((8, COLS), f32),
         ],
         [
-            core, after(arrived, plain_rows), gates, chosen, logits, inv_row, switch_cols, cotangent,
+            core, after(arrived, plain_half), gates, chosen, logits, inv_row, switch_cols, cotangent,
             resid_cols,
             inv_two, gain_two_cols,
         ],
@@ -664,26 +732,37 @@
         [after(act, grad_res), down_mat],
         flops=2 * HIDDEN * WIDTH * ROWS, moved=8 * MIB,
     )[0]
-    keep, send, extra, trees, tail = call(
+    plain_rows = plain_all(cot_blocks, down_mat, 2, after(plain_half, grad_res))
+    own = after(own, ffn, plain_rows)
+    keep, send, extra, grad_rows, scaled, bias_sum = call(
         attend_back_body,
         [
-            sds(blocks8, f32), sds(blocks8, bf16), sds((EXTRA, COLS), f32),
-            sds((NDP, QKV_CHUNK + OUT_CHUNK, WIDTH), bf16), sds((8, WIDTH), f32),
+            sds(blocks8, bf16), sds(blocks8, bf16), sds((EXTRA, COLS), f32),
+            sds((ROWS, WIDTH), bf16), sds((ROWS, QKV), bf16), sds((1, QKV), f32),
         ],
         [
-            core, own, swap(own), w_out, qkv, probs, mixed, plain, inv_one, cosine, sine_table,
-            w_qkv, rows_one, router_low, rows_two, gain_two[None], gain_own,
-        ],
-        scratch=[pltpu.VMEM((ROWS, WIDTH), bf16)],
-        smem=1, flops=2_000_000_000, moved=14 * MIB,
+            core, own, swap(own), w_out, qkv, probs, plain, inv_one, cosine, sine_table, w_qkv,
+            rows_one, gain_own,
+        ],
+        smem=1, flops=1_000_000_000,
+        moved=10 * MIB,
     )
     payload = call(
         payload_body,
         [sds((NCHIP, SENT, COLS), bf16)],
         [keep, swap(send), extra, swap(extra)],
-        moved=4 * MIB,
+        moved=4 * MIB, limit=16,
     )[0]
     arrived = over_chips(payload)
+    trees, tail = call(
+        attend_weights_body,
+        [sds((NDP, QKV_CHUNK + OUT_CHUNK, WIDTH), bf16), sds((8, WIDTH), f32)],
+        [
+            after(scaled, payload), bias_sum, rows_one, mixed, grad_rows, router_low, rows_two,
+            gain_two[None],
+        ],
+        flops=1_000_000_000, moved=8 * MIB,
+    )
     tree_sums = over_trees(trees)
     grads = hidden_all(
         after(resid_blocks, payload), plain_rows, chosen_all, switch_mat, gate_mat, up_mat
@@ -695,25 +774,29 @@
         first_norm_body,
         [sds((ROWS, COLS), f32), sds((8, WIDTH), f32)],
         [arrived, tokens, inv_one, grad_res],
-        moved=2 * MIB,
+        moved=2 * MIB, limit=24,
     )
     chunk = QKV_CHUNK + OUT_CHUNK
     wide = call(
         trees_body,
         [sds((NDP, chunk + 16, WIDTH), bf16)],
         [after(tree_sums, *grads), tail, small],
-        moved=6 * MIB,
+        moved=6 * MIB, limit=24,
     )[0]
     everything = over_trees(wide)
-    output = (resid_cols + after(ffn, everything).astype(f32)).astype(bf16)
-    grad_query, grad_key, grad_value, grad_out_proj, tail = call(
+    (
+        grad_query, grad_key, grad_value, grad_out_proj, query_bias, key_bias, value_bias,
+        grad_router, grad_switch, gain_one_sum, gain_two_sum, output,
+    ) = call(
         last_body,
         [
             sds((WIDTH, HDIM), f32), sds((WIDTH, HDIM), f32), sds((WIDTH, HDIM), f32),
-            sds((HDIM, WIDTH), f32), sds((16, WIDTH), f32),
-        ],
-        [everything, gain_one[None]],
-        moved=7 * MIB,
+            sds((HDIM, WIDTH), f32), sds((1, HDIM), f32), sds((1, HDIM), f32),
+            sds((1, HDIM), f32), sds((EXPERTS, WIDTH), f32), sds((1, WIDTH), f32),
+            sds((1, WIDTH), f32), sds((1, WIDTH), f32), sds((ROWS, COLS), bf16),
+        ],
+        [everything, gain_one[None], resid_cols, ffn],
+        moved=7 * MIB, limit=24,
     )
 
     gate_r, gate_s, up_r, up_s, down_r, down_s = weight_grads(
@@ -726,23 +809,23 @@
     return (
         output,
         input_grad,
-        tail[8] / gain_one,
+        gain_one_sum.reshape(-1),
         grad_query,
-        tail[EXPERTS + 1, :HDIM],
+        query_bias.reshape(-1),
         grad_key,
-        tail[EXPERTS + 1, HDIM : 2 * HDIM],
+        key_bias.reshape(-1),
         grad_value,
-        tail[EXPERTS + 1, 2 * HDIM : QKV],
+        value_bias.reshape(-1),
         grad_out_proj,
-        tail[9],
-        tail[:EXPERTS].T,
+        gain_two_sum.reshape(-1),
+        grad_router.T,
         routed_cols(gate_r),
         routed_cols(up_r),
         down_r.reshape(EXPERTS, EFF, WIDTH),
         gate_s.T,
         up_s.T,
         down_s,
-        tail[EXPERTS],
+        grad_switch.reshape(-1),
     )
 
 

time: 325 us -> 288 us (0.89)
  local copies, waits for them, and re-layouts: 62 us -> 17 us
  Pallas kernels: 109 us -> 144 us
  blocking collectives: 40.9 us -> 21.5 us
  waiting for transfers between devices: 35.3 us -> 31 us
    unnamed x132 -> x84, local copies, waits for them, and re-layouts: 53.4 us -> 13.5 us
    pallas_call x12 -> x14, Pallas kernels: 30 us -> 53.9 us  [call(): pl.pallas_call(body, in_specs=specs, out_specs=[pl.BlockSpec(memory_space...]
    all_to_all x2 -> x1, blocking collectives: 40.9 us -> 21.5 us  [over_chips(): return lax.all_to_all(blocks, CHIPS, 0, 0)]
    all_to_all x5, waiting for transfers between devices: 30.1 us -> 17.7 us  [over_chips(): return lax.all_to_all(blocks, CHIPS, 0, 0)]
    ppermute x9 -> x8, waiting for transfers between devices: 5.13 us -> 13.2 us  [swap(): return lax.ppermute(block, 'core', SWAP)]
    pallas_call x2 -> x3, Pallas kernels: 45.5 us -> 53.6 us  [the longest x1 32.6 us: hidden_all(): pl.pallas_call(hidden_all_body, grid=(ALL_ROWS // BLOCK,), in_specs=[pl.B...]
    concatenate x1, other arithmetic: 0.48 us -> 3.92 us  [on_device(): jnp.concatenate([expert_down.reshape(ROUTED, WIDTH), shared_down], axis=0)]
  transfers between devices with their start and end apart: 19 -> 18, of which waited for: 7 -> 9; matrix products, arithmetic and copies ran while one was open for 7% -> 7% of each run, Pallas kernels for 34% -> 49%
where the time goes in v3:
time: 288 us; the launch traced here: 286 us
  Pallas kernels  144 us (50%)
  starting transfers between devices  42.2 us (15%)
  waiting for transfers between devices  31 us (11%)
  blocking collectives  21.5 us (7%)
  local copies, waits for them, and re-layouts  17 us (6%)
  other arithmetic  16.7 us (6%)
  between operations  14.1 us (5%)
    pallas_call x14, Pallas kernels, call(): pl.pallas_call(body, in_specs=specs, out_specs=[pl.BlockSpec(memory_space...  53.9 us
    pallas_call x1, Pallas kernels, weight_grads(): pl.pallas_call(weights_body, grid=(WIDTH // step,), in_specs=[once((HIDDE...  36.5 us
    pallas_call x1, Pallas kernels, hidden_all(): pl.pallas_call(hidden_all_body, grid=(ALL_ROWS // BLOCK,), in_specs=[pl.B...  32.6 us
    all_to_all x5, starting transfers between devices, over_chips(): return lax.all_to_all(blocks, CHIPS, 0, 0)  26.8 us
    all_to_all x1, blocking collectives, over_chips(): return lax.all_to_all(blocks, CHIPS, 0, 0)  21.5 us
    pallas_call x2, Pallas kernels, plain_all(): pl.pallas_call(plain_all_body, grid=(NDP // 4,), in_specs=[pl.BlockSpec((...  21 us
    all_to_all x5, waiting for transfers between devices, over_chips(): return lax.all_to_all(blocks, CHIPS, 0, 0)  17.7 us
    all_to_all x2, starting transfers between devices, over_trees(): return lax.all_to_all(blocks, TREES, 0, 0)  14.1 us
  transfers between devices with their start and end apart: 18, of which 9 were waited for; matrix products, arithmetic and copies ran while one was open for 7% of the time, Pallas kernels for 49%

profile of v3, /device:TPU:6, one launch (start us, length us, event | category | flops | bytes accessed | tf_op | source)
XLA Modules:
  0.0 286.5 jit_solution(5707520036822289166)
XLA Ops:
  7.2 0.9 copy-done.1
  8.1 0.9 copy-done.7
  9.7 1.3 shard_map.366
  11.7 5.9 %all-to-all-start = ((bf16[8,640,128]{2,1,0:T(8,128)(2,1)}), bf16[8,640,128]{2,1,0:T(8,128)(2,1)S(1)}, u32[]{:S(2)}, u32[]{:S(2)}) async-start(bf16[8,640,128]{2,1,0:T(8,128)(2,1)} %get-tuple-element.89), calls=%async_computation | async-start | bytes 2621440 | tf_op jit(solution)/shard_map/all_to_all | solution.py:575
  19.0 1.4 multiply_sine_fusion
  20.4 1.0 and_convert_fusion.see_ref
  21.5 3.9 %pad_maximum_fusion.down_ref = bf16[880,2048]{1,0:T(8,128)(2,1)} fusion(bf16[352,2048]{1,0:T(8,128)(2,1)} %param.44, bf16[528,2048]{1,0:T(8,128)(2,1)S(1)} %bitcast.56), kind=kLoop, calls=%fused_computation.2 | loop fusion | flops 7208960 | bytes 7208960 | tf_op jit(solution)/shard_map/concatenate | solution.py:628
  26.0 1.5 multiply_convert_fusion.2.w_ref
  27.5 4.1 %multiply_convert_fusion = (bf16[880,2048]{1,0:T(8,128)(2,1)}, bf16[880,2048]{1,0:T(8,128)(2,1)}) fusion(bf16[352,2048]{1,0:T(8,128)(2,1)S(1)} %bitcast.57, bf16[528,2048]{1,0:T(8,128)(2,1)S(1)} %bitcast.54, f32[2048]{0:T(1024)S(1)} %convert_element_type.61, bf16[352,2048]{1,0:T(8,128)(2,1)S(1)} %bitcast.58, bf16[528,2048]{1,0:T(8,128)(2,1)S(1)} %bitcast.55), kind=kLoop, calls=%fused_computation | loop fusion | flops 21626880 | bytes 14426112 | tf_op jit(solution)/shard_map/convert_element_type | solution.py:624
  31.6 3.7 %all-to-all-done.own_ref = bf16[8,640,128]{2,1,0:T(8,128)(2,1)S(1)} async-done(((bf16[8,640,128]{2,1,0:T(8,128)(2,1)}), bf16[8,640,128]{2,1,0:T(8,128)(2,1)S(1)}, u32[]{:S(2)}, u32[]{:S(2)}) %all-to-all-start) | async-done | bytes 1310752 | tf_op jit(solution)/shard_map/all_to_all | solution.py:575
  35.3 3.0 %collective-permute-done.other_ref = bf16[8,640,128]{2,1,0:T(8,128)(2,1)S(1)} collective-permute-done((bf16[8,640,128]{2,1,0:T(8,128)(2,1)S(1)}, bf16[8,640,128]{2,1,0:T(8,128)(2,1)S(1)}, u32[]{:S(2)}, u32[]{:S(2)}) %collective-permute-start) | collective-permute-done | bytes 1310752 | tf_op jit(solution)/shard_map/ppermute | solution.py:587
  38.4 1.1 copy-done.24
  39.4 7.3 %shard_map.367 = (bf16[8,320,128]{2,1,0:T(8,128)(2,1)}, bf16[8,320,128]{2,1,0:T(8,128)(2,1)}, bf16[320,2048]{1,0:T(8,128)(2,1)}, bf16[320,2048]{1,0:T(8,128)(2,1...) custom-call(s32[1]{0:T(128)} %bitcast.core_ref, ...), custom_call_target="tpu_custom_call" | custom-call | flops 900000000 | bytes 8388608 | tf_op jit(solution)/shard_map/pallas_call | solution.py:67
  46.8 2.2 collective-permute-done.1
  49.0 2.2 add_convert_fusion
  51.2 4.2 %all-to-all-start.1 = ((bf16[8,320,128]{2,1,0:T(8,128)(2,1)}), bf16[8,320,128]{2,1,0:T(8,128)(2,1)S(1)}, u32[]{:S(2)}, u32[]{:S(2)}) async-start(bf16[8,320,128]{2,1,0:T(8,128)(2,1)} %add_convert_fusion), calls=%async_computation.1 | async-start | bytes 1310720 | tf_op jit(solution)/shard_map/all_to_all | solution.py:575
  55.4 5.3 %shard_map.368.plain_ref = bf16[880,320]{1,0:T(8,128)(2,1)} custom-call(bf16[320,2048]{1,0:T(8,128)(2,1)} %get-tuple-element.93.rows_ref, bf16[880,2048]{1,0:T(8,128)(2,1)} %pad_maximum_fusion.down_ref), custom_call_target="tpu_custom_call" | custom-call | flops 1153433600 | bytes 6291456 | tf_op jit(solution)/shard_map/pallas_call | solution.py:67
  60.7 5.8 %all-to-all-done.1.arrived_ref = bf16[8,320,128]{2,1,0:T(8,128)(2,1)S(1)} async-done(((bf16[8,320,128]{2,1,0:T(8,128)(2,1)}), bf16[8,320,128]{2,1,0:T(8,128)(2,1)S(1)}, u32[]{:S(2)}, u32[]{:S(2)}) %all-to-all-start.1) | async-done | bytes 655392 | tf_op jit(solution)/shard_map/all_to_all | solution.py:575
  67.4 2.1 shard_map.369
  69.6 21.5 %all_to_all.40.own_ref = bf16[8,320,128]{2,1,0:T(8,128)(2,1)S(1)} all-to-all(bf16[8,320,128]{2,1,0:T(8,128)(2,1)} %get-tuple-element.95), channel_id=1, replica_groups=mesh['z'=4,'xhi'=2,'xlo'=2,'y'=4,'core'=2] {'xlo','y'}, dimensions={0} | all-to-all | bytes 1310720 | tf_op jit(solution)/shard_map/all_to_all | solution.py:575
  91.9 1.4 collective-permute-done.2.other_ref
  94.1 12.8 %shard_map.370 = (bf16[8,320,128]{2,1,0:T(8,128)(2,1)}, bf16[8,320,128]{2,1,0:T(8,128)(2,1)}, bf16[880,320]{1,0:T(8,128)(2,1)}, f32[3,8,128]{2,1,0:T(8,128)}, bf...) custom-call(s32[1]{0:T(128)} %bitcast.core_ref, ...), custom_call_target="tpu_custom_call" | custom-call | flops 4613734400 | bytes 20971520 | tf_op jit(solution)/shard_map/pallas_call | solution.py:67
  107.4 1.8 collective-permute-done.4.extra_came_ref
  109.3 1.1 copy-done.6
  111.0 1.0 shard_map.371
  112.1 5.2 %all-to-all-start.3 = ((bf16[8,368,128]{2,1,0:T(8,128)(2,1)}), bf16[8,368,128]{2,1,0:T(8,128)(2,1)S(1)}, u32[]{:S(2)}, u32[]{:S(2)}) async-start(bf16[8,368,128]{2,1,0:T(8,128)(2,1)} %shard_map.371), calls=%async_computation.3 | async-start | bytes 1507328 | tf_op jit(solution)/shard_map/all_to_all | solution.py:575
  117.9 1.3 constant_dynamic-slice_fusion.switch_ref
  119.2 10.5 %shard_map.372.refs_0_ = bf16[880,2560]{1,0:T(8,128)(2,1)} custom-call(bf16[8,16,352,128]{3,2,1,0:T(8,128)(2,1)} %bitcast.50, bf16[880,2048]{1,0:T(8,128)(2,1)} %pad_maximum_fusion.down_ref), custom_call_target="tpu_custom_call" | custom-call | flops 4613734400 | bytes 14680064 | tf_op jit(solution)/shard_map/pallas_call | solution.py:496
  129.7 0.9 copy-done.16
  130.5 2.5 shard_map.373
  133.0 5.7 %all-to-all-start.4 = ((bf16[8,320,128]{2,1,0:T(8,128)(2,1)}), bf16[8,320,128]{2,1,0:T(8,128)(2,1)S(1)}, u32[]{:S(2)}, u32[]{:S(2)}) async-start(bf16[8,320,128]{2,1,0:T(8,128)(2,1)} %get-tuple-element.107), calls=%async_computation.4 | async-start | bytes 1310720 | tf_op jit(solution)/shard_map/all_to_all | solution.py:575
  138.7 5.0 %shard_map.374 = bf16[5120,128]{1,0:T(8,128)(2,1)} custom-call(bf16[880,320]{1,0:T(8,128)(2,1)} %get-tuple-element.110.act_ref, bf16[880,2048]{1,0:T(8,128)(2,1)} %pad_maximum_fusion.down_ref), custom_call_target="tpu_custom_call" | custom-call | flops 1153433600 | bytes 8388608 | tf_op jit(solution)/shard_map/pallas_call | solution.py:67
  143.7 10.5 %shard_map.375.plain_ref = bf16[880,2560]{1,0:T(8,128)(2,1)} custom-call(bf16[8,16,352,128]{3,2,1,0:T(8,128)(2,1)} %bitcast.51, bf16[880,2048]{1,0:T(8,128)(2,1)} %pad_maximum_fusion.down_ref, bf16[880,2560]{1,0:T(8,128)(2,1)} %shard_map.372.refs_0_), custom_call_target="tpu_custom_call", output_to_operand_aliasing={{}: (2, {})} | custom-call | flops 4613734400 | bytes 14680064 | tf_op jit(solution)/shard_map/pallas_call | solution.py:496
  154.3 2.1 collective-permute-done.5.other_ref
  157.2 6.8 %shard_map.376 = (bf16[8,320,128]{2,1,0:T(8,128)(2,1)}, bf16[8,320,128]{2,1,0:T(8,128)(2,1)}, f32[24,128]{1,0:T(8,128)}, bf16[320,2048]{1,0:T(8,128)(2,1)}, bf16[320,384]{1,0:T(8,128)(2,1)}, /*index=5*/f32[1,384]{1,0:T(1,128)}) custom-call(s32[1]{0:T(128)} %bitcast.core_ref, bf16[8,320,128]{2,1,0:T(8,128)(2,1)} %copy-done.17, ...), custom_call_target="tpu_custom_call" | custom-call | flops 1000000000 | bytes 10485760 | tf_op jit(solution)/shard_map/pallas_call | solution.py:67
  164.6 2.7 collective-permute-done.7.extra_came_ref
  167.3 1.1 copy-done.5
  169.1 1.0 shard_map.377
  170.2 5.7 %all-to-all-start.6 = ((bf16[8,368,128]{2,1,0:T(8,128)(2,1)}), bf16[8,368,128]{2,1,0:T(8,128)(2,1)S(1)}, u32[]{:S(2)}, u32[]{:S(2)}) async-start(bf16[8,368,128]{2,1,0:T(8,128)(2,1)} %shard_map.377), calls=%async_computation.6 | async-start | bytes 1507328 | tf_op jit(solution)/shard_map/all_to_all | solution.py:575
  176.7 5.2 %shard_map.378 = (bf16[8,64,2048]{2,1,0:T(8,128)(2,1)}, f32[8,2048]{1,0:T(8,128)}) custom-call(bf16[320,384]{1,0:T(8,128)(2,1)} %get-tuple-element.123.scaled_ref, f32[1,384]{1,0:T(1,128)} %get-tuple-element.124.bias_ref, bf16[320,2048]{1,0:T(8,128)(2,1)} %get-tuple-element.117.rows_ref, bf16[320,128]{1,0:T(8,128)(2,1)} %get-tuple-element.125.mixed_ref, ...), custom_call_target="tpu_custom_call" | custom-call | flops 1000000000 | bytes 8388608 | tf_op jit(solution)/shard_map/pallas_call | solution.py:67
  181.8 8.2 %all-to-all-done.6.arrived_ref = bf16[8,368,128]{2,1,0:T(8,128)(2,1)S(1)} async-done(((bf16[8,368,128]{2,1,0:T(8,128)(2,1)}), bf16[8,368,128]{2,1,0:T(8,128)(2,1)S(1)}, u32[]{:S(2)}, u32[]{:S(2)}) %all-to-all-start.6) | async-done | bytes 753696 | tf_op jit(solution)/shard_map/all_to_all | solution.py:575
  190.0 6.9 %all-to-all-start.5 = ((bf16[8,64,2048]{2,1,0:T(8,128)(2,1)}), bf16[8,64,2048]{2,1,0:T(8,128)(2,1)S(1)}, u32[]{:S(2)}, u32[]{:S(2)}) async-start(bf16[8,64,2048]{2,1,0:T(8,128)(2,1)} %get-tuple-element.129), calls=%async_computation.5 | async-start | bytes 4194304 | tf_op jit(solution)/shard_map/all_to_all | solution.py:579
  197.7 32.6 %shard_map.379 = (bf16[880,2560]{1,0:T(8,128)(2,1)}, bf16[880,2560]{1,0:T(8,128)(2,1)}, bf16[880,2560]{1,0:T(8,128)(2,1)}) custom-call(bf16[8,16,320,128]{3,2,1,0:T(8,128)(2,1)} %bitcast.66, bf16[880,2560]{1,0:T(8,128)(2,1)} %shard_map.375.plain_ref, f32[8,2560]{1,0:T(8,128)} %reshape.166.chosen_ref, bf16[8,2048]{1,0:T(8,128)(2,1)} %multiply_convert_fusion.3.switch_ref, ...), custom_call_target="tpu_custom_call" | custom-call | flops 18454937600 | bytes 41943040 | tf_op jit(solution)/shard_map/pallas_call | solution.py:516
  231.5 1.5 copy-done
  232.9 7.2 %all-to-all-start.7 = ((bf16[8,80,2048]{2,1,0:T(8,128)(2,1)}), bf16[8,80,2048]{2,1,0:T(8,128)(2,1)S(1)}, u32[]{:S(2)}, u32[]{:S(2)}) async-start(bf16[8,80,2048]{2,1,0:T(8,128)(2,1)} %copy-done), calls=%async_computation.7 | async-start | bytes 5242880 | tf_op jit(solution)/shard_map/all_to_all | solution.py:579
  240.1 36.5 %shard_map.383 = (f32[528,2048]{1,0:T(8,128)}, f32[352,2048]{1,0:T(8,128)}, f32[528,2048]{1,0:T(8,128)}, f32[352,2048]{1,0:T(8,128)}, f32[528,2048]{1,0:T(8,128)}, /*index=5*/f32[352,2048]{1,0:T(8,128)}) custom-call(bf16[880,2560]{1,0:T(8,128)(2,1)} %get-tuple-element.151.grad_gate_ref, bf16[880,2560]{1,0:T(8,128)(2,1)} %get-tuple-element.133.grad_up_ref, ...), custom_call_target="tpu_custom_call" | custom-call | flops 27682406400 | bytes 58720256 | tf_op jit(solution)/shard_map/pallas_call | solution.py:546
  276.7 0.9 copy-done.9
  277.5 2.4 shard_map.382
  (115 shorter events, 12.8 us)
Async XLA Ops:
  7.2 112.0 %all-gather.5.cloned.1.call-start = ((), (), s32[]{:S(2)}) async-start(), calls=%async_computation.10 | async-start | bytes 11624448 | tf_op jit(solution)/shard_map/all_gather | solution.py:659
  9.7 10.7 %copy-start.32 = (s32[320]{0:T(512)S(1)}, s32[320]{0:T(512)}, u32[]{:S(2)}) copy-start(s32[320]{0:T(512)} %param.26) | copy-start | bytes 3844
  9.7 10.7 %copy-start.33 = (s32[320]{0:T(512)S(1)}, s32[320]{0:T(512)}, u32[]{:S(2)}) copy-start(s32[320]{0:T(512)} %param.28) | copy-start | bytes 3844
  9.7 10.7 %copy-start.37 = (s32[320]{0:T(512)S(1)}, s32[320]{0:T(512)}, u32[]{:S(2)}) copy-start(s32[320]{0:T(512)} %param.27) | copy-start | bytes 3844
  9.7 11.7 %copy-start.21 = (bf16[6,88,2048]{2,1,0:T(8,128)(2,1)S(1)}, bf16[6,88,2048]{2,1,0:T(8,128)(2,1)}, u32[]{:S(2)}) copy-start(bf16[6,88,2048]{2,1,0:T(8,128)(2,1)} %param.41) | copy-start | bytes 6488068
  11.7 23.7 %all-to-all-start = ((bf16[8,640,128]{2,1,0:T(8,128)(2,1)}), bf16[8,640,128]{2,1,0:T(8,128)(2,1)S(1)}, u32[]{:S(2)}, u32[]{:S(2)}) async-start(bf16[8,640,128]{2,1,0:T(8,128)(2,1)} %get-tuple-element.89), calls=%async_computation | async-start | bytes 2621440 | tf_op jit(solution)/shard_map/all_to_all | solution.py:575
  21.4 4.0 %copy-start.38 = (bf16[128]{0:T(256)(128)(2,1)S(1)}, bf16[128]{0:T(256)(128)(2,1)}, u32[]{:S(2)}) copy-start(bf16[128]{0:T(256)(128)(2,1)} %param.35) | copy-start | bytes 772
  21.4 4.0 %copy-start.39 = (bf16[128]{0:T(256)(128)(2,1)S(1)}, bf16[128]{0:T(256)(128)(2,1)}, u32[]{:S(2)}) copy-start(bf16[128]{0:T(256)(128)(2,1)} %param.33) | copy-start | bytes 772
  21.4 4.0 %copy-start.40 = (bf16[128]{0:T(256)(128)(2,1)S(1)}, bf16[128]{0:T(256)(128)(2,1)}, u32[]{:S(2)}) copy-start(bf16[128]{0:T(256)(128)(2,1)} %param.31) | copy-start | bytes 772
  21.4 4.6 %copy-start.34 = (bf16[2048]{0:T(1024)(128)(2,1)S(1)}, bf16[2048]{0:T(1024)(128)(2,1)}, u32[]{:S(2)}) copy-start(bf16[2048]{0:T(1024)(128)(2,1)} %param.37) | copy-start | bytes 12292
  21.4 4.6 %copy-start.35 = (bf16[2048]{0:T(1024)(128)(2,1)S(1)}, bf16[2048]{0:T(1024)(128)(2,1)}, u32[]{:S(2)}) copy-start(bf16[2048]{0:T(1024)(128)(2,1)} %param.29) | copy-start | bytes 12292
  21.4 4.6 %copy-start.27 = (bf16[2048,128]{1,0:T(8,128)(2,1)S(1)}, bf16[2048,128]{1,0:T(8,128)(2,1)}, u32[]{:S(2)}) copy-start(bf16[2048,128]{1,0:T(8,128)(2,1)} %param.34) | copy-start | bytes 1572868
  21.4 4.6 %copy-start.28 = (bf16[2048,128]{1,0:T(8,128)(2,1)S(1)}, bf16[2048,128]{1,0:T(8,128)(2,1)}, u32[]{:S(2)}) copy-start(bf16[2048,128]{1,0:T(8,128)(2,1)} %param.32) | copy-start | bytes 1572868
  21.4 4.6 %copy-start.29 = (bf16[2048,128]{1,0:T(8,128)(2,1)S(1)}, bf16[2048,128]{1,0:T(8,128)(2,1)}, u32[]{:S(2)}) copy-start(bf16[2048,128]{1,0:T(8,128)(2,1)} %param.30) | copy-start | bytes 1572868
  21.5 6.1 %copy-start.20 = (bf16[6,2048,88]{1,2,0:T(8,128)(2,1)S(1)}, bf16[6,2048,88]{1,2,0:T(8,128)(2,1)}, u32[]{:S(2)}) copy-start(bf16[6,2048,88]{1,2,0:T(8,128)(2,1)} %param.39) | copy-start | bytes 6488068
  21.5 6.1 %copy-start.22 = (bf16[2048,352]{0,1:T(8,128)(2,1)S(1)}, bf16[2048,352]{0,1:T(8,128)(2,1)}, u32[]{:S(2)}) copy-start(bf16[2048,352]{0,1:T(8,128)(2,1)} %param.43) | copy-start | bytes 4325380
  21.5 6.1 %copy-start.23 = (bf16[2048,352]{0,1:T(8,128)(2,1)S(1)}, bf16[2048,352]{0,1:T(8,128)(2,1)}, u32[]{:S(2)}) copy-start(bf16[2048,352]{0,1:T(8,128)(2,1)} %param.42) | copy-start | bytes 4325380
  25.4 2.1 copy-start.19
  26.0 91.3 %copy-start.30 = (f32[2048]{0:T(1024)}, f32[2048]{0:T(1024)S(1)}, u32[]{:S(2)}) copy-start(f32[2048]{0:T(1024)S(1)} %convert_element_type.61) | copy-start | bytes 24580
  35.3 3.0 %copy-start.15 = (bf16[8,640,128]{2,1,0:T(8,128)(2,1)}, bf16[8,640,128]{2,1,0:T(8,128)(2,1)S(1)}, u32[]{:S(2)}) copy-start(bf16[8,640,128]{2,1,0:T(8,128)(2,1)S(1)} %all-to-all-done.own_ref) | copy-start | bytes 3932164
  35.3 3.0 %collective-permute-start = (bf16[8,640,128]{2,1,0:T(8,128)(2,1)S(1)}, bf16[8,640,128]{2,1,0:T(8,128)(2,1)S(1)}, u32[]{:S(2)}, u32[]{:S(2)}) collective-permute-start(bf16[8,640,128]{2,1,0:T(8,128)(2,1)S(1)} %all-to-all-done.own_ref), channel_id=1, source_target_pairs={{0,1},{1,0},{2,3},{3,2},{4,5},{5,4},{6,7},{7,6},{8,9},{9,8},{10,11... | collective-permute-start | bytes 3932168 | tf_op jit(solution)/shard_map/ppermute | solution.py:587
  46.7 2.3 collective-permute-start.1
  51.2 15.4 %all-to-all-start.1 = ((bf16[8,320,128]{2,1,0:T(8,128)(2,1)}), bf16[8,320,128]{2,1,0:T(8,128)(2,1)S(1)}, u32[]{:S(2)}, u32[]{:S(2)}) async-start(bf16[8,320,128]{2,1,0:T(8,128)(2,1)} %add_convert_fusion), calls=%async_computation.1 | async-start | bytes 1310720 | tf_op jit(solution)/shard_map/all_to_all | solution.py:575
  55.4 142.3 %all-gather.7.cloned.1.call-start = ((), (), s32[]{:S(2)}) async-start(), calls=%async_computation.11 | async-start | bytes 10567680 | tf_op jit(solution)/shard_map/all_gather | solution.py:691
  55.4 35.7 %copy-start.36 = (bf16[2048]{0:T(1024)(128)(2,1)S(1)}, bf16[2048]{0:T(1024)(128)(2,1)}, u32[]{:S(2)}) copy-start(bf16[2048]{0:T(1024)(128)(2,1)} %param.45) | copy-start | bytes 12292
  55.4 35.8 %copy-start.31 = (bf16[2048,6]{0,1:T(8,128)(2,1)S(1)}, bf16[2048,6]{0,1:T(8,128)(2,1)}, u32[]{:S(2)}) copy-start(bf16[2048,6]{0,1:T(8,128)(2,1)} %param.38) | copy-start | bytes 73732
  91.0 2.2 copy-start.26
  91.1 2.2 collective-permute-start.2
  106.9 2.3 collective-permute-start.3
  107.2 2.0 collective-permute-start.4
  109.3 1.1 copy-start.6
  112.1 17.6 %all-to-all-start.3 = ((bf16[8,368,128]{2,1,0:T(8,128)(2,1)}), bf16[8,368,128]{2,1,0:T(8,128)(2,1)S(1)}, u32[]{:S(2)}, u32[]{:S(2)}) async-start(bf16[8,368,128]{2,1,0:T(8,128)(2,1)} %shard_map.371), calls=%async_computation.3 | async-start | bytes 1507328 | tf_op jit(solution)/shard_map/all_to_all | solution.py:575
  133.0 21.2 %all-to-all-start.4 = ((bf16[8,320,128]{2,1,0:T(8,128)(2,1)}), bf16[8,320,128]{2,1,0:T(8,128)(2,1)S(1)}, u32[]{:S(2)}, u32[]{:S(2)}) async-start(bf16[8,320,128]{2,1,0:T(8,128)(2,1)} %get-tuple-element.107), calls=%async_computation.4 | async-start | bytes 1310720 | tf_op jit(solution)/shard_map/all_to_all | solution.py:575
  154.2 2.1 copy-start.17
  154.2 2.1 collective-permute-start.5
  164.0 3.3 %collective-permute-start.6 = (bf16[8,320,128]{2,1,0:T(8,128)(2,1)}, bf16[8,320,128]{2,1,0:T(8,128)(2,1)S(1)}, u32[]{:S(2)}, u32[]{:S(2)}) collective-permute-start(bf16[8,320,128]{2,1,0:T(8,128)(2,1)} %get-tuple-element.121), channel_id=1, source_target_pairs={{0,1},{1,0},{2,3},{3,2},{4,5},{5,4},{6,7},{7,6},{8,9},{9,8},{10,11... | collective-permute-start | bytes 1966088 | tf_op jit(solution)/shard_map/ppermute | solution.py:587
  164.2 3.1 %collective-permute-start.7 = (f32[24,128]{1,0:T(8,128)}, f32[24,128]{1,0:T(8,128)S(1)}, u32[]{:S(2)}, u32[]{:S(2)}) collective-permute-start(f32[24,128]{1,0:T(8,128)} %get-tuple-element.122.extra_ref), channel_id=1, source_target_pairs={{0,1},{1,0},{2,3},{3,2},{4,5},{5,4},{6,7},{7,6},{8,9},{9,8},{10,11... | collective-permute-start | bytes 36872 | tf_op jit(solution)/shard_map/ppermute | solution.py:587
  167.3 1.1 copy-start.5
  170.2 19.9 %all-to-all-start.6 = ((bf16[8,368,128]{2,1,0:T(8,128)(2,1)}), bf16[8,368,128]{2,1,0:T(8,128)(2,1)S(1)}, u32[]{:S(2)}, u32[]{:S(2)}) async-start(bf16[8,368,128]{2,1,0:T(8,128)(2,1)} %shard_map.377), calls=%async_computation.6 | async-start | bytes 1507328 | tf_op jit(solution)/shard_map/all_to_all | solution.py:575
  190.0 41.1 %all-to-all-start.5 = ((bf16[8,64,2048]{2,1,0:T(8,128)(2,1)}), bf16[8,64,2048]{2,1,0:T(8,128)(2,1)S(1)}, u32[]{:S(2)}, u32[]{:S(2)}) async-start(bf16[8,64,2048]{2,1,0:T(8,128)(2,1)} %get-tuple-element.129), calls=%async_computation.5 | async-start | bytes 4194304 | tf_op jit(solution)/shard_map/all_to_all | solution.py:579
  196.9 79.7 %reduce-scatter.2.cloned.1.call-start = ((), (), s32[]{:S(2)}) async-start(), calls=%async_computation.9 | async-start | bytes 1392640 | tf_op jit(solution)/shard_map/reduce_scatter | solution.py:770
  197.7 32.6 %copy-start.2 = (bf16[320,128]{1,0:T(8,128)(2,1)S(1)}, bf16[320,128]{1,0:T(8,128)(2,1)}, u32[]{:S(2)}) copy-start(bf16[320,128]{1,0:T(8,128)(2,1)} %tokens_ref.5) | copy-start | bytes 245764
  197.7 32.6 %copy-start.4 = (f32[320,128]{1,0:T(8,128)S(1)}, f32[320,128]{1,0:T(8,128)}, u32[]{:S(2)}) copy-start(f32[320,128]{1,0:T(8,128)} %get-tuple-element.116.inv_ref) | copy-start | bytes 491524
  197.7 32.6 %copy-start.8 = (f32[320,128]{1,0:T(8,128)S(1)}, f32[320,128]{1,0:T(8,128)}, u32[]{:S(2)}) copy-start(f32[320,128]{1,0:T(8,128)} %get-tuple-element.109.grad_res_ref) | copy-start | bytes 491524
  197.7 33.4 %copy-start.10 = (f32[8,2048]{1,0:T(8,128)S(1)}, f32[8,2048]{1,0:T(8,128)}, u32[]{:S(2)}) copy-start(f32[8,2048]{1,0:T(8,128)} %get-tuple-element.136.tail_ref) | copy-start | bytes 196612
  231.5 1.5 copy-start
  232.9 43.7 %all-to-all-start.7 = ((bf16[8,80,2048]{2,1,0:T(8,128)(2,1)}), bf16[8,80,2048]{2,1,0:T(8,128)(2,1)S(1)}, u32[]{:S(2)}, u32[]{:S(2)}) async-start(bf16[8,80,2048]{2,1,0:T(8,128)(2,1)} %copy-done), calls=%async_computation.7 | async-start | bytes 5242880 | tf_op jit(solution)/shard_map/all_to_all | solution.py:579
  240.1 36.5 %copy-start.3 = (f32[320,128]{1,0:T(8,128)S(1)}, f32[320,128]{1,0:T(8,128)}, u32[]{:S(2)}) copy-start(f32[320,128]{1,0:T(8,128)} %get-tuple-element.105.resid_ref) | copy-start | bytes 491524
  (12 other events, 9.8 us)
Sparse Core Ops, SparseCore 0:
  11.8 89.4 all-gather.4
  104.4 88.3 all-gather.6
  200.1 65.2 reduce-scatter.1

commit v4 on v3

--- a/solution.py
+++ b/solution.py
@@ -31,6 +31,7 @@
 ALL_ROWS = NDP * ROWS
 EXTRA = 24
 SHOWN = 32
+TALL = 2 * ROWS + SHOWN
 SENT = ROWS + 2 * EXTRA
 QKV = 3 * HDIM
 OUT_CHUNK = HDIM // NDP
@@ -133,11 +134,10 @@
 
 def attend_body(
     core_ref, own_ref, other_ref, w_ref, bias_ref, cos_ref, sin_ref, see_ref, w_out_ref,
-    keep_ref, send_ref, rows_ref, cot_ref, inv_ref, plain_ref, qkv_ref, probs_ref, mixed_ref,
+    keep_ref, send_ref, rows_ref, inv_ref, plain_ref, qkv_ref, probs_ref, mixed_ref,
 ):
     core = core_ref[0]
     lay_rows(rows_ref, core, own_ref, other_ref)
-    lay_rows(cot_ref, core, own_ref, other_ref, slice(ROWS, 2 * ROWS))
     rows = rows_ref[...]
     inverse = mean_square_inverse(rows)
     inv_ref[...] = jnp.broadcast_to(inverse, (ROWS, COLS))
@@ -161,8 +161,8 @@
     part_chips(core, dot_plain(mixed, w_out_ref[...]), keep_ref, send_ref)
 
 
-def start_body(tokens_ref, cot_ref, routes_ref, wide_ref, tall_ref, chosen_ref):
-    tokens, cot = tokens_ref[...], cot_ref[...]
+def start_body(tokens_ref, routes_ref, wide_ref, shown_ref, chosen_ref):
+    tokens = tokens_ref[...]
     place = lax.broadcasted_iota(jnp.int32, (8, ROWS), 0)
     routes = routes_ref[...]
     found = place >= EXPERTS
@@ -172,20 +172,22 @@
     chosen_ref[...] = chosen
     last = jnp.concatenate([chosen[:, 2 * COLS :], jnp.zeros((8, HALF), f32)], axis=1)
     shown = [chosen[:, :COLS], chosen[:, COLS : 2 * COLS], last, jnp.zeros((8, COLS), f32)]
-    tall_ref[:ROWS] = cot
-    tall_ref[ROWS:] = jnp.concatenate(shown, axis=0).astype(bf16)
+    shown_ref[...] = jnp.concatenate(shown, axis=0).astype(bf16)
     for chip in range(NCHIP):
-        wide_ref[chip, :ROWS] = tokens
-        wide_ref[chip, ROWS:] = cot
-
-
-def residual_body(tokens_ref, arrived_ref, resid_ref, wide_ref, low_ref):
+        wide_ref[chip] = tokens
+
+
+def residual_body(
+    tokens_ref, arrived_ref, cot_ref, shown_ref, resid_ref, wide_ref, tall_ref
+):
     total = tokens_ref[...].astype(f32)
     for chip in range(NCHIP):
         total = total + arrived_ref[chip].astype(f32)
     resid_ref[...] = total
     low = total.astype(bf16)
-    low_ref[...] = low
+    tall_ref[:ROWS] = low
+    tall_ref[ROWS : 2 * ROWS] = cot_ref[...]
+    tall_ref[2 * ROWS :] = shown_ref[...]
     for chip in range(NCHIP):
         wide_ref[chip] = low
 
@@ -290,8 +292,8 @@
 
 def attend_back_body(
     core_ref, own_ref, other_ref, w_out_ref, qkv_ref, probs_ref, plain_ref, inv_ref, cos_ref,
-    sin_ref, w_ref, rows_ref, gain_own_ref,
-    keep_ref, send_ref, extra_ref, grad_rows_ref, scaled_ref, bias_ref,
+    sin_ref, w_ref, rows_ref, gain_own_ref, mixed_ref, router_ref, rows_two_ref, gain_two_ref,
+    keep_ref, send_ref, extra_ref, trees_ref, tail_ref, grad_rows_ref,
 ):
     core = core_ref[0]
     lay_rows(grad_rows_ref, core, own_ref, other_ref)
@@ -310,8 +312,7 @@
     d_low = jnp.concatenate([dq, dk, dv], axis=1).astype(bf16)
     d_wide = d_low.astype(f32)
     inverse = inv_ref[...]
-    scaled_ref[...] = (d_wide * jnp.concatenate([inverse] * 3, axis=1)).astype(bf16)
-    bias_ref[...] = jnp.sum(d_wide, axis=0, keepdims=True)
+    scaled = (d_wide * jnp.concatenate([inverse] * 3, axis=1)).astype(bf16)
     part = dot_last(d_low, w_ref[...])
     part_chips(core, part, keep_ref, send_ref)
     rows = rows_ref[...]
@@ -325,17 +326,13 @@
         extra_ref[NTP + block : NTP + block + 1] = stat[:, block * COLS : (block + 1) * COLS]
     extra_ref[NTP + 3 :] = gain_own_ref[: EXTRA - NTP - 3]
 
-
-def attend_weights_body(
-    scaled_ref, bias_ref, rows_ref, mixed_ref, grad_rows_ref, router_ref, rows_two_ref, gain_two_ref,
-    trees_ref, tail_ref,
-):
-    grad_w = dot_first(scaled_ref[...], rows_ref[...]).astype(bf16)
-    grad_out = dot_first(mixed_ref[...], grad_rows_ref[...]).astype(bf16)
+    grad_w = dot_first(scaled, rows).astype(bf16)
+    grad_out = dot_first(mixed_ref[...], grad_attn).astype(bf16)
     for tree in range(NDP):
         trees_ref[tree, :QKV_CHUNK] = grad_w[tree * QKV_CHUNK : (tree + 1) * QKV_CHUNK]
         trees_ref[tree, QKV_CHUNK:] = grad_out[tree * OUT_CHUNK : (tree + 1) * OUT_CHUNK]
-    bias = jnp.concatenate([bias_ref[...], jnp.zeros((1, WIDTH - QKV), f32)], axis=1)
+    bias = jnp.sum(d_wide, axis=0, keepdims=True)
+    bias = jnp.concatenate([bias, jnp.zeros((1, WIDTH - QKV), f32)], axis=1)
     router = dot_plain(router_ref[...], rows_two_ref[...]) * gain_two_ref[...]
     place = lax.broadcasted_iota(jnp.int32, (8, WIDTH), 0)
     router = jnp.where(place == EXPERTS + 1, bias, router)
@@ -408,8 +405,7 @@
             )
 
 
-def plain_all_body(blocks_ref, down_ref, *refs):
-    out_ref, rows_ref = refs[-2:]
+def plain_all_body(blocks_ref, down_ref, out_ref, rows_ref):
     lay_trees(rows_ref, blocks_ref, 2)
     out_ref[...] = dot_last(down_ref[...], rows_ref[...]).astype(bf16)
 
@@ -423,29 +419,36 @@
     grad_gate_ref, grad_up_ref, act_ref, rows_ref, sems,
 ):
 
-    def copy(tree, block):
-        where = slice(tree * ROWS, (tree + 1) * ROWS), slice(block * COLS, (block + 1) * COLS)
-        return pltpu.make_async_copy(
-            blocks_ref.at[tree, block, :ROWS], rows_ref.at[where], sems.at[tree, block]
-        )
+    def copies(trees):
+        for tree in trees:
+            for block in range(NTP):
+                where = (
+                    slice(tree * ROWS, (tree + 1) * ROWS),
+                    slice(block * COLS, (block + 1) * COLS),
+                )
+                yield pltpu.make_async_copy(
+                    blocks_ref.at[tree, block, :ROWS], rows_ref.at[where], sems.at[tree, block]
+                )
 
     step = pl.program_id(0)
 
     @pl.when(step == 0)
     def _():
-        for tree in range(NDP):
-            for block in range(NTP):
-                copy(tree, block).start()
+        for copy in copies(READY[0]):
+            copy.start()
 
     for number, trees in enumerate(READY):
 
         @pl.when(step == number)
-        def _(trees=trees):
-            for tree in trees:
-                for block in range(NTP):
-                    copy(tree, block).wait()
-
-    rows = rows_ref[pl.ds(pl.multiple_of(step * BLOCK, BLOCK), BLOCK), :]
+        def _(number=number, trees=trees):
+            for copy in copies(trees):
+                copy.wait()
+            if number == 0:
+                for copy in copies(range(len(READY[0]), NDP)):
+                    copy.start()
+
+    spot = pl.ds(pl.multiple_of(step * BLOCK, BLOCK), BLOCK)
+    rows = rows_ref[spot, :]
     inverse = to_row(mean_square_inverse(rows))
     _, probs = routing(rows, inverse, switch_ref[...])
     mix = probs * chosen_ref[...]
@@ -491,25 +494,22 @@
 PAIR_FLOPS = 2 * HIDDEN * WIDTH * ALL_ROWS
 
 
-def plain_all(blocks, down_mat, first, held):
-    held = [] if held is None else [held]
+def plain_all(blocks, down_mat):
     return pl.pallas_call(
         plain_all_body,
-        grid=(NDP // 4,),
+        grid=(NDP // 2,),
         in_specs=[
-            pl.BlockSpec((2, NTP, ROWS, COLS), lambda i: (first + i, 0, 0, 0)),
+            pl.BlockSpec((2, NTP, ROWS, COLS), lambda i: (i, 0, 1, 0)),
             once((HIDDEN, WIDTH)),
-        ]
-        + [pl.BlockSpec(memory_space=pltpu.HBM)] * len(held),
-        out_specs=pl.BlockSpec((HIDDEN, PAIR), lambda i: (0, first + i)),
+        ],
+        out_specs=pl.BlockSpec((HIDDEN, PAIR), lambda i: (0, i)),
         out_shape=sds((HIDDEN, ALL_ROWS), bf16),
         scratch_shapes=[pltpu.VMEM((PAIR, WIDTH), bf16)],
-        input_output_aliases={2: 0} if held else {},
         compiler_params=pltpu.CompilerParams(vmem_limit_bytes=60 * MIB),
         cost_estimate=pl.CostEstimate(
-            flops=PAIR_FLOPS // 2, bytes_accessed=14 * MIB, transcendentals=0
+            flops=PAIR_FLOPS, bytes_accessed=20 * MIB, transcendentals=0
         ),
-    )(blocks, down_mat, *held)
+    )(blocks, down_mat)
 
 
 def hidden_all(blocks, plain, chosen, switch_mat, gate_mat, up_mat):
@@ -532,7 +532,7 @@
         ],
         compiler_params=pltpu.CompilerParams(vmem_limit_bytes=60 * MIB),
         cost_estimate=pl.CostEstimate(
-            flops=2 * PAIR_FLOPS, bytes_accessed=40 * MIB, transcendentals=HIDDEN * ALL_ROWS
+            flops=3 * PAIR_FLOPS, bytes_accessed=40 * MIB, transcendentals=HIDDEN * ALL_ROWS
         ),
     )(blocks, plain, chosen, switch_mat, gate_mat, up_mat)
 
@@ -540,9 +540,10 @@
 WIDE = 2
 
 
-def weight_grads(grad_gate, grad_up, act, resid, cot, gain):
+def weight_grads(grad_gate, grad_up, act, blocks, gain):
     step = WIDE * COLS
-    wide = pl.BlockSpec((NDP, WIDE, ROWS, COLS), lambda i: (0, i, 0, 0))
+    resid = pl.BlockSpec((NDP, WIDE, ROWS, COLS), lambda i: (0, i, 0, 0))
+    cot = pl.BlockSpec((NDP, WIDE, ROWS, COLS), lambda i: (0, i, 1, 0))
     return pl.pallas_call(
         weights_body,
         grid=(WIDTH // step,),
@@ -550,8 +551,8 @@
             once((HIDDEN, ALL_ROWS)),
             once((HIDDEN, ALL_ROWS)),
             once((HIDDEN, ALL_ROWS)),
-            wide,
-            wide,
+            resid,
+            cot,
             pl.BlockSpec((1, step), lambda i: (0, i)),
         ],
         out_specs=[
@@ -564,7 +565,7 @@
         cost_estimate=pl.CostEstimate(
             flops=3 * PAIR_FLOPS, bytes_accessed=56 * MIB, transcendentals=0
         ),
-    )(grad_gate, grad_up, act, resid, cot, gain)
+    )(grad_gate, grad_up, act, blocks, blocks, gain)
 
 
 def widen(block, count):
@@ -645,29 +646,24 @@
         | (segments[None, :] == parents[:, None])
     ) & (positions[None, :] <= positions[:, None])
     visible = visible.astype(f32)
-    wide, tall, chosen = call(
+    wide, shown, chosen = call(
         start_body,
         [
-            sds((NCHIP, 2 * ROWS, COLS), bf16), sds((ROWS + SHOWN, COLS), bf16),
-            sds((8, ROWS), f32),
-        ],
-        [tokens, cotangent, routes.T],
-        moved=2 * MIB, limit=16,
-    )
+            sds((NCHIP, ROWS, COLS), bf16), sds((SHOWN, COLS), bf16), sds((8, ROWS), f32),
+        ],
+        [tokens, routes.T],
+        moved=2 * MIB,
+    )
+    cot_rows = lax.all_gather(cotangent, TENSOR, axis=1, tiled=True)
     own = over_chips(wide)
-    own = after(own, gate_mat, up_mat, down_mat, w_qkv, bias, cosine, sine_table, visible)
-    cot_blocks = lax.all_gather(tall, TREES + TENSOR, axis=0)
-    cot_blocks = cot_blocks.reshape(NDP, NTP, ROWS + SHOWN, COLS)
-    chosen_all = cot_blocks[:, 0, ROWS : ROWS + EXTRA].reshape(NDP, 3, 8, COLS)
-    chosen_all = jnp.transpose(chosen_all, (2, 0, 1, 3)).reshape(8, NDP, 3 * COLS)
-    chosen_all = chosen_all[:, :, :ROWS].reshape(8, ALL_ROWS).astype(f32)
+    own = after(own, down_mat, w_qkv, bias, cosine, sine_table, visible)
     other = swap(own)
     blocks8 = (NCHIP, ROWS, COLS)
-    keep, send, rows_one, cot_rows, inv_one, plain, qkv, probs, mixed = call(
+    keep, send, rows_one, inv_one, plain, qkv, probs, mixed = call(
         attend_body,
         [
             sds(blocks8, bf16), sds(blocks8, bf16), sds((ROWS, WIDTH), bf16),
-            sds((ROWS, WIDTH), bf16), sds((ROWS, COLS), f32), sds((ROWS, QKV), f32), sds((ROWS, QKV), bf16),
+            sds((ROWS, COLS), f32), sds((ROWS, QKV), f32), sds((ROWS, QKV), bf16),
             sds((ROWS, ROWS), f32), sds((ROWS, HDIM), bf16),
         ],
         [core, own, other, w_qkv, bias, cosine, sine_table, visible, w_out],
@@ -680,16 +676,18 @@
         [cot_rows, down_mat],
         flops=2 * HIDDEN * WIDTH * ROWS, moved=6 * MIB,
     )[0]
-    resid_cols, wide, low = call(
+    resid_cols, wide, tall = call(
         residual_body,
-        [sds((ROWS, COLS), f32), sds(blocks8, bf16), sds((ROWS, COLS), bf16)],
-        [tokens, after(arrived, grad_plain)],
+        [sds((ROWS, COLS), f32), sds(blocks8, bf16), sds((TALL, COLS), bf16)],
+        [tokens, after(arrived, grad_plain), cotangent, shown],
         moved=2 * MIB,
     )
 
-    own = over_chips(wide)
-    resid_blocks = lax.all_gather(low, TREES + TENSOR, axis=0)
-    resid_blocks = resid_blocks.reshape(NDP, NTP, ROWS, COLS)
+    own = after(over_chips(wide), gate_mat, up_mat)
+    blocks = lax.all_gather(tall, TREES + TENSOR, axis=0).reshape(NDP, NTP, TALL, COLS)
+    chosen_all = blocks[:, 0, 2 * ROWS : 2 * ROWS + EXTRA].reshape(NDP, 3, 8, COLS)
+    chosen_all = jnp.transpose(chosen_all, (2, 0, 1, 3)).reshape(8, NDP, 3 * COLS)
+    chosen_all = chosen_all[:, :, :ROWS].reshape(8, ALL_ROWS).astype(f32)
     (
         keep, send, act, extra, rows_two, inv_two, inv_row, gates, logits,
     ) = call(
@@ -711,7 +709,6 @@
         moved=4 * MIB, limit=16,
     )[0]
     arrived = over_chips(payload)
-    plain_half = plain_all(cot_blocks, down_mat, 0, None)
     wide, grad_res, router_low, gain_own = call(
         second_norm_body,
         [
@@ -719,7 +716,7 @@
             sds((8, COLS), f32),
         ],
         [
-            core, after(arrived, plain_half), gates, chosen, logits, inv_row, switch_cols, cotangent,
+            core, arrived, gates, chosen, logits, inv_row, switch_cols, cotangent,
             resid_cols,
             inv_two, gain_two_cols,
         ],
@@ -732,20 +729,24 @@
         [after(act, grad_res), down_mat],
         flops=2 * HIDDEN * WIDTH * ROWS, moved=8 * MIB,
     )[0]
-    plain_rows = plain_all(cot_blocks, down_mat, 2, after(plain_half, grad_res))
-    own = after(own, ffn, plain_rows)
-    keep, send, extra, grad_rows, scaled, bias_sum = call(
+    own = after(own, ffn)
+    keep, send, extra, trees, tail = pl.pallas_call(
         attend_back_body,
-        [
+        in_specs=[pl.BlockSpec(memory_space=pltpu.SMEM)]
+        + [pl.BlockSpec(memory_space=pltpu.VMEM)] * 16,
+        out_specs=[pl.BlockSpec(memory_space=pltpu.VMEM)] * 5,
+        out_shape=[
             sds(blocks8, bf16), sds(blocks8, bf16), sds((EXTRA, COLS), f32),
-            sds((ROWS, WIDTH), bf16), sds((ROWS, QKV), bf16), sds((1, QKV), f32),
-        ],
-        [
-            core, own, swap(own), w_out, qkv, probs, plain, inv_one, cosine, sine_table, w_qkv,
-            rows_one, gain_own,
-        ],
-        smem=1, flops=1_000_000_000,
-        moved=10 * MIB,
+            sds((NDP, QKV_CHUNK + OUT_CHUNK, WIDTH), bf16), sds((8, WIDTH), f32),
+        ],
+        scratch_shapes=[pltpu.VMEM((ROWS, WIDTH), bf16)],
+        compiler_params=pltpu.CompilerParams(vmem_limit_bytes=60 * MIB),
+        cost_estimate=pl.CostEstimate(
+            flops=2_000_000_000, bytes_accessed=14 * MIB, transcendentals=0
+        ),
+    )(
+        core, own, swap(own), w_out, qkv, probs, plain, inv_one, cosine, sine_table, w_qkv,
+        rows_one, gain_own, mixed, router_low, rows_two, gain_two[None],
     )
     payload = call(
         payload_body,
@@ -754,26 +755,19 @@
         moved=4 * MIB, limit=16,
     )[0]
     arrived = over_chips(payload)
-    trees, tail = call(
-        attend_weights_body,
-        [sds((NDP, QKV_CHUNK + OUT_CHUNK, WIDTH), bf16), sds((8, WIDTH), f32)],
-        [
-            after(scaled, payload), bias_sum, rows_one, mixed, grad_rows, router_low, rows_two,
-            gain_two[None],
-        ],
-        flops=1_000_000_000, moved=8 * MIB,
-    )
+    plain_rows = plain_all(after(blocks, payload), down_mat)
+    trees = after(trees, plain_rows)
     tree_sums = over_trees(trees)
     grads = hidden_all(
-        after(resid_blocks, payload), plain_rows, chosen_all, switch_mat, gate_mat, up_mat
+        blocks, after(plain_rows, trees), chosen_all, switch_mat, gate_mat, up_mat
     )
     ffn = lax.psum_scatter(
-        after(ffn, resid_blocks, payload), TENSOR, scatter_dimension=0, tiled=True
+        after(ffn, blocks, payload), TENSOR, scatter_dimension=0, tiled=True
     )
     input_grad, small = call(
         first_norm_body,
         [sds((ROWS, COLS), f32), sds((8, WIDTH), f32)],
-        [arrived, tokens, inv_one, grad_res],
+        [after(arrived, plain_rows), tokens, inv_one, grad_res],
         moved=2 * MIB, limit=24,
     )
     chunk = QKV_CHUNK + OUT_CHUNK
@@ -800,7 +794,7 @@
     )
 
     gate_r, gate_s, up_r, up_s, down_r, down_s = weight_grads(
-        after(grads[0], wide, input_grad), *grads[1:], resid_blocks, cot_blocks, gain_two[None]
+        after(grads[0], wide, input_grad), *grads[1:], blocks, gain_two[None]
     )
 
     def routed_cols(mat):

time: 288 us -> 277 us (0.962)
  blocking collectives: 21.5 us -> 0 us
  waiting for transfers between devices: 31 us -> 44.3 us
  Pallas kernels: 144 us -> 137 us
  starting transfers between devices: 42.2 us -> 46.9 us
  local copies, waits for them, and re-layouts: 17 us -> 13.7 us
  other arithmetic: 16.7 us -> 19.7 us
    all_to_all x1 -> x0, blocking collectives: 21.5 us -> none  [over_chips(): return lax.all_to_all(blocks, CHIPS, 0, 0)]
    pallas_call x14 -> x12, Pallas kernels: 53.9 us -> 41.8 us  [call(): pl.pallas_call(body, in_specs=specs, out_specs=[pl.BlockSpec(memory_space...]
    all_to_all x5 -> x6, waiting for transfers between devices: 17.7 us -> 27.7 us  [over_chips(): return lax.all_to_all(blocks, CHIPS, 0, 0)]
    pallas_call x2, Pallas kernels: 21 us -> 26.2 us  [the longest x1 17 us: plain_all(): pl.pallas_call(plain_all_body, grid=(NDP // 2,), in_specs=[pl.BlockSpec((...]
    all_to_all x5 -> x6, starting transfers between devices: 26.8 us -> 31.2 us  [over_chips(): return lax.all_to_all(blocks, CHIPS, 0, 0)]
    all_gather x2, waiting for transfers between devices: 0.01 us -> 3.48 us  [the longest x1 1.87 us: on_device(): cot_rows = lax.all_gather(cotangent, TENSOR, axis=1, tiled=True)]
    unnamed x84 -> x58, local copies, waits for them, and re-layouts: 13.5 us -> 10.3 us
  transfers between devices with their start and end apart: 18 -> 19, of which waited for: 9 -> 12; matrix products, arithmetic and copies ran while one was open for 7% -> 8% of each run, Pallas kernels for 49% -> 48%
where the time goes in v4:
time: 277 us; the launch traced here: 276 us
  Pallas kernels  137 us (49%)
  starting transfers between devices  46.9 us (17%)
  waiting for transfers between devices  44.3 us (16%)
  other arithmetic  19.7 us (7%)
  between operations  14 us (5%)
  local copies, waits for them, and re-layouts  13.7 us (5%)
    pallas_call x12, Pallas kernels, call(): pl.pallas_call(body, in_specs=specs, out_specs=[pl.BlockSpec(memory_space...  41.8 us
    pallas_call x1, Pallas kernels, weight_grads(): pl.pallas_call(weights_body, grid=(WIDTH // step,), in_specs=[once((HIDDE...  36.4 us
    pallas_call x1, Pallas kernels, hidden_all(): pl.pallas_call(hidden_all_body, grid=(ALL_ROWS // BLOCK,), in_specs=[pl.B...  32.7 us
    all_to_all x6, starting transfers between devices, over_chips(): return lax.all_to_all(blocks, CHIPS, 0, 0)  31.2 us
    all_to_all x6, waiting for transfers between devices, over_chips(): return lax.all_to_all(blocks, CHIPS, 0, 0)  27.7 us
    pallas_call x1, Pallas kernels, plain_all(): pl.pallas_call(plain_all_body, grid=(NDP // 2,), in_specs=[pl.BlockSpec((...  17 us
    all_to_all x2, starting transfers between devices, over_trees(): return lax.all_to_all(blocks, TREES, 0, 0)  14.3 us
    ppermute x8, waiting for transfers between devices, swap(): return lax.ppermute(block, 'core', SWAP)  12.4 us
  transfers between devices with their start and end apart: 19, of which 12 were waited for; matrix products, arithmetic and copies ran while one was open for 8% of the time, Pallas kernels for 48%

profile of v4, /device:TPU:6, one launch (start us, length us, event | category | flops | bytes accessed | tf_op | source)
XLA Modules:
  0.0 275.8 jit_solution(14740186570463397020)
XLA Ops:
  8.0 1.8 shard_map.366
  9.8 5.9 %all-to-all-start = ((bf16[8,320,128]{2,1,0:T(8,128)(2,1)}), bf16[8,320,128]{2,1,0:T(8,128)(2,1)S(1)}, u32[]{:S(2)}, u32[]{:S(2)}) async-start(bf16[8,320,128]{2,1,0:T(8,128)(2,1)} %get-tuple-element.86), calls=%async_computation | async-start | bytes 1310720 | tf_op jit(solution)/shard_map/all_to_all | solution.py:576
  17.9 1.8 and_convert_fusion.see_ref
  19.7 2.8 %multiply_convert_fusion.2.w_ref = bf16[2048,384]{1,0:T(8,128)(2,1)} fusion(bf16[2048,128]{1,0:T(8,128)(2,1)} %param.34, bf16[2048,128]{1,0:T(8,128)(2,1)} %param.32, bf16[2048,128]{1,0:T(8,128)(2,1)} %param.30, f32[2048]{0:T(1024)S(1)} %convert_element_type.61), kind=kLoop, calls=%fused_computation.3 | loop fusion | flops 6291456 | bytes 3153920 | tf_op jit(solution)/shard_map/convert_element_type | solution.py:631
  22.5 1.4 multiply_sine_fusion
  24.5 2.2 pad_maximum_fusion.down_ref
  26.7 2.1 collective-permute-done.other_ref
  28.9 0.8 copy-done.20
  29.7 5.9 %shard_map.367 = (bf16[8,320,128]{2,1,0:T(8,128)(2,1)}, bf16[8,320,128]{2,1,0:T(8,128)(2,1)}, bf16[320,2048]{1,0:T(8,128)(2,1)}, f32[320,128]{1,0:T(8,128)}, f32...) custom-call(s32[1]{0:T(128)} %bitcast.core_ref, ...), custom_call_target="tpu_custom_call" | custom-call | flops 900000000 | bytes 8388608 | tf_op jit(solution)/shard_map/pallas_call | solution.py:68
  35.9 2.1 collective-permute-done.1
  38.0 2.2 add_convert_fusion
  40.2 5.7 %all-to-all-start.1 = ((bf16[8,320,128]{2,1,0:T(8,128)(2,1)}), bf16[8,320,128]{2,1,0:T(8,128)(2,1)S(1)}, u32[]{:S(2)}, u32[]{:S(2)}) async-start(bf16[8,320,128]{2,1,0:T(8,128)(2,1)} %add_convert_fusion), calls=%async_computation.1 | async-start | bytes 1310720 | tf_op jit(solution)/shard_map/all_to_all | solution.py:576
  45.9 1.9 all-gather.4.cloned.1.call-done.rows_ref
  47.8 5.3 %shard_map.368.plain_ref = bf16[880,320]{1,0:T(8,128)(2,1)} custom-call(bf16[320,2048]{1,0:T(8,128)(2,1)} %all-gather.4.cloned.1.call-done.rows_ref, bf16[880,2048]{1,0:T(8,128)(2,1)} %pad_maximum_fusion.down_ref), custom_call_target="tpu_custom_call" | custom-call | flops 1153433600 | bytes 6291456 | tf_op jit(solution)/shard_map/pallas_call | solution.py:68
  53.1 3.1 %all-to-all-done.1.arrived_ref = bf16[8,320,128]{2,1,0:T(8,128)(2,1)S(1)} async-done(((bf16[8,320,128]{2,1,0:T(8,128)(2,1)}), bf16[8,320,128]{2,1,0:T(8,128)(2,1)S(1)}, u32[]{:S(2)}, u32[]{:S(2)}) %all-to-all-start.1) | async-done | bytes 655392 | tf_op jit(solution)/shard_map/all_to_all | solution.py:576
  56.2 0.8 copy-done.13
  57.0 2.2 shard_map.369
  59.2 4.2 %all-to-all-start.2 = ((bf16[8,320,128]{2,1,0:T(8,128)(2,1)}), bf16[8,320,128]{2,1,0:T(8,128)(2,1)S(1)}, u32[]{:S(2)}, u32[]{:S(2)}) async-start(bf16[8,320,128]{2,1,0:T(8,128)(2,1)} %get-tuple-element.92), calls=%async_computation.2 | async-start | bytes 1310720 | tf_op jit(solution)/shard_map/all_to_all | solution.py:576
  63.5 5.8 %multiply_convert_fusion = (bf16[880,2048]{1,0:T(8,128)(2,1)}, bf16[880,2048]{1,0:T(8,128)(2,1)}) fusion(bf16[352,2048]{1,0:T(8,128)(2,1)} %bitcast.51, bf16[528,2048]{1,0:T(8,128)(2,1)S(1)} %bitcast.48, f32[2048]{0:T(1024)S(1)} %convert_element_type.70, bf16[352,2048]{1,0:T(8,128)(2,1)} %bitcast.52, bf16[528,2048]{1,0:T(8,128)(2,1)} %bitcast.49), kind=kLoop, calls=%fused_computation | loop fusion | flops 21626880 | bytes 14426112 | tf_op jit(solution)/shard_map/convert_element_type | solution.py:625
  69.3 4.4 %all-to-all-done.2.own_ref = bf16[8,320,128]{2,1,0:T(8,128)(2,1)S(1)} async-done(((bf16[8,320,128]{2,1,0:T(8,128)(2,1)}), bf16[8,320,128]{2,1,0:T(8,128)(2,1)S(1)}, u32[]{:S(2)}, u32[]{:S(2)}) %all-to-all-start.2) | async-done | bytes 655392 | tf_op jit(solution)/shard_map/all_to_all | solution.py:576
  74.5 1.3 collective-permute-done.2.other_ref
  76.6 12.5 %shard_map.370 = (bf16[8,320,128]{2,1,0:T(8,128)(2,1)}, bf16[8,320,128]{2,1,0:T(8,128)(2,1)}, bf16[880,320]{1,0:T(8,128)(2,1)}, f32[3,8,128]{2,1,0:T(8,128)}, bf...) custom-call(s32[1]{0:T(128)} %bitcast.core_ref, ...), custom_call_target="tpu_custom_call" | custom-call | flops 4613734400 | bytes 20971520 | tf_op jit(solution)/shard_map/pallas_call | solution.py:68
  89.6 1.8 collective-permute-done.4.extra_came_ref
  91.4 1.1 copy-done.4
  93.2 1.0 shard_map.371
  94.3 4.3 %all-to-all-start.3 = ((bf16[8,368,128]{2,1,0:T(8,128)(2,1)}), bf16[8,368,128]{2,1,0:T(8,128)(2,1)S(1)}, u32[]{:S(2)}, u32[]{:S(2)}) async-start(bf16[8,368,128]{2,1,0:T(8,128)(2,1)} %shard_map.371), calls=%async_computation.3 | async-start | bytes 1507328 | tf_op jit(solution)/shard_map/all_to_all | solution.py:576
  99.1 1.2 constant_dynamic-slice_fusion.switch_ref
  100.4 11.3 %all-to-all-done.3.arrived_ref = bf16[8,368,128]{2,1,0:T(8,128)(2,1)S(1)} async-done(((bf16[8,368,128]{2,1,0:T(8,128)(2,1)}), bf16[8,368,128]{2,1,0:T(8,128)(2,1)S(1)}, u32[]{:S(2)}, u32[]{:S(2)}) %all-to-all-start.3) | async-done | bytes 753696 | tf_op jit(solution)/shard_map/all_to_all | solution.py:576
  111.7 0.9 copy-done.11
  112.5 2.5 shard_map.372
  115.0 4.7 %all-to-all-start.4 = ((bf16[8,320,128]{2,1,0:T(8,128)(2,1)}), bf16[8,320,128]{2,1,0:T(8,128)(2,1)S(1)}, u32[]{:S(2)}, u32[]{:S(2)}) async-start(bf16[8,320,128]{2,1,0:T(8,128)(2,1)} %get-tuple-element.103), calls=%async_computation.4 | async-start | bytes 1310720 | tf_op jit(solution)/shard_map/all_to_all | solution.py:576
  119.7 6.0 %shard_map.373 = bf16[5120,128]{1,0:T(8,128)(2,1)} custom-call(bf16[880,320]{1,0:T(8,128)(2,1)} %get-tuple-element.106.act_ref, bf16[880,2048]{1,0:T(8,128)(2,1)} %pad_maximum_fusion.down_ref), custom_call_target="tpu_custom_call" | custom-call | flops 1153433600 | bytes 8388608 | tf_op jit(solution)/shard_map/pallas_call | solution.py:68
  125.7 8.9 %all-to-all-done.4.own_ref = bf16[8,320,128]{2,1,0:T(8,128)(2,1)S(1)} async-done(((bf16[8,320,128]{2,1,0:T(8,128)(2,1)}), bf16[8,320,128]{2,1,0:T(8,128)(2,1)S(1)}, u32[]{:S(2)}, u32[]{:S(2)}) %all-to-all-start.4) | async-done | bytes 655392 | tf_op jit(solution)/shard_map/all_to_all | solution.py:576
  134.7 2.3 collective-permute-done.5.other_ref
  137.8 9.2 %shard_map.374 = (bf16[8,320,128]{2,1,0:T(8,128)(2,1)}, bf16[8,320,128]{2,1,0:T(8,128)(2,1)}, f32[24,128]{1,0:T(8,128)}, bf16[8,64,2048]{2,1,0:T(8,128)(2,1)}, f32[8,2048]{1,0:T(8,128)}) custom-call(s32[1]{0:T(128)} %bitcast.core_ref, bf16[8,320,128]{2,1,0:T(8,128)(2,1)} %copy-done.12, bf16[8,320,128]{2,1,0:T(8,128)(2,1)} %copy-done.18, ...), custom_call_target="tpu_custom_call" | custom-call | flops 2000000000 | bytes 14680064 | tf_op jit(solution)/shard_map/pallas_call | solution.py:733
  147.6 2.7 collective-permute-done.7.extra_came_ref
  150.3 1.1 copy-done.3
  152.2 1.0 shard_map.375
  153.2 6.4 %all-to-all-start.6 = ((bf16[8,368,128]{2,1,0:T(8,128)(2,1)}), bf16[8,368,128]{2,1,0:T(8,128)(2,1)S(1)}, u32[]{:S(2)}, u32[]{:S(2)}) async-start(bf16[8,368,128]{2,1,0:T(8,128)(2,1)} %shard_map.375), calls=%async_computation.6 | async-start | bytes 1507328 | tf_op jit(solution)/shard_map/all_to_all | solution.py:576
  159.6 1.6 all-gather.6.cloned.1.call-done
  162.8 17.0 %shard_map.376.plain_ref = bf16[880,2560]{1,0:T(8,128)(2,1)} custom-call(bf16[8,16,672,128]{3,2,1,0:T(8,128)(2,1)} %bitcast.62, bf16[880,2048]{1,0:T(8,128)(2,1)} %pad_maximum_fusion.down_ref), custom_call_target="tpu_custom_call" | custom-call | flops 9227468800 | bytes 20971520 | tf_op jit(solution)/shard_map/pallas_call | solution.py:498
  179.8 7.1 %all-to-all-start.5 = ((bf16[8,64,2048]{2,1,0:T(8,128)(2,1)}), bf16[8,64,2048]{2,1,0:T(8,128)(2,1)S(1)}, u32[]{:S(2)}, u32[]{:S(2)}) async-start(bf16[8,64,2048]{2,1,0:T(8,128)(2,1)} %get-tuple-element.123), calls=%async_computation.5 | async-start | bytes 4194304 | tf_op jit(solution)/shard_map/all_to_all | solution.py:580
  186.9 32.7 %shard_map.377 = (bf16[880,2560]{1,0:T(8,128)(2,1)}, bf16[880,2560]{1,0:T(8,128)(2,1)}, bf16[880,2560]{1,0:T(8,128)(2,1)}) custom-call(bf16[8,16,672,128]{3,2,1,0:T(8,128)(2,1)} %bitcast.63, bf16[880,2560]{1,0:T(8,128)(2,1)} %shard_map.376.plain_ref, f32[8,2560]{1,0:T(8,128)} %reshape.162.chosen_ref, bf16[8,2048]{1,0:T(8,128)(2,1)} %multiply_convert_fusion.3.switch_ref, ...), custom_call_target="tpu_custom_call" | custom-call | flops 27682406400 | bytes 41943040 | tf_op jit(solution)/shard_map/pallas_call | solution.py:516
  220.8 1.5 copy-done
  222.3 7.2 %all-to-all-start.7 = ((bf16[8,80,2048]{2,1,0:T(8,128)(2,1)}), bf16[8,80,2048]{2,1,0:T(8,128)(2,1)S(1)}, u32[]{:S(2)}, u32[]{:S(2)}) async-start(bf16[8,80,2048]{2,1,0:T(8,128)(2,1)} %copy-done), calls=%async_computation.7 | async-start | bytes 5242880 | tf_op jit(solution)/shard_map/all_to_all | solution.py:580
  229.5 36.4 %shard_map.381 = (f32[528,2048]{1,0:T(8,128)}, f32[352,2048]{1,0:T(8,128)}, f32[528,2048]{1,0:T(8,128)}, f32[352,2048]{1,0:T(8,128)}, f32[528,2048]{1,0:T(8,128)}, /*index=5*/f32[352,2048]{1,0:T(8,128)}) custom-call(bf16[880,2560]{1,0:T(8,128)(2,1)} %get-tuple-element.145.grad_gate_ref, bf16[880,2560]{1,0:T(8,128)(2,1)} %get-tuple-element.126.grad_up_ref, ...), custom_call_target="tpu_custom_call" | custom-call | flops 27682406400 | bytes 58720256 | tf_op jit(solution)/shard_map/pallas_call | solution.py:547
  266.0 0.9 copy-done.7
  266.9 2.4 shard_map.380
  (88 shorter events, 12.1 us)
Async XLA Ops:
  7.2 16.7 %copy-start.25 = (bf16[128]{0:T(256)(128)(2,1)S(1)}, bf16[128]{0:T(256)(128)(2,1)}, u32[]{:S(2)}) copy-start(bf16[128]{0:T(256)(128)(2,1)} %param.35) | copy-start | bytes 772
  7.2 16.7 %copy-start.26 = (bf16[128]{0:T(256)(128)(2,1)S(1)}, bf16[128]{0:T(256)(128)(2,1)}, u32[]{:S(2)}) copy-start(bf16[128]{0:T(256)(128)(2,1)} %param.33) | copy-start | bytes 772
  7.2 16.7 %copy-start.27 = (bf16[128]{0:T(256)(128)(2,1)S(1)}, bf16[128]{0:T(256)(128)(2,1)}, u32[]{:S(2)}) copy-start(bf16[128]{0:T(256)(128)(2,1)} %param.31) | copy-start | bytes 772
  7.2 17.2 %copy-start.16 = (bf16[6,88,2048]{2,1,0:T(8,128)(2,1)S(1)}, bf16[6,88,2048]{2,1,0:T(8,128)(2,1)}, u32[]{:S(2)}) copy-start(bf16[6,88,2048]{2,1,0:T(8,128)(2,1)} %param.41) | copy-start | bytes 6488068
  7.2 40.5 %all-gather.4.cloned.1.call-start = ((), (), s32[]{:S(2)}) async-start(), calls=%async_computation.9 | async-start | bytes 1392640 | tf_op jit(solution)/shard_map/all_gather | solution.py:657
  9.8 16.9 %all-to-all-start = ((bf16[8,320,128]{2,1,0:T(8,128)(2,1)}), bf16[8,320,128]{2,1,0:T(8,128)(2,1)S(1)}, u32[]{:S(2)}, u32[]{:S(2)}) async-start(bf16[8,320,128]{2,1,0:T(8,128)(2,1)} %get-tuple-element.86), calls=%async_computation | async-start | bytes 1310720 | tf_op jit(solution)/shard_map/all_to_all | solution.py:576
  15.7 8.7 %copy-start.17 = (bf16[352,2048]{1,0:T(8,128)(2,1)S(1)}, bf16[352,2048]{1,0:T(8,128)(2,1)}, u32[]{:S(2)}) copy-start(bf16[352,2048]{1,0:T(8,128)(2,1)} %param.44) | copy-start | bytes 4325380
  26.7 2.2 copy-start.14
  26.7 2.2 collective-permute-start
  28.9 0.8 copy-start.20
  35.6 2.4 collective-permute-start.1
  40.2 16.0 %all-to-all-start.1 = ((bf16[8,320,128]{2,1,0:T(8,128)(2,1)}), bf16[8,320,128]{2,1,0:T(8,128)(2,1)S(1)}, u32[]{:S(2)}, u32[]{:S(2)}) async-start(bf16[8,320,128]{2,1,0:T(8,128)(2,1)} %add_convert_fusion), calls=%async_computation.1 | async-start | bytes 1310720 | tf_op jit(solution)/shard_map/all_to_all | solution.py:576
  45.8 13.4 %copy-start.23 = (bf16[2048]{0:T(1024)(128)(2,1)S(1)}, bf16[2048]{0:T(1024)(128)(2,1)}, u32[]{:S(2)}) copy-start(bf16[2048]{0:T(1024)(128)(2,1)} %param.37) | copy-start | bytes 12292
  45.8 17.6 %copy-start.15 = (bf16[6,2048,88]{1,2,0:T(8,128)(2,1)S(1)}, bf16[6,2048,88]{1,2,0:T(8,128)(2,1)}, u32[]{:S(2)}) copy-start(bf16[6,2048,88]{1,2,0:T(8,128)(2,1)} %param.40) | copy-start | bytes 6488068
  45.9 115.4 %all-gather.6.cloned.1.call-start = ((), (), s32[]{:S(2)}) async-start(), calls=%async_computation.11 | async-start | bytes 22192128 | tf_op jit(solution)/shard_map/all_gather | solution.py:687
  56.2 0.8 copy-start.13
  59.2 39.3 %copy-start.21 = (f32[2048]{0:T(1024)}, f32[2048]{0:T(1024)S(1)}, u32[]{:S(2)}) copy-start(f32[2048]{0:T(1024)S(1)} %convert_element_type.70) | copy-start | bytes 24580
  59.2 14.4 %all-to-all-start.2 = ((bf16[8,320,128]{2,1,0:T(8,128)(2,1)}), bf16[8,320,128]{2,1,0:T(8,128)(2,1)S(1)}, u32[]{:S(2)}, u32[]{:S(2)}) async-start(bf16[8,320,128]{2,1,0:T(8,128)(2,1)} %get-tuple-element.92), calls=%async_computation.2 | async-start | bytes 1310720 | tf_op jit(solution)/shard_map/all_to_all | solution.py:576
  63.5 10.2 %copy-start.24 = (bf16[2048]{0:T(1024)(128)(2,1)S(1)}, bf16[2048]{0:T(1024)(128)(2,1)}, u32[]{:S(2)}) copy-start(bf16[2048]{0:T(1024)(128)(2,1)} %param.45) | copy-start | bytes 12292
  63.5 10.3 %copy-start.22 = (bf16[2048,6]{0,1:T(8,128)(2,1)S(1)}, bf16[2048,6]{0,1:T(8,128)(2,1)}, u32[]{:S(2)}) copy-start(bf16[2048,6]{0,1:T(8,128)(2,1)} %param.38) | copy-start | bytes 73732
  73.7 2.1 copy-start.19
  73.7 2.1 collective-permute-start.2
  75.8 0.8 copy-start.28
  89.1 2.3 collective-permute-start.3
  89.3 2.2 collective-permute-start.4
  91.4 1.1 copy-start.4
  92.5 0.7 copy-start.10
  94.3 17.4 %all-to-all-start.3 = ((bf16[8,368,128]{2,1,0:T(8,128)(2,1)}), bf16[8,368,128]{2,1,0:T(8,128)(2,1)S(1)}, u32[]{:S(2)}, u32[]{:S(2)}) async-start(bf16[8,368,128]{2,1,0:T(8,128)(2,1)} %shard_map.371), calls=%async_computation.3 | async-start | bytes 1507328 | tf_op jit(solution)/shard_map/all_to_all | solution.py:576
  111.6 0.9 copy-start.11
  115.0 19.6 %all-to-all-start.4 = ((bf16[8,320,128]{2,1,0:T(8,128)(2,1)}), bf16[8,320,128]{2,1,0:T(8,128)(2,1)S(1)}, u32[]{:S(2)}, u32[]{:S(2)}) async-start(bf16[8,320,128]{2,1,0:T(8,128)(2,1)} %get-tuple-element.103), calls=%async_computation.4 | async-start | bytes 1310720 | tf_op jit(solution)/shard_map/all_to_all | solution.py:576
  134.7 2.3 copy-start.12
  134.7 2.3 collective-permute-start.5
  137.0 0.8 copy-start.18
  147.1 3.3 %collective-permute-start.6 = (bf16[8,320,128]{2,1,0:T(8,128)(2,1)}, bf16[8,320,128]{2,1,0:T(8,128)(2,1)S(1)}, u32[]{:S(2)}, u32[]{:S(2)}) collective-permute-start(bf16[8,320,128]{2,1,0:T(8,128)(2,1)} %get-tuple-element.120), channel_id=1, source_target_pairs={{0,1},{1,0},{2,3},{3,2},{4,5},{5,4},{6,7},{7,6},{8,9},{9,8},{10,11... | collective-permute-start | bytes 1966088 | tf_op jit(solution)/shard_map/ppermute | solution.py:588
  147.1 3.2 %collective-permute-start.7 = (f32[24,128]{1,0:T(8,128)}, f32[24,128]{1,0:T(8,128)S(1)}, u32[]{:S(2)}, u32[]{:S(2)}) collective-permute-start(f32[24,128]{1,0:T(8,128)} %get-tuple-element.121.extra_ref), channel_id=1, source_target_pairs={{0,1},{1,0},{2,3},{3,2},{4,5},{5,4},{6,7},{7,6},{8,9},{9,8},{10,11... | collective-permute-start | bytes 36872 | tf_op jit(solution)/shard_map/ppermute | solution.py:588
  150.3 1.1 copy-start.3
  151.4 0.7 copy-start.9
  153.2 26.6 %all-to-all-start.6 = ((bf16[8,368,128]{2,1,0:T(8,128)(2,1)}), bf16[8,368,128]{2,1,0:T(8,128)(2,1)S(1)}, u32[]{:S(2)}, u32[]{:S(2)}) async-start(bf16[8,368,128]{2,1,0:T(8,128)(2,1)} %shard_map.375), calls=%async_computation.6 | async-start | bytes 1507328 | tf_op jit(solution)/shard_map/all_to_all | solution.py:576
  159.6 106.4 %reduce-scatter.2.cloned.1.call-start = ((), (), s32[]{:S(2)}) async-start(), calls=%async_computation.10 | async-start | bytes 1392640 | tf_op jit(solution)/shard_map/reduce_scatter | solution.py:764
  179.8 40.7 %all-to-all-start.5 = ((bf16[8,64,2048]{2,1,0:T(8,128)(2,1)}), bf16[8,64,2048]{2,1,0:T(8,128)(2,1)S(1)}, u32[]{:S(2)}, u32[]{:S(2)}) async-start(bf16[8,64,2048]{2,1,0:T(8,128)(2,1)} %get-tuple-element.123), calls=%async_computation.5 | async-start | bytes 4194304 | tf_op jit(solution)/shard_map/all_to_all | solution.py:580
  186.9 32.8 %copy-start.1 = (bf16[320,128]{1,0:T(8,128)(2,1)S(1)}, bf16[320,128]{1,0:T(8,128)(2,1)}, u32[]{:S(2)}) copy-start(bf16[320,128]{1,0:T(8,128)(2,1)} %tokens_ref.5) | copy-start | bytes 245764
  186.9 32.8 %copy-start.5 = (f32[320,128]{1,0:T(8,128)S(1)}, f32[320,128]{1,0:T(8,128)}, u32[]{:S(2)}) copy-start(f32[320,128]{1,0:T(8,128)} %get-tuple-element.111.inv_ref) | copy-start | bytes 491524
  186.9 32.8 %copy-start.6 = (f32[320,128]{1,0:T(8,128)S(1)}, f32[320,128]{1,0:T(8,128)}, u32[]{:S(2)}) copy-start(f32[320,128]{1,0:T(8,128)} %get-tuple-element.105.grad_res_ref) | copy-start | bytes 491524
  186.9 33.6 %copy-start.8 = (f32[8,2048]{1,0:T(8,128)S(1)}, f32[8,2048]{1,0:T(8,128)}, u32[]{:S(2)}) copy-start(f32[8,2048]{1,0:T(8,128)} %get-tuple-element.129.tail_ref) | copy-start | bytes 196612
  220.8 1.5 copy-start
  222.3 43.7 %all-to-all-start.7 = ((bf16[8,80,2048]{2,1,0:T(8,128)(2,1)}), bf16[8,80,2048]{2,1,0:T(8,128)(2,1)S(1)}, u32[]{:S(2)}, u32[]{:S(2)}) async-start(bf16[8,80,2048]{2,1,0:T(8,128)(2,1)} %copy-done), calls=%async_computation.7 | async-start | bytes 5242880 | tf_op jit(solution)/shard_map/all_to_all | solution.py:580
  229.5 36.5 %copy-start.2 = (f32[320,128]{1,0:T(8,128)S(1)}, f32[320,128]{1,0:T(8,128)}, u32[]{:S(2)}) copy-start(f32[320,128]{1,0:T(8,128)} %get-tuple-element.101.resid_ref) | copy-start | bytes 491524
  266.0 0.9 copy-start.7
Sparse Core Ops, SparseCore 0:
  9.7 38.0 all-gather.3
  59.3 101.8 all-gather.5
  163.6 63.6 reduce-scatter.1

commit v5 on v4

--- a/solution.py
+++ b/solution.py
@@ -405,8 +405,15 @@
             )
 
 
-def plain_all_body(blocks_ref, down_ref, out_ref, rows_ref):
-    lay_trees(rows_ref, blocks_ref, 2)
+def plain_all_body(blocks_ref, shown_ref, down_ref, out_ref, chosen_ref, rows_ref):
+    lay_trees(rows_ref, blocks_ref, GROUP)
+    chosen = []
+    for tree in range(GROUP):
+        shown = shown_ref[tree, 0].astype(f32)
+        chosen.append(
+            jnp.concatenate([shown[:8], shown[8:16], shown[16:24]], axis=1)[:, :ROWS]
+        )
+    chosen_ref[...] = jnp.concatenate(chosen, axis=1)
     out_ref[...] = dot_last(down_ref[...], rows_ref[...]).astype(bf16)
 
 
@@ -490,26 +497,31 @@
     return pl.BlockSpec(shape, lambda i: zero, pipeline_mode=pl.Buffered(1))
 
 
-PAIR = 2 * ROWS
+GROUP = 4
+TOGETHER = GROUP * ROWS
 PAIR_FLOPS = 2 * HIDDEN * WIDTH * ALL_ROWS
 
 
 def plain_all(blocks, down_mat):
     return pl.pallas_call(
         plain_all_body,
-        grid=(NDP // 2,),
+        grid=(NDP // GROUP,),
         in_specs=[
-            pl.BlockSpec((2, NTP, ROWS, COLS), lambda i: (i, 0, 1, 0)),
+            pl.BlockSpec((GROUP, NTP, ROWS, COLS), lambda i: (i, 0, 1, 0)),
+            pl.BlockSpec((GROUP, 1, SHOWN, COLS), lambda i: (i, 0, 2 * ROWS // SHOWN, 0)),
             once((HIDDEN, WIDTH)),
         ],
-        out_specs=pl.BlockSpec((HIDDEN, PAIR), lambda i: (0, i)),
-        out_shape=sds((HIDDEN, ALL_ROWS), bf16),
-        scratch_shapes=[pltpu.VMEM((PAIR, WIDTH), bf16)],
+        out_specs=[
+            pl.BlockSpec((HIDDEN, TOGETHER), lambda i: (0, i)),
+            pl.BlockSpec((8, TOGETHER), lambda i: (0, i)),
+        ],
+        out_shape=[sds((HIDDEN, ALL_ROWS), bf16), sds((8, ALL_ROWS), f32)],
+        scratch_shapes=[pltpu.VMEM((TOGETHER, WIDTH), bf16)],
         compiler_params=pltpu.CompilerParams(vmem_limit_bytes=60 * MIB),
         cost_estimate=pl.CostEstimate(
             flops=PAIR_FLOPS, bytes_accessed=20 * MIB, transcendentals=0
         ),
-    )(blocks, down_mat)
+    )(blocks, blocks, down_mat)
 
 
 def hidden_all(blocks, plain, chosen, switch_mat, gate_mat, up_mat):
@@ -685,9 +697,6 @@
 
     own = after(over_chips(wide), gate_mat, up_mat)
     blocks = lax.all_gather(tall, TREES + TENSOR, axis=0).reshape(NDP, NTP, TALL, COLS)
-    chosen_all = blocks[:, 0, 2 * ROWS : 2 * ROWS + EXTRA].reshape(NDP, 3, 8, COLS)
-    chosen_all = jnp.transpose(chosen_all, (2, 0, 1, 3)).reshape(8, NDP, 3 * COLS)
-    chosen_all = chosen_all[:, :, :ROWS].reshape(8, ALL_ROWS).astype(f32)
     (
         keep, send, act, extra, rows_two, inv_two, inv_row, gates, logits,
     ) = call(
@@ -755,7 +764,7 @@
         moved=4 * MIB, limit=16,
     )[0]
     arrived = over_chips(payload)
-    plain_rows = plain_all(after(blocks, payload), down_mat)
+    plain_rows, chosen_all = plain_all(after(blocks, payload), down_mat)
     trees = after(trees, plain_rows)
     tree_sums = over_trees(trees)
     grads = hidden_all(

time: 277 us -> 275 us (level)
  no operation moved by 1% of the time
where the time goes in v5:
time: 275 us; the launch traced here: 274 us
  Pallas kernels  136 us (49%)
  starting transfers between devices  47.1 us (17%)
  waiting for transfers between devices  44.4 us (16%)
  other arithmetic  19.7 us (7%)
  between operations  14 us (5%)
  local copies, waits for them, and re-layouts  12.2 us (4%)
    pallas_call x12, Pallas kernels, call(): pl.pallas_call(body, in_specs=specs, out_specs=[pl.BlockSpec(memory_space...  41.8 us
    pallas_call x1, Pallas kernels, weight_grads(): pl.pallas_call(weights_body, grid=(WIDTH // step,), in_specs=[once((HIDDE...  36.4 us
    pallas_call x1, Pallas kernels, hidden_all(): pl.pallas_call(hidden_all_body, grid=(ALL_ROWS // BLOCK,), in_specs=[pl.B...  32.8 us
    all_to_all x6, starting transfers between devices, over_chips(): return lax.all_to_all(blocks, CHIPS, 0, 0)  31.2 us
    all_to_all x6, waiting for transfers between devices, over_chips(): return lax.all_to_all(blocks, CHIPS, 0, 0)  27.7 us
    pallas_call x1, Pallas kernels, plain_all(): pl.pallas_call(plain_all_body, grid=(NDP // GROUP,), in_specs=[pl.BlockSp...  16 us
    all_to_all x2, starting transfers between devices, over_trees(): return lax.all_to_all(blocks, TREES, 0, 0)  14.5 us
    ppermute x8, waiting for transfers between devices, swap(): return lax.ppermute(block, 'core', SWAP)  12.5 us
  transfers between devices with their start and end apart: 19, of which 12 were waited for; matrix products, arithmetic and copies ran while one was open for 8% of the time, Pallas kernels for 48%

profile of v5, /device:TPU:6, one launch (start us, length us, event | category | flops | bytes accessed | tf_op | source)
XLA Modules:
  0.0 273.6 jit_solution(4844651679389140859)
XLA Ops:
  8.0 1.8 shard_map.366
  9.8 5.9 %all-to-all-start = ((bf16[8,320,128]{2,1,0:T(8,128)(2,1)}), bf16[8,320,128]{2,1,0:T(8,128)(2,1)S(1)}, u32[]{:S(2)}, u32[]{:S(2)}) async-start(bf16[8,320,128]{2,1,0:T(8,128)(2,1)} %get-tuple-element.88), calls=%async_computation | async-start | bytes 1310720 | tf_op jit(solution)/shard_map/all_to_all | solution.py:588
  17.9 1.8 and_convert_fusion.see_ref
  19.7 2.8 %multiply_convert_fusion.2.w_ref = bf16[2048,384]{1,0:T(8,128)(2,1)} fusion(bf16[2048,128]{1,0:T(8,128)(2,1)} %param.34, bf16[2048,128]{1,0:T(8,128)(2,1)} %param.32, bf16[2048,128]{1,0:T(8,128)(2,1)} %param.30, f32[2048]{0:T(1024)S(1)} %convert_element_type.56), kind=kLoop, calls=%fused_computation.3 | loop fusion | flops 6291456 | bytes 3153920 | tf_op jit(solution)/shard_map/convert_element_type | solution.py:643
  22.5 1.4 multiply_sine_fusion
  24.5 2.2 pad_maximum_fusion.down_ref
  26.7 2.1 collective-permute-done.other_ref
  28.9 0.8 copy-done.20
  29.7 5.9 %shard_map.367 = (bf16[8,320,128]{2,1,0:T(8,128)(2,1)}, bf16[8,320,128]{2,1,0:T(8,128)(2,1)}, bf16[320,2048]{1,0:T(8,128)(2,1)}, f32[320,128]{1,0:T(8,128)}, f32...) custom-call(s32[1]{0:T(128)} %bitcast.core_ref, ...), custom_call_target="tpu_custom_call" | custom-call | flops 900000000 | bytes 8388608 | tf_op jit(solution)/shard_map/pallas_call | solution.py:68
  35.9 2.1 collective-permute-done.1
  38.0 2.2 add_convert_fusion
  40.2 5.7 %all-to-all-start.1 = ((bf16[8,320,128]{2,1,0:T(8,128)(2,1)}), bf16[8,320,128]{2,1,0:T(8,128)(2,1)S(1)}, u32[]{:S(2)}, u32[]{:S(2)}) async-start(bf16[8,320,128]{2,1,0:T(8,128)(2,1)} %add_convert_fusion), calls=%async_computation.1 | async-start | bytes 1310720 | tf_op jit(solution)/shard_map/all_to_all | solution.py:588
  45.9 1.9 all-gather.4.cloned.1.call-done.rows_ref
  47.8 5.3 %shard_map.368.plain_ref = bf16[880,320]{1,0:T(8,128)(2,1)} custom-call(bf16[320,2048]{1,0:T(8,128)(2,1)} %all-gather.4.cloned.1.call-done.rows_ref, bf16[880,2048]{1,0:T(8,128)(2,1)} %pad_maximum_fusion.down_ref), custom_call_target="tpu_custom_call" | custom-call | flops 1153433600 | bytes 6291456 | tf_op jit(solution)/shard_map/pallas_call | solution.py:68
  53.1 3.1 %all-to-all-done.1.arrived_ref = bf16[8,320,128]{2,1,0:T(8,128)(2,1)S(1)} async-done(((bf16[8,320,128]{2,1,0:T(8,128)(2,1)}), bf16[8,320,128]{2,1,0:T(8,128)(2,1)S(1)}, u32[]{:S(2)}, u32[]{:S(2)}) %all-to-all-start.1) | async-done | bytes 655392 | tf_op jit(solution)/shard_map/all_to_all | solution.py:588
  56.2 0.8 copy-done.13
  57.0 2.2 shard_map.369
  59.2 4.2 %all-to-all-start.2 = ((bf16[8,320,128]{2,1,0:T(8,128)(2,1)}), bf16[8,320,128]{2,1,0:T(8,128)(2,1)S(1)}, u32[]{:S(2)}, u32[]{:S(2)}) async-start(bf16[8,320,128]{2,1,0:T(8,128)(2,1)} %get-tuple-element.94), calls=%async_computation.2 | async-start | bytes 1310720 | tf_op jit(solution)/shard_map/all_to_all | solution.py:588
  63.5 5.8 %multiply_convert_fusion = (bf16[880,2048]{1,0:T(8,128)(2,1)}, bf16[880,2048]{1,0:T(8,128)(2,1)}) fusion(bf16[352,2048]{1,0:T(8,128)(2,1)} %bitcast.49, bf16[528,2048]{1,0:T(8,128)(2,1)S(1)} %bitcast.46, f32[2048]{0:T(1024)S(1)} %convert_element_type.65, bf16[352,2048]{1,0:T(8,128)(2,1)} %bitcast.50, bf16[528,2048]{1,0:T(8,128)(2,1)} %bitcast.47), kind=kLoop, calls=%fused_computation | loop fusion | flops 21626880 | bytes 14426112 | tf_op jit(solution)/shard_map/convert_element_type | solution.py:637
  69.3 4.4 %all-to-all-done.2.own_ref = bf16[8,320,128]{2,1,0:T(8,128)(2,1)S(1)} async-done(((bf16[8,320,128]{2,1,0:T(8,128)(2,1)}), bf16[8,320,128]{2,1,0:T(8,128)(2,1)S(1)}, u32[]{:S(2)}, u32[]{:S(2)}) %all-to-all-start.2) | async-done | bytes 655392 | tf_op jit(solution)/shard_map/all_to_all | solution.py:588
  74.5 1.3 collective-permute-done.2.other_ref
  76.6 12.5 %shard_map.370 = (bf16[8,320,128]{2,1,0:T(8,128)(2,1)}, bf16[8,320,128]{2,1,0:T(8,128)(2,1)}, bf16[880,320]{1,0:T(8,128)(2,1)}, f32[3,8,128]{2,1,0:T(8,128)}, bf...) custom-call(s32[1]{0:T(128)} %bitcast.core_ref, ...), custom_call_target="tpu_custom_call" | custom-call | flops 4613734400 | bytes 20971520 | tf_op jit(solution)/shard_map/pallas_call | solution.py:68
  89.6 1.8 collective-permute-done.4.extra_came_ref
  91.4 1.1 copy-done.4
  93.2 1.0 shard_map.371
  94.3 4.3 %all-to-all-start.3 = ((bf16[8,368,128]{2,1,0:T(8,128)(2,1)}), bf16[8,368,128]{2,1,0:T(8,128)(2,1)S(1)}, u32[]{:S(2)}, u32[]{:S(2)}) async-start(bf16[8,368,128]{2,1,0:T(8,128)(2,1)} %shard_map.371), calls=%async_computation.3 | async-start | bytes 1507328 | tf_op jit(solution)/shard_map/all_to_all | solution.py:588
  99.1 1.2 constant_dynamic-slice_fusion.switch_ref
  100.4 11.3 %all-to-all-done.3.arrived_ref = bf16[8,368,128]{2,1,0:T(8,128)(2,1)S(1)} async-done(((bf16[8,368,128]{2,1,0:T(8,128)(2,1)}), bf16[8,368,128]{2,1,0:T(8,128)(2,1)S(1)}, u32[]{:S(2)}, u32[]{:S(2)}) %all-to-all-start.3) | async-done | bytes 753696 | tf_op jit(solution)/shard_map/all_to_all | solution.py:588
  111.6 0.9 copy-done.11
  112.5 2.5 shard_map.372
  115.0 4.7 %all-to-all-start.4 = ((bf16[8,320,128]{2,1,0:T(8,128)(2,1)}), bf16[8,320,128]{2,1,0:T(8,128)(2,1)S(1)}, u32[]{:S(2)}, u32[]{:S(2)}) async-start(bf16[8,320,128]{2,1,0:T(8,128)(2,1)} %get-tuple-element.105), calls=%async_computation.4 | async-start | bytes 1310720 | tf_op jit(solution)/shard_map/all_to_all | solution.py:588
  119.7 6.1 %shard_map.373 = bf16[5120,128]{1,0:T(8,128)(2,1)} custom-call(bf16[880,320]{1,0:T(8,128)(2,1)} %get-tuple-element.108.act_ref, bf16[880,2048]{1,0:T(8,128)(2,1)} %pad_maximum_fusion.down_ref), custom_call_target="tpu_custom_call" | custom-call | flops 1153433600 | bytes 8388608 | tf_op jit(solution)/shard_map/pallas_call | solution.py:68
  125.8 8.9 %all-to-all-done.4.own_ref = bf16[8,320,128]{2,1,0:T(8,128)(2,1)S(1)} async-done(((bf16[8,320,128]{2,1,0:T(8,128)(2,1)}), bf16[8,320,128]{2,1,0:T(8,128)(2,1)S(1)}, u32[]{:S(2)}, u32[]{:S(2)}) %all-to-all-start.4) | async-done | bytes 655392 | tf_op jit(solution)/shard_map/all_to_all | solution.py:588
  134.7 2.4 collective-permute-done.5.other_ref
  137.9 9.2 %shard_map.374 = (bf16[8,320,128]{2,1,0:T(8,128)(2,1)}, bf16[8,320,128]{2,1,0:T(8,128)(2,1)}, f32[24,128]{1,0:T(8,128)}, bf16[8,64,2048]{2,1,0:T(8,128)(2,1)}, f32[8,2048]{1,0:T(8,128)}) custom-call(s32[1]{0:T(128)} %bitcast.core_ref, bf16[8,320,128]{2,1,0:T(8,128)(2,1)} %copy-done.12, bf16[8,320,128]{2,1,0:T(8,128)(2,1)} %copy-done.18, ...), custom_call_target="tpu_custom_call" | custom-call | flops 2000000000 | bytes 14680064 | tf_op jit(solution)/shard_map/pallas_call | solution.py:742
  147.6 2.7 %collective-permute-done.7.extra_came_ref = f32[24,128]{1,0:T(8,128)S(1)} collective-permute-done((f32[24,128]{1,0:T(8,128)}, f32[24,128]{1,0:T(8,128)S(1)}, u32[]{:S(2)}, u32[]{:S(2)}) %collective-permute-start.7) | collective-permute-done | bytes 12320 | tf_op jit(solution)/shard_map/ppermute | solution.py:600
  150.4 1.1 copy-done.3
  152.2 1.0 shard_map.375
  153.2 6.4 %all-to-all-start.6 = ((bf16[8,368,128]{2,1,0:T(8,128)(2,1)}), bf16[8,368,128]{2,1,0:T(8,128)(2,1)S(1)}, u32[]{:S(2)}, u32[]{:S(2)}) async-start(bf16[8,368,128]{2,1,0:T(8,128)(2,1)} %shard_map.375), calls=%async_computation.6 | async-start | bytes 1507328 | tf_op jit(solution)/shard_map/all_to_all | solution.py:588
  159.6 1.6 all-gather.6.cloned.1.call-done
  161.2 16.0 %shard_map.376 = (bf16[880,2560]{1,0:T(8,128)(2,1)}, f32[8,2560]{1,0:T(8,128)}) custom-call(bf16[8,16,672,128]{3,2,1,0:T(8,128)(2,1)} %bitcast.41, bf16[8,16,672,128]{3,2,1,0:T(8,128)(2,1)} %bitcast.42, bf16[880,2048]{1,0:T(8,128)(2,1)} %pad_maximum_fusion.down_ref), custom_call_target="tpu_custom_call" | custom-call | flops 9227468800 | bytes 20971520 | tf_op jit(solution)/shard_map/pallas_call | solution.py:506
  177.3 7.3 %all-to-all-start.5 = ((bf16[8,64,2048]{2,1,0:T(8,128)(2,1)}), bf16[8,64,2048]{2,1,0:T(8,128)(2,1)S(1)}, u32[]{:S(2)}, u32[]{:S(2)}) async-start(bf16[8,64,2048]{2,1,0:T(8,128)(2,1)} %get-tuple-element.126), calls=%async_computation.5 | async-start | bytes 4194304 | tf_op jit(solution)/shard_map/all_to_all | solution.py:592
  184.6 32.8 %shard_map.377 = (bf16[880,2560]{1,0:T(8,128)(2,1)}, bf16[880,2560]{1,0:T(8,128)(2,1)}, bf16[880,2560]{1,0:T(8,128)(2,1)}) custom-call(bf16[8,16,672,128]{3,2,1,0:T(8,128)(2,1)} %bitcast.43, bf16[880,2560]{1,0:T(8,128)(2,1)} %get-tuple-element.127.plain_ref, f32[8,2560]{1,0:T(8,128)} %get-tuple-element.128.chosen_ref, ...), custom_call_target="tpu_custom_call" | custom-call | flops 27682406400 | bytes 41943040 | tf_op jit(solution)/shard_map/pallas_call | solution.py:528
  218.6 1.5 copy-done
  220.1 7.2 %all-to-all-start.7 = ((bf16[8,80,2048]{2,1,0:T(8,128)(2,1)}), bf16[8,80,2048]{2,1,0:T(8,128)(2,1)S(1)}, u32[]{:S(2)}, u32[]{:S(2)}) async-start(bf16[8,80,2048]{2,1,0:T(8,128)(2,1)} %copy-done), calls=%async_computation.7 | async-start | bytes 5242880 | tf_op jit(solution)/shard_map/all_to_all | solution.py:592
  227.3 36.4 %shard_map.381 = (f32[528,2048]{1,0:T(8,128)}, f32[352,2048]{1,0:T(8,128)}, f32[528,2048]{1,0:T(8,128)}, f32[352,2048]{1,0:T(8,128)}, f32[528,2048]{1,0:T(8,128)}, /*index=5*/f32[352,2048]{1,0:T(8,128)}) custom-call(bf16[880,2560]{1,0:T(8,128)(2,1)} %get-tuple-element.149.grad_gate_ref, bf16[880,2560]{1,0:T(8,128)(2,1)} %get-tuple-element.130.grad_up_ref, ...), custom_call_target="tpu_custom_call" | custom-call | flops 27682406400 | bytes 58720256 | tf_op jit(solution)/shard_map/pallas_call | solution.py:559
  263.8 0.9 copy-done.7
  264.6 2.4 shard_map.380
  (84 shorter events, 10.5 us)
Async XLA Ops:
  7.2 16.7 %copy-start.25 = (bf16[128]{0:T(256)(128)(2,1)S(1)}, bf16[128]{0:T(256)(128)(2,1)}, u32[]{:S(2)}) copy-start(bf16[128]{0:T(256)(128)(2,1)} %param.35) | copy-start | bytes 772
  7.2 16.7 %copy-start.26 = (bf16[128]{0:T(256)(128)(2,1)S(1)}, bf16[128]{0:T(256)(128)(2,1)}, u32[]{:S(2)}) copy-start(bf16[128]{0:T(256)(128)(2,1)} %param.33) | copy-start | bytes 772
  7.2 16.7 %copy-start.27 = (bf16[128]{0:T(256)(128)(2,1)S(1)}, bf16[128]{0:T(256)(128)(2,1)}, u32[]{:S(2)}) copy-start(bf16[128]{0:T(256)(128)(2,1)} %param.31) | copy-start | bytes 772
  7.2 17.3 %copy-start.16 = (bf16[6,88,2048]{2,1,0:T(8,128)(2,1)S(1)}, bf16[6,88,2048]{2,1,0:T(8,128)(2,1)}, u32[]{:S(2)}) copy-start(bf16[6,88,2048]{2,1,0:T(8,128)(2,1)} %param.41) | copy-start | bytes 6488068
  7.2 40.5 %all-gather.4.cloned.1.call-start = ((), (), s32[]{:S(2)}) async-start(), calls=%async_computation.9 | async-start | bytes 1392640 | tf_op jit(solution)/shard_map/all_gather | solution.py:669
  9.8 16.9 %all-to-all-start = ((bf16[8,320,128]{2,1,0:T(8,128)(2,1)}), bf16[8,320,128]{2,1,0:T(8,128)(2,1)S(1)}, u32[]{:S(2)}, u32[]{:S(2)}) async-start(bf16[8,320,128]{2,1,0:T(8,128)(2,1)} %get-tuple-element.88), calls=%async_computation | async-start | bytes 1310720 | tf_op jit(solution)/shard_map/all_to_all | solution.py:588
  15.7 8.8 %copy-start.17 = (bf16[352,2048]{1,0:T(8,128)(2,1)S(1)}, bf16[352,2048]{1,0:T(8,128)(2,1)}, u32[]{:S(2)}) copy-start(bf16[352,2048]{1,0:T(8,128)(2,1)} %param.44) | copy-start | bytes 4325380
  26.7 2.2 copy-start.14
  26.7 2.2 collective-permute-start
  28.9 0.8 copy-start.20
  35.6 2.4 collective-permute-start.1
  40.2 16.0 %all-to-all-start.1 = ((bf16[8,320,128]{2,1,0:T(8,128)(2,1)}), bf16[8,320,128]{2,1,0:T(8,128)(2,1)S(1)}, u32[]{:S(2)}, u32[]{:S(2)}) async-start(bf16[8,320,128]{2,1,0:T(8,128)(2,1)} %add_convert_fusion), calls=%async_computation.1 | async-start | bytes 1310720 | tf_op jit(solution)/shard_map/all_to_all | solution.py:588
  45.9 13.4 %copy-start.23 = (bf16[2048]{0:T(1024)(128)(2,1)S(1)}, bf16[2048]{0:T(1024)(128)(2,1)}, u32[]{:S(2)}) copy-start(bf16[2048]{0:T(1024)(128)(2,1)} %param.37) | copy-start | bytes 12292
  45.9 17.6 %copy-start.15 = (bf16[6,2048,88]{1,2,0:T(8,128)(2,1)S(1)}, bf16[6,2048,88]{1,2,0:T(8,128)(2,1)}, u32[]{:S(2)}) copy-start(bf16[6,2048,88]{1,2,0:T(8,128)(2,1)} %param.40) | copy-start | bytes 6488068
  45.9 115.4 %all-gather.6.cloned.1.call-start = ((), (), s32[]{:S(2)}) async-start(), calls=%async_computation.11 | async-start | bytes 22192128 | tf_op jit(solution)/shard_map/all_gather | solution.py:699
  56.2 0.8 copy-start.13
  59.2 39.3 %copy-start.21 = (f32[2048]{0:T(1024)}, f32[2048]{0:T(1024)S(1)}, u32[]{:S(2)}) copy-start(f32[2048]{0:T(1024)S(1)} %convert_element_type.65) | copy-start | bytes 24580
  59.2 14.4 %all-to-all-start.2 = ((bf16[8,320,128]{2,1,0:T(8,128)(2,1)}), bf16[8,320,128]{2,1,0:T(8,128)(2,1)S(1)}, u32[]{:S(2)}, u32[]{:S(2)}) async-start(bf16[8,320,128]{2,1,0:T(8,128)(2,1)} %get-tuple-element.94), calls=%async_computation.2 | async-start | bytes 1310720 | tf_op jit(solution)/shard_map/all_to_all | solution.py:588
  63.5 10.2 %copy-start.24 = (bf16[2048]{0:T(1024)(128)(2,1)S(1)}, bf16[2048]{0:T(1024)(128)(2,1)}, u32[]{:S(2)}) copy-start(bf16[2048]{0:T(1024)(128)(2,1)} %param.45) | copy-start | bytes 12292
  63.5 10.3 %copy-start.22 = (bf16[2048,6]{0,1:T(8,128)(2,1)S(1)}, bf16[2048,6]{0,1:T(8,128)(2,1)}, u32[]{:S(2)}) copy-start(bf16[2048,6]{0,1:T(8,128)(2,1)} %param.38) | copy-start | bytes 73732
  73.7 2.1 copy-start.19
  73.7 2.1 collective-permute-start.2
  75.8 0.8 copy-start.28
  89.1 2.3 collective-permute-start.3
  89.3 2.2 collective-permute-start.4
  91.4 1.1 copy-start.4
  92.5 0.7 copy-start.10
  94.3 17.4 %all-to-all-start.3 = ((bf16[8,368,128]{2,1,0:T(8,128)(2,1)}), bf16[8,368,128]{2,1,0:T(8,128)(2,1)S(1)}, u32[]{:S(2)}, u32[]{:S(2)}) async-start(bf16[8,368,128]{2,1,0:T(8,128)(2,1)} %shard_map.371), calls=%async_computation.3 | async-start | bytes 1507328 | tf_op jit(solution)/shard_map/all_to_all | solution.py:588
  111.6 0.9 copy-start.11
  115.0 19.7 %all-to-all-start.4 = ((bf16[8,320,128]{2,1,0:T(8,128)(2,1)}), bf16[8,320,128]{2,1,0:T(8,128)(2,1)S(1)}, u32[]{:S(2)}, u32[]{:S(2)}) async-start(bf16[8,320,128]{2,1,0:T(8,128)(2,1)} %get-tuple-element.105), calls=%async_computation.4 | async-start | bytes 1310720 | tf_op jit(solution)/shard_map/all_to_all | solution.py:588
  134.7 2.4 copy-start.12
  134.7 2.4 collective-permute-start.5
  137.1 0.8 copy-start.18
  147.1 3.3 %collective-permute-start.6 = (bf16[8,320,128]{2,1,0:T(8,128)(2,1)}, bf16[8,320,128]{2,1,0:T(8,128)(2,1)S(1)}, u32[]{:S(2)}, u32[]{:S(2)}) collective-permute-start(bf16[8,320,128]{2,1,0:T(8,128)(2,1)} %get-tuple-element.122), channel_id=1, source_target_pairs={{0,1},{1,0},{2,3},{3,2},{4,5},{5,4},{6,7},{7,6},{8,9},{9,8},{10,11... | collective-permute-start | bytes 1966088 | tf_op jit(solution)/shard_map/ppermute | solution.py:600
  147.1 3.2 %collective-permute-start.7 = (f32[24,128]{1,0:T(8,128)}, f32[24,128]{1,0:T(8,128)S(1)}, u32[]{:S(2)}, u32[]{:S(2)}) collective-permute-start(f32[24,128]{1,0:T(8,128)} %get-tuple-element.123.extra_ref), channel_id=1, source_target_pairs={{0,1},{1,0},{2,3},{3,2},{4,5},{5,4},{6,7},{7,6},{8,9},{9,8},{10,11... | collective-permute-start | bytes 36872 | tf_op jit(solution)/shard_map/ppermute | solution.py:600
  150.4 1.1 copy-start.3
  151.5 0.7 copy-start.9
  153.2 24.1 %all-to-all-start.6 = ((bf16[8,368,128]{2,1,0:T(8,128)(2,1)}), bf16[8,368,128]{2,1,0:T(8,128)(2,1)S(1)}, u32[]{:S(2)}, u32[]{:S(2)}) async-start(bf16[8,368,128]{2,1,0:T(8,128)(2,1)} %shard_map.375), calls=%async_computation.6 | async-start | bytes 1507328 | tf_op jit(solution)/shard_map/all_to_all | solution.py:588
  159.6 104.1 %reduce-scatter.2.cloned.1.call-start = ((), (), s32[]{:S(2)}) async-start(), calls=%async_computation.10 | async-start | bytes 1392640 | tf_op jit(solution)/shard_map/reduce_scatter | solution.py:773
  177.3 41.0 %all-to-all-start.5 = ((bf16[8,64,2048]{2,1,0:T(8,128)(2,1)}), bf16[8,64,2048]{2,1,0:T(8,128)(2,1)S(1)}, u32[]{:S(2)}, u32[]{:S(2)}) async-start(bf16[8,64,2048]{2,1,0:T(8,128)(2,1)} %get-tuple-element.126), calls=%async_computation.5 | async-start | bytes 4194304 | tf_op jit(solution)/shard_map/all_to_all | solution.py:592
  184.6 32.8 %copy-start.1 = (bf16[320,128]{1,0:T(8,128)(2,1)S(1)}, bf16[320,128]{1,0:T(8,128)(2,1)}, u32[]{:S(2)}) copy-start(bf16[320,128]{1,0:T(8,128)(2,1)} %tokens_ref.5) | copy-start | bytes 245764
  184.6 32.8 %copy-start.5 = (f32[320,128]{1,0:T(8,128)S(1)}, f32[320,128]{1,0:T(8,128)}, u32[]{:S(2)}) copy-start(f32[320,128]{1,0:T(8,128)} %get-tuple-element.113.inv_ref) | copy-start | bytes 491524
  184.6 32.8 %copy-start.6 = (f32[320,128]{1,0:T(8,128)S(1)}, f32[320,128]{1,0:T(8,128)}, u32[]{:S(2)}) copy-start(f32[320,128]{1,0:T(8,128)} %get-tuple-element.107.grad_res_ref) | copy-start | bytes 491524
  184.6 33.7 %copy-start.8 = (f32[8,2048]{1,0:T(8,128)S(1)}, f32[8,2048]{1,0:T(8,128)}, u32[]{:S(2)}) copy-start(f32[8,2048]{1,0:T(8,128)} %get-tuple-element.133.tail_ref) | copy-start | bytes 196612
  218.6 1.5 copy-start
  220.1 43.7 %all-to-all-start.7 = ((bf16[8,80,2048]{2,1,0:T(8,128)(2,1)}), bf16[8,80,2048]{2,1,0:T(8,128)(2,1)S(1)}, u32[]{:S(2)}, u32[]{:S(2)}) async-start(bf16[8,80,2048]{2,1,0:T(8,128)(2,1)} %copy-done), calls=%async_computation.7 | async-start | bytes 5242880 | tf_op jit(solution)/shard_map/all_to_all | solution.py:592
  227.3 36.5 %copy-start.2 = (f32[320,128]{1,0:T(8,128)S(1)}, f32[320,128]{1,0:T(8,128)}, u32[]{:S(2)}) copy-start(f32[320,128]{1,0:T(8,128)} %get-tuple-element.103.resid_ref) | copy-start | bytes 491524
  263.7 0.9 copy-start.7
Sparse Core Ops, SparseCore 0:
  9.7 38.0 all-gather.3
  59.3 101.8 all-gather.5
  163.6 63.9 reduce-scatter.1
